TPU v7x, 32 devices: a whole 2x2x4 slice. The times are simulated.
32 devices in a mesh: seq: 8 (over y, x, core), batch: 4 (over z).
Axes of the slice: x: 2, y: 2, z: 4, core: 2. Of those that a mesh axis runs over, the one named last changes fastest.
Arguments:
- tokens: float32 [8, 1024, 1024], P('batch', 'seq'), may hold values from -6 to 6
- lengths: int32 [8], P('batch'), may hold values from 102 to 1024, as said below
- out_grad: float32 [8, 1024, 1024], P('batch', 'seq'), may hold values from -6 to 6
- first_gain: float32 [1024], P('seq'), may hold values from 0.25 to 1.75
- smooth_alpha: float32 [1024, 16], P('seq'), may hold values from -9 to -2
- smooth_delta: float32 [1024, 16], P('seq'), may hold values from -3 to 2
- smooth_beta: float32 [1024, 16], P('seq'), may hold values from -4 to 4
- smooth_gamma: float32 [1024, 16], P('seq'), may hold values from -4 to 4
- smooth_omega: float32 [1024], P('seq'), may hold values from -4 to 4
- value_weight: float32 [1024, 2048], P('seq'), may hold values from -0.1875 to 0.1875
- mix_weight: float32 [1024, 4224], P('seq'), may hold values from -0.1875 to 0.1875
- query_affine: float32 [128, 3], P('seq'), may hold values from -10 to 10
- merge_weight: float32 [2048, 1024], P('seq'), may hold values from -0.75 to 0.75
- second_gain: float32 [1024], P('seq'), may hold values from 0.25 to 1.75
- widen_weight: float32 [1024, 4096], P('seq'), may hold values from -0.1875 to 0.1875
- narrow_weight: float32 [4096, 1024], P('seq'), may hold values from -0.09375 to 0.09375
Outputs:
- block_out: float32 [8, 1024, 1024], P('batch', 'seq')
- tokens_grad: float32 [8, 1024, 1024], P('batch', 'seq')
- first_gain_grad: float32 [1024], P('seq')
- smooth_alpha_grad: float32 [1024, 16], P('seq')
- smooth_delta_grad: float32 [1024, 16], P('seq')
- smooth_beta_grad: float32 [1024, 16], P('seq')
- smooth_gamma_grad: float32 [1024, 16], P('seq')
- smooth_omega_grad: float32 [1024], P('seq')
- value_weight_grad: float32 [1024, 2048], P('seq')
- mix_weight_grad: float32 [1024, 4224], P('seq')
- query_affine_grad: float32 [128, 3], P('seq')
- merge_weight_grad: float32 [2048, 1024], P('seq')
- second_gain_grad: float32 [1024], P('seq')
- widen_weight_grad: float32 [1024, 4096], P('seq')
- narrow_weight_grad: float32 [4096, 1024], P('seq')
Inputs may be any that keep to these rules, and one draw needn't show every extreme that they name: `lengths`: in every group of 2 consecutive slots at least one sequence has length 1024.
All inputs are finite; a program needn't handle non-finite values.
Results may differ from a plain program's by a relative error of at most 0.0003.
Values sent between devices are 32-bit elements; how exact they have to be, the bound alone decides.
A program may use at most 512 MiB of HBM per device.

v0:
```python
import jax
import jax.numpy as jnp
from jax import lax
from jax.sharding import PartitionSpec as P

precise = lax.Precision.HIGHEST
norm_eps = 1e-05
masked_score = -1000000000.0


def entering(value, axis, join, neutral, backward):
    count, mine = (lax.axis_size(axis), lax.axis_index(axis))
    pieces = jax.tree.map(lambda part: lax.all_gather(part, axis), value)
    if backward:
        pieces = jax.tree.map(lambda part: part[::-1], pieces)
        mine = count - 1 - mine
    total = jax.tree.map(
        lambda part, zero: jnp.full_like(part, 0) + jnp.asarray(zero, part.dtype), value, neutral
    )

    def step(position, total):
        longer = join(total, jax.tree.map(lambda part: part[position], pieces))
        return jax.tree.map(lambda new, old: jnp.where(position < mine, new, old), longer, total)

    return lax.fori_loop(0, count - 1, step, total)


def layer_norm(signal, norm_gain):
    centre = jnp.mean(signal, axis=-1, keepdims=True)
    shifted = signal - centre
    spread = jnp.mean(shifted * shifted, axis=-1, keepdims=True)
    return shifted * lax.rsqrt(spread + norm_eps) * norm_gain


def smoothing_tables(alpha_logit, delta_logit, expand_gain, project_gain, block_len):
    alpha_rate = jax.nn.sigmoid(alpha_logit)
    damp_rate = jax.nn.sigmoid(delta_logit)
    log_decay = jnp.log1p(-alpha_rate * damp_rate)
    offsets = jnp.arange(block_len + 1, dtype=jnp.float32)
    powers = jnp.exp(offsets[:, None, None] * log_decay[None])
    rising = jnp.exp(-offsets[:block_len, None, None] * log_decay[None])
    input_gain = alpha_rate * expand_gain
    out_scale = project_gain.shape[1] ** (-0.5)
    weighted = powers[:block_len] * (input_gain * project_gain * out_scale)[None]
    toeplitz = jnp.einsum("tdn,sdn->dts", weighted, rising, precision=precise)
    causal = offsets[:block_len, None] >= offsets[None, :block_len]
    toeplitz = jnp.where(causal[None], toeplitz, 0.0)
    return (powers, input_gain, toeplitz)


def gated_mix(
    masked_in,
    normed,
    smoothed,
    skip_gain,
    value_weight,
    mix_weight,
    query_affine,
    merge_weight,
    valid_mask,
    block_len,
):
    model_width = masked_in.shape[-1]
    shared_dim = query_affine.shape[0]
    value_dim = value_weight.shape[1]
    values = jax.nn.silu(jnp.einsum("bld,dv->blv", normed, value_weight, precision=precise))
    mixed_in = jax.nn.silu(smoothed + skip_gain * normed)
    projected = jnp.einsum("bld,dk->blk", mixed_in, mix_weight, precision=precise)
    second_cut = model_width + shared_dim
    third_cut = second_cut + value_dim
    update = jax.nn.sigmoid(projected[..., :model_width])
    shared = jax.nn.silu(projected[..., model_width:second_cut])
    reset_gate = jax.nn.silu(projected[..., second_cut:third_cut])
    candidate_in = projected[..., third_cut:]
    queries = shared * query_affine[:, 0] + query_affine[:, 2]
    key_rows = shared * query_affine[:, 1]
    blocks = masked_in.shape[0] * masked_in.shape[1] // block_len
    scores = jnp.einsum("cqz,ckz->cqk", queries, key_rows, precision=precise) * shared_dim ** (-0.5)
    key_valid = valid_mask.reshape(blocks, 1, block_len)
    scores = jnp.where(key_valid > 0.5, scores, masked_score)
    soft_weights = jax.nn.softmax(scores, axis=-1)
    attended = jnp.einsum("cqk,ckv->cqv", soft_weights, values, precision=precise)
    candidate = jax.nn.silu(
        candidate_in
        + jnp.einsum("blv,vd->bld", attended * reset_gate, merge_weight, precision=precise)
    )
    return masked_in + update * (candidate - masked_in)


def feed_forward(middle, norm_gain, widen_weight, narrow_weight, valid_mask):
    normed_two = layer_norm(middle, norm_gain)
    hidden = jax.nn.silu(jnp.einsum("bld,df->blf", normed_two, widen_weight, precision=precise))
    return (
        middle + jnp.einsum("blf,fd->bld", hidden, narrow_weight, precision=precise)
    ) * valid_mask[:, :, None]


def chain_step(earlier, later):
    return (earlier[0] * later[0], later[0] * earlier[1] + later[1])


def per_device(
    tokens,
    lengths,
    out_grad,
    first_gain,
    smooth_alpha,
    smooth_delta,
    smooth_beta,
    smooth_gamma,
    smooth_omega,
    value_weight,
    mix_weight,
    query_affine,
    merge_weight,
    second_gain,
    widen_weight,
    narrow_weight,
):
    block_len = tokens.shape[1]
    offsets = lax.axis_index("seq") * block_len + lax.iota(jnp.int32, block_len)
    valid_mask = (offsets[None, :] < lengths[:, None]).astype(jnp.float32)
    gathered = (
        lax.all_gather(first_gain, "seq", axis=0, tiled=True),
        lax.all_gather(smooth_alpha, "seq", axis=0, tiled=True),
        lax.all_gather(smooth_delta, "seq", axis=0, tiled=True),
        lax.all_gather(smooth_beta, "seq", axis=0, tiled=True),
        lax.all_gather(smooth_gamma, "seq", axis=0, tiled=True),
        lax.all_gather(smooth_omega, "seq", axis=0, tiled=True),
        lax.all_gather(value_weight, "seq", axis=0, tiled=True),
        lax.all_gather(mix_weight, "seq", axis=0, tiled=True),
        lax.all_gather(query_affine, "seq", axis=0, tiled=True),
        lax.all_gather(merge_weight, "seq", axis=0, tiled=True),
    )
    (
        gain_one,
        alpha_full,
        delta_full,
        beta_full,
        gamma_full,
        omega_full,
        value_full,
        mix_full,
        affine_full,
        merge_full,
    ) = gathered

    def front_part(signal, norm_gain, alpha_logit, delta_logit, expand_gain, project_gain):
        masked_in = signal * valid_mask[:, :, None]
        normed = layer_norm(masked_in, norm_gain)
        powers, input_gain, toeplitz = smoothing_tables(
            alpha_logit, delta_logit, expand_gain, project_gain, block_len
        )
        local_sum = jnp.einsum("dts,bsd->btd", toeplitz, normed, precision=precise)
        end_state = input_gain[None] * jnp.einsum(
            "sdn,bsd->bdn", powers[:block_len][::-1], normed, precision=precise
        )
        return (masked_in, normed, local_sum, end_state, powers)

    def attn_part(
        masked_in,
        normed,
        local_sum,
        carry_in,
        powers,
        project_gain,
        skip_gain,
        value_mat,
        mix_mat,
        affine,
        merge_mat,
    ):
        out_scale = project_gain.shape[1] ** (-0.5)
        carried = jnp.einsum(
            "tdn,bdn->btd",
            powers[1:] * (project_gain * out_scale)[None],
            carry_in,
            precision=precise,
        )
        return gated_mix(
            masked_in,
            normed,
            local_sum + carried,
            skip_gain,
            value_mat,
            mix_mat,
            affine,
            merge_mat,
            valid_mask,
            block_len,
        )

    def ffn_part(middle, norm_gain, widen_mat, narrow_mat):
        return feed_forward(middle, norm_gain, widen_mat, narrow_mat, valid_mask)

    sectioned, front_pull = jax.vjp(
        front_part, tokens, gain_one, alpha_full, delta_full, beta_full, gamma_full
    )
    masked_in, normed, local_sum, end_state, powers = sectioned
    decays = powers[-1]
    carry_in = entering(
        (decays, end_state),
        "seq",
        chain_step,
        (jnp.ones_like(decays), jnp.zeros_like(end_state)),
        False,
    )[1]
    ffn_full = (
        lax.all_gather(second_gain, "seq", axis=0, tiled=True),
        lax.all_gather(widen_weight, "seq", axis=0, tiled=True),
        lax.all_gather(narrow_weight, "seq", axis=0, tiled=True),
    )
    middle, attn_pull = jax.vjp(
        attn_part,
        masked_in,
        normed,
        local_sum,
        carry_in,
        powers,
        gamma_full,
        omega_full,
        value_full,
        mix_full,
        affine_full,
        merge_full,
    )
    block_out, ffn_pull = jax.vjp(ffn_part, middle, ffn_full[0], ffn_full[1], ffn_full[2])
    grad_middle, grad_second, grad_widen, grad_narrow = ffn_pull(out_grad)
    (
        grad_masked,
        grad_normed,
        grad_local,
        grad_carry,
        grad_powers,
        grad_gamma_late,
        grad_omega,
        grad_value,
        grad_mix,
        grad_affine,
        grad_merge,
    ) = attn_pull(grad_middle)
    adjoint = entering(
        (decays, grad_carry),
        "seq",
        chain_step,
        (jnp.ones_like(decays), jnp.zeros_like(grad_carry)),
        True,
    )[1]
    grad_decays = jnp.sum(adjoint * carry_in, axis=0)
    grad_powers = jnp.concatenate([grad_powers[:-1], grad_powers[-1:] + grad_decays[None]], axis=0)
    grad_tokens, grad_first, grad_alpha, grad_delta, grad_beta, grad_gamma_early = front_pull(
        (grad_masked, grad_normed, grad_local, adjoint, grad_powers)
    )
    grad_gamma = grad_gamma_early + grad_gamma_late
    shards = (
        lax.psum_scatter(grad_first, "seq", scatter_dimension=0, tiled=True),
        lax.psum_scatter(grad_alpha, "seq", scatter_dimension=0, tiled=True),
        lax.psum_scatter(grad_delta, "seq", scatter_dimension=0, tiled=True),
        lax.psum_scatter(grad_beta, "seq", scatter_dimension=0, tiled=True),
        lax.psum_scatter(grad_gamma, "seq", scatter_dimension=0, tiled=True),
        lax.psum_scatter(grad_omega, "seq", scatter_dimension=0, tiled=True),
        lax.psum_scatter(grad_value, "seq", scatter_dimension=0, tiled=True),
        lax.psum_scatter(grad_mix, "seq", scatter_dimension=0, tiled=True),
        lax.psum_scatter(grad_affine, "seq", scatter_dimension=0, tiled=True),
        lax.psum_scatter(grad_merge, "seq", scatter_dimension=0, tiled=True),
        lax.psum_scatter(grad_second, "seq", scatter_dimension=0, tiled=True),
        lax.psum_scatter(grad_widen, "seq", scatter_dimension=0, tiled=True),
        lax.psum_scatter(grad_narrow, "seq", scatter_dimension=0, tiled=True),
    )
    totals = lax.psum(
        (
            shards[0],
            shards[1],
            shards[2],
            shards[3],
            shards[4],
            shards[5],
            shards[6],
            shards[7],
            shards[8],
            shards[9],
            shards[10],
            shards[11],
            shards[12],
        ),
        "batch",
    )
    return (
        block_out,
        grad_tokens,
        totals[0],
        totals[1],
        totals[2],
        totals[3],
        totals[4],
        totals[5],
        totals[6],
        totals[7],
        totals[8],
        totals[9],
        totals[10],
        totals[11],
        totals[12],
    )


def solution(mesh):
    in_specs = (
        P("batch", "seq", None),
        P("batch"),
        P("batch", "seq", None),
        P("seq"),
        P("seq", None),
        P("seq", None),
        P("seq", None),
        P("seq", None),
        P("seq"),
        P("seq", None),
        P("seq", None),
        P("seq", None),
        P("seq", None),
        P("seq"),
        P("seq", None),
        P("seq", None),
    )
    out_specs = (
        P("batch", "seq", None),
        P("batch", "seq", None),
        P("seq"),
        P("seq", None),
        P("seq", None),
        P("seq", None),
        P("seq", None),
        P("seq"),
        P("seq", None),
        P("seq", None),
        P("seq", None),
        P("seq", None),
        P("seq"),
        P("seq", None),
        P("seq", None),
    )
    return jax.shard_map(
        per_device, mesh=mesh, in_specs=in_specs, out_specs=out_specs, check_vma=False
    )
```

profile of v0, /device:TPU:0, one launch (start us, length us, event | category | flops | bytes accessed | tf_op | source)
XLA Modules:
  0.0 1648.6 jit_solution(1901059246262222921)
XLA Ops:
  7.3 10.3 all-gather.2
  24.4 8.9 all_gather.59
  33.4 8.2 all_gather.58
  41.6 8.9 all_gather.56
  50.5 8.2 all_gather.57
  59.6 7.6 multiply_exponential_fusion
  67.4 7.3 slice.62
  74.7 13.1 rev.12
  87.8 16.4 broadcast_multiply_fusion
  109.5 7.2 slice.63
  117.1 128.9 %fusion.46 = f32[1024,128,128]{2,1,0:T(8,128)} fusion(f32[1024,16]{1,0:T(8,128)S(1)} %copy.244, f32[128]{0:T(128)S(1)} %get-tuple-element.374, f32[1024,16]{1,0:T(8,128)S(1)} %copy.245, f32[129,1024,16]{0,2,1:T(8,128)} %multiply_exponential_fusion), kind=kOutput, calls=%fused_computation.63 | convolution fusion | flops 3225419776 | bytes 75629056 | tf_op jit(solution)/shard_map/jvp(tdn,sdn->dts)/dot_general | solution.py:45
  246.1 109.5 %fusion.8 = f32[1024,2,128]{2,1,0:T(2,128)} fusion(f32[2,128,1024]{1,0,2:T(2,128)S(1)} %copy.247, f32[1024,128,128]{2,1,0:T(8,128)} %fusion.46, pred[128,128]{1,0:T(8,128)(4,1)S(1)} %broadcast_compare_fusion), kind=kOutput, calls=%fused_computation.12 | convolution fusion | flops 419430400 | bytes 69222400 | tf_op jit(solution)/shard_map/jvp(dts,bsd->btd)/dot_general | solution.py:154
  357.8 5.3 copy.248
  364.1 8.9 all-gather.4
  373.0 7.8 all-gather.3
  380.8 8.7 all-gather.5
  389.5 11.4 all_gather.60
  400.9 7.3 while.28
  410.2 14.7 fusion.50
  427.2 2.8 bitcast_add_fusion.2
  430.1 10.6 fusion.44
  440.6 21.5 %fusion.20 = f32[2,128,4224]{2,1,0:T(8,128)S(1)} fusion(f32[1024,4224]{1,0:T(8,128)} %all-gather.14.cloned.1.call-done, f32[2,128,1024]{2,1,0:T(8,128)} %bitcast_add_fusion.2), kind=kOutput, calls=%fused_computation.24 | convolution fusion | flops 13288603648 | bytes 22675456 | tf_op jit(solution)/shard_map/jvp(bld,dk->blk)/dot_general | solution.py:68
  464.7 3.6 fusion.133
  468.3 14.9 fusion.184
  483.6 18.7 %fusion.32 = f32[2,128,4096]{2,1,0:T(8,128)} fusion(f32[1024,4096]{1,0:T(8,128)} %all-gather.20.cloned.1.call-done, f32[2,128,1024]{2,1,0:T(8,128)S(1)} %get-tuple-element.354, f32[1024]{0:T(1024)S(1)} %bitcast.169, f32[2,128]{1,0:T(2,128)S(1)} %fusion.159, f32[2,128]{1,0:T(2,128)S(1)} %broadcast_multiply_fusion.3), kind=kOutput, calls=%fused_computation.37 | convolution fusion | flops 12885688320 | bytes 22026240 | tf_op jit(solution)/shard_map/jvp(bld,df->blf)/dot_general | solution.py:92
  502.3 19.8 %all-gather.22.cloned.1.call-done = f32[4096,1024]{1,0:T(8,128)} async-done(((f32[512,1024]{1,0:T(8,128)}), f32[4096,1024]{1,0:T(8,128)}) %all-gather.22.cloned.1.call-update) | async-done | bytes 16777232 | tf_op jit(solution)/shard_map/all_gather | solution.py:211
  522.1 20.6 %fusion.52 = f32[2,128,4096]{2,1,0:T(8,128)} fusion(f32[2,128,4096]{2,1,0:T(8,128)} %fusion.32, f32[4096,1024]{1,0:T(8,128)} %all-gather.22.cloned.1.call-done, f32[2,128,1024]{2,1,0:T(8,128)} %param.22, f32[2,128]{1,0:T(2,128)S(1)} %get-tuple-element.372), kind=kOutput, calls=%fused_computation.74 | convolution fusion | flops 12894601216 | bytes 26215424 | tf_op jit(solution)/shard_map/transpose(jvp(blf,fd->bld))/dot_general | solution.py:94
  542.7 17.0 %multiply_reduce_fusion.5 = (f32[2,128]{1,0:T(2,128)S(1)}, f32[2,128,1024]{2,1,0:T(8,128)S(1)}) fusion(f32[2,128,1024]{2,1,0:T(8,128)S(1)} %get-tuple-element.354, f32[1024]{0:T(1024)S(1)} %bitcast.170, f32[2,128]{1,0:T(2,128)S(1)} %broadcast_multiply_fusion.3, f32[2,128,4096]{2,1,0:T(8,128)} %fusion.52, f32[1024,4096]{1,0:T(8,128)S(1)} %copy-done), kind=kOutput, calls=%fused_computation.131 | convolution fusion | flops 12885950464 | bytes 23074816 | tf_op jit(solution)/shard_map/transpose(jvp(bld,df->blf))/dot_general | solution.py:92
  564.0 11.7 fusion.69
  575.7 6.0 multiply_reduce_fusion.12
  583.2 16.5 multiply_reduce_fusion.1
  601.2 19.5 %fusion.74 = f32[2,1024,16]{2,0,1:T(2,128)} fusion(f32[1024,2,128]{2,1,0:T(2,128)S(1)} %copy.259, f32[129,1024,16]{0,2,1:T(8,128)} %multiply_exponential_fusion, f32[1024,16]{1,0:T(8,128)} %copy.252), kind=kOutput, calls=%fused_computation.101 | convolution fusion | flops 52428800 | bytes 10092544 | tf_op jit(solution)/shard_map/transpose(jvp(tdn,bdn->btd))/dot_general | solution.py:174
  622.8 5.9 fusion.71
  630.0 9.4 convolution_bitcast_fusion.4
  639.5 11.3 convolution_bitcast_fusion.3
  650.8 17.8 %convolution_bitcast_fusion.2 = f32[1024,4096]{1,0:T(8,128)} fusion(f32[2,128,4096]{2,1,0:T(8,128)} %fusion.52, f32[2,128,1024]{2,1,0:T(8,128)S(1)} %get-tuple-element.354, f32[1024]{0:T(1024)S(1)} %bitcast.173, f32[2,128]{1,0:T(2,128)S(1)} %fusion.159, f32[2,128]{1,0:T(2,128)S(1)} %broadcast_multiply_fusion.3), kind=kOutput, calls=%fused_computation.43 | convolution fusion | flops 12885688320 | bytes 22026240 | tf_op jit(solution)/shard_map/transpose(jvp(bld,df->blf))/dot_general | solution.py:92
  669.9 18.1 %convolution_bitcast_fusion.1 = f32[4096,1024]{1,0:T(8,128)} fusion(f32[2,128,1024]{2,1,0:T(8,128)S(1)} %copy-done.39, f32[2,128,4096]{2,1,0:T(8,128)} %fusion.32, f32[2,128]{1,0:T(2,128)S(1)} %get-tuple-element.372), kind=kOutput, calls=%fused_computation.42 | convolution fusion | flops 12889358336 | bytes 22021120 | tf_op jit(solution)/shard_map/transpose(jvp(blf,fd->bld))/dot_general | solution.py:94
  689.2 20.4 %convolution_bitcast_fusion = f32[1024,4224]{1,0:T(8,128)} fusion(f32[2,128,1024]{2,1,0:T(8,128)} %copy-done.22, f32[2,128,128]{2,1,0:T(8,128)S(1)} %get-tuple-element.359, f32[2,128,2048]{2,1,0:T(8,128)} %copy-done.13, f32[2,128,1024]{2,1,0:T(8,128)} %copy-done.16, f32[2,128,1024]{2,1,0:T(8,128)S(1)} %copy-done.15), kind=kOutput, calls=%fused_computation.41 | convolution fusion | flops 13291847680 | bytes 22675456 | tf_op jit(solution)/shard_map/transpose(jvp(bld,dk->blk))/dot_general | solution.py:68
  711.4 110.4 %fusion.188 = f32[1024,128,128]{2,1,0:T(8,128)} fusion(f32[1024,2,128]{2,1,0:T(2,128)S(1)} %copy.259, f32[2,128,1024]{1,0,2:T(2,128)S(1)} %copy.247), kind=kOutput, calls=%fused_computation.243 | convolution fusion | flops 402653184 | bytes 69206016 | tf_op jit(solution)/shard_map/transpose(jvp(dts,bsd->btd))/dot_general | solution.py:154
  821.9 114.4 %fusion.4 = f32[1024,128,16]{1,2,0:T(8,128)} fusion(f32[1024,128,128]{2,1,0:T(8,128)} %fusion.188, pred[128,128]{1,0:T(8,128)(4,1)} %copy-done.31, f32[1024,16]{1,0:T(8,128)} %copy-done.10, f32[128]{0:T(128)S(1)} %copy-done.62), kind=kOutput, calls=%fused_computation.8 | convolution fusion | flops 3240099840 | bytes 75579904 | tf_op jit(solution)/shard_map/transpose(jvp(tdn,sdn->dts))/dot_general | solution.py:45
  936.3 30.4 %fusion.34 = (f32[1024,16]{1,0:T(8,128)}, f32[1024,16]{1,0:T(8,128)}, f32[128,1024,16]{0,2,1:T(8,128)}, f32[128,1024,16]{0,2,1:T(8,128)}) fusion(f32[129,1024,16]{0,2,1:T(8,128)S(1)} %bitcast.163, f32[1024,128,16]{1,2,0:T(8,128)} %fusion.4, f32[1024,16]{1,0:T(8,128)} %copy-done.17, f32[1024,16]{1,0:T(8,128)} %copy.252, f32[1024,2,128]{2,1,0:T(2,128)} %copy-done.5, ...), kind=kOutput, calls=%fused_computation.47 | convolution fusion | flops 62881792 | bytes 43384832 | tf_op jit(solution)/shard_map/transpose(jvp(tdn,bdn->btd))/dot_general | solution.py:174
  968.0 64.9 %fusion.36 = f32[1024,16]{1,0:T(8,128)S(1)} fusion(f32[1024,16]{1,0:T(8,128)} %copy-done.10, f32[128]{0:T(128)S(1)} %copy-done.62, f32[1024,16]{1,0:T(8,128)} %copy-done.17, f32[1024,128,128]{2,1,0:T(8,128)} %fusion.188, pred[128,128]{1,0:T(8,128)(4,1)} %copy-done.31, f32[129,1024,16]{0,2,1:T(8,128)} %multiply_exponential_fusion), kind=kOutput, calls=%fused_computation.50 | convolution fusion | flops 3248472064 | bytes 76628480 | tf_op jit(solution)/shard_map/transpose(jvp(tdn,sdn->dts))/dot_general | solution.py:45
  1034.6 9.0 pad_slice_fusion
  1043.7 2.8 rev.14
  1046.5 13.4 while.29
  1061.8 4.1 multiply_reduce_fusion.2
  1067.1 6.0 copy.273
  1073.1 12.1 slice_add_fusion
  1085.2 15.5 convolution_bitcast_fusion.5
  1100.7 13.5 rev.15
  1114.2 31.4 %fusion.25 = f32[1024,16]{1,0:T(8,128)S(1)} fusion(f32[1,1024,16]{0,2,1:T(8,128)} %slice_add_fusion, f32[128,1024,16]{0,2,1:T(8,128)} %pad_slice_fusion, f32[128,1024,16]{0,2,1:T(8,128)} %get-tuple-element.357, f32[128,1024,16]{0,2,1:T(8,128)} %rev.15, f32[1024,16]{1,0:T(8,128)S(1)} %copy-done.11), kind=kLoop, calls=%fused_computation.30 | loop fusion | flops 14778368 | bytes 25362432 | tf_op jit(solution)/shard_map/transpose(jvp())/reduce_sum | solution.py:40
  1148.6 8.9 reduce-scatter.23.cloned.1.call-done
  1158.8 60.9 %fusion.6 = f32[1024,2,128]{2,1,0:T(2,128)S(1)} fusion(f32[1024,2,128]{2,1,0:T(2,128)S(1)} %copy-done.6, f32[1024,128,128]{2,1,0:T(8,128)} %fusion.46, pred[128,128]{1,0:T(8,128)(4,1)S(1)} %copy-done.32), kind=kOutput, calls=%fused_computation.10 | convolution fusion | flops 419430400 | bytes 69222400 | tf_op jit(solution)/shard_map/transpose(jvp(dts,bsd->btd))/dot_general | solution.py:154
  1221.0 19.0 %fusion.78 = f32[2,128,1024]{2,1,0:T(8,128)} fusion(f32[2,128,1024]{2,1,0:T(8,128)S(1)} %copy-done.4, f32[4096,1024]{1,0:T(8,128)} %all-gather.22.cloned.1.call-done, f32[2,128,4096]{2,1,0:T(8,128)} %fusion.32, f32[2,128]{1,0:T(2,128)S(1)} %copy-done.56), kind=kOutput, calls=%fused_computation.104 | convolution fusion | flops 12889620480 | bytes 23069696 | tf_op jit(solution)/shard_map/jvp(blf,fd->bld)/dot_general | solution.py:94
  1240.9 9.5 fusion.103
  1251.7 11.8 multiply_reduce_fusion.4
  1264.1 23.1 %all-reduce.13 = (f32[1024]{0:T(1024)S(1)}, f32[1024]{0:T(1024)S(1)}, f32[1024]{0:T(1024)S(1)}) all-reduce(f32[1024]{0:T(1024)S(1)} %get-tuple-element.310, f32[1024]{0:T(1024)S(1)} %copy-done.66, f32[1024]{0:T(1024)S(1)} %copy-done.65), channel_id=4, replica_groups=mesh['seq'=8,'batch'=4] {'seq'}, use_global_device_ids=true, to_apply=%region_16.17.clone | all-reduce | flops 3072 | bytes 24576
  1287.4 2.8 add_multiply_fusion
  1290.2 8.2 reduce-scatter.17.cloned.1.call-done
  1298.4 34.6 %reduce-scatter.19.cloned.1.call-done = f32[128,16]{0,1:T(8,128)} async-done(((f32[1024,16]{0,1:T(8,128)}), f32[128,16]{0,1:T(8,128)}) %reduce-scatter.19.cloned.1.call-update) | async-done | bytes 8208 | tf_op jit(solution)/shard_map/reduce_scatter | solution.py:260
  1333.0 22.0 %all-reduce.14 = (f32[128]{0:T(128)}, f32[128,16]{0,1:T(8,128)}, f32[128,16]{0,1:T(8,128)}, f32[128,16]{0,1:T(8,128)}, f32[128,16]{0,1:T(8,128)}, /*index=5*/f32[128]{0:T(128)}, f32[16,3]{0,1:T(4,128)}, f32[128]{0:T(128)}) all-reduce(f32[128]{0:T(128)S(1)} %dynamic-slice.1, ...), channel_id=1, replica_groups=mesh['seq'=8,'batch'=4] {'batch'}, use_global_device_ids=true, to_apply=%region_17.18 | all-reduce | flops 8624 | bytes 68992 | tf_op jit(solution)/shard_map/psum | solution.py:270
  1355.0 277.3 %all-reduce.18.cloned.1.call-done = (f32[128,2048]{1,0:T(8,128)}, f32[128,4224]{1,0:T(8,128)}, f32[256,1024]{1,0:T(8,128)}, f32[128,4096]{1,0:T(8,128)}, f32[512,1024]{1,0:T(8,128)}) async-done(((f32[128,2048]{1,0:T(8,128)}, f32[128,4224]{1,0:T(8,128)}, f32[256,1024]{1,0:T(8,128)}, f32[128,4096]{1,0:T(8,128)}, f32[512,1024]{1,0:T(8,128)}), (f32[128,2048]{1,0:T(8,128)}, f32[128,4224]{1,0:T(8,128)}, ...) | async-done | bytes 8454160 | tf_op jit(solution)/shard_map/psum | solution.py:270
  1632.3 2.4 copy.310
  1634.7 3.2 copy.311
  (330 shorter events, 76.3 us)
Async XLA Ops:
  7.2 26.2 %copy-start.70 = (f32[128,16]{0,1:T(8,128)S(1)}, f32[128,16]{0,1:T(8,128)}, u32[]{:S(2)}) copy-start(f32[128,16]{0,1:T(8,128)} %param.26) | copy-start | bytes 24580
  7.2 34.4 %copy-start.71 = (f32[128,16]{0,1:T(8,128)S(1)}, f32[128,16]{0,1:T(8,128)}, u32[]{:S(2)}) copy-start(f32[128,16]{0,1:T(8,128)} %param.24) | copy-start | bytes 24580
  7.2 43.3 %copy-start.72 = (f32[128,16]{0,1:T(8,128)S(1)}, f32[128,16]{0,1:T(8,128)}, u32[]{:S(2)}) copy-start(f32[128,16]{0,1:T(8,128)} %param.25) | copy-start | bytes 24580
  7.2 393.7 %all-gather.24.cloned.1.call-start = ((), (), s32[]{:S(2)}) async-start(), calls=%async_computation.24 | async-start | bytes 1179648 | tf_op jit(solution)/shard_map/all_gather | solution.py:13
  17.6 409.6 %copy-start.53 = (f32[8,1,128]{2,1,0:T(1,128)}, f32[8,1,128]{2,1,0:T(1,128)S(1)}, u32[]{:S(2)}) copy-start(f32[8,1,128]{2,1,0:T(1,128)S(1)} %all-gather.2) | copy-start | bytes 12292
  18.8 649.9 %copy-start.55 = (f32[2,128]{1,0:T(2,128)}, f32[2,128]{1,0:T(2,128)S(1)}, u32[]{:S(2)}) copy-start(f32[2,128]{1,0:T(2,128)S(1)} %get-tuple-element.372) | copy-start | bytes 3076
  20.3 406.9 %copy-start.59 = (f32[2,128]{1,0:T(2,128)}, f32[2,128]{1,0:T(2,128)S(1)}, u32[]{:S(2)}) copy-start(f32[2,128]{1,0:T(2,128)S(1)} %broadcast_multiply_fusion.4) | copy-start | bytes 3076
  21.8 405.4 %copy-start.63 = (f32[2,128]{1,0:T(2,128)}, f32[2,128]{1,0:T(2,128)S(1)}, u32[]{:S(2)}) copy-start(f32[2,128]{1,0:T(2,128)S(1)} %fusion.158) | copy-start | bytes 3076
  23.8 406.2 %copy-start.7 = (f32[2,128,1024]{2,1,0:T(8,128)}, f32[2,128,1024]{2,1,0:T(8,128)S(1)}, u32[]{:S(2)}) copy-start(f32[2,128,1024]{2,1,0:T(8,128)S(1)} %multiply_multiply_fusion) | copy-start | bytes 3145732
  33.4 33.8 %copy-start.43 = (f32[1024,16]{0,1:T(8,128)}, f32[1024,16]{0,1:T(8,128)S(1)}, u32[]{:S(2)}) copy-start(f32[1024,16]{0,1:T(8,128)S(1)} %all_gather.59) | copy-start | bytes 196612
  41.6 25.6 %copy-start.45 = (f32[1024,16]{0,1:T(8,128)}, f32[1024,16]{0,1:T(8,128)S(1)}, u32[]{:S(2)}) copy-start(f32[1024,16]{0,1:T(8,128)S(1)} %all_gather.58) | copy-start | bytes 196612
  59.6 57.4 %copy-start.10 = (f32[1024,16]{1,0:T(8,128)}, f32[1024,16]{1,0:T(8,128)S(1)}, u32[]{:S(2)}) copy-start(f32[1024,16]{1,0:T(8,128)S(1)} %copy.244) | copy-start | bytes 196612
  106.2 323.8 %all-gather.16.cloned.1.call-start = ((), (), s32[]{:S(2)}) async-start(), calls=%async_computation.11 | async-start | bytes 9437184 | tf_op jit(solution)/shard_map/all_gather | solution.py:130
  107.0 333.6 %all-gather.14.cloned.1.call-start = ((), (), s32[]{:S(2)}) async-start(), calls=%async_computation.10 | async-start | bytes 19464192 | tf_op jit(solution)/shard_map/all_gather | solution.py:131
  107.7 360.6 %all-gather.18.cloned.1.call-start = ((), (), s32[]{:S(2)}) async-start(), calls=%async_computation.12 | async-start | bytes 9437184 | tf_op jit(solution)/shard_map/all_gather | solution.py:133
  108.3 375.3 %all-gather.20.cloned.1.call-start = ((), (), s32[]{:S(2)}) async-start(), calls=%async_computation.13 | async-start | bytes 18874368 | tf_op jit(solution)/shard_map/all_gather | solution.py:210
  108.9 413.2 %all-gather.22.cloned.1.call-start = ((), (), s32[]{:S(2)}) async-start(), calls=%async_computation.14 | async-start | bytes 18874368 | tf_op jit(solution)/shard_map/all_gather | solution.py:211
  109.4 934.3 %all-gather.26.cloned.1.call-start = ((), (), s32[]{:S(2)}) async-start(), calls=%async_computation.25 | async-start | bytes 1179648 | tf_op jit(solution)/shard_map/all_gather | solution.py:13
  116.9 129.1 %copy-start.17 = (f32[1024,16]{1,0:T(8,128)}, f32[1024,16]{1,0:T(8,128)S(1)}, u32[]{:S(2)}) copy-start(f32[1024,16]{1,0:T(8,128)S(1)} %copy.245) | copy-start | bytes 196612
  116.9 129.1 %copy-start.61 = (f32[128]{0:T(128)}, f32[128]{0:T(128)S(1)}, u32[]{:S(2)}) copy-start(f32[128]{0:T(128)S(1)} %get-tuple-element.374) | copy-start | bytes 1540
  117.0 129.0 %copy-start.31 = (pred[128,128]{1,0:T(8,128)(4,1)}, pred[128,128]{1,0:T(8,128)(4,1)S(1)}, u32[]{:S(2)}) copy-start(pred[128,128]{1,0:T(8,128)(4,1)S(1)} %broadcast_compare_fusion) | copy-start | bytes 49156
  357.8 23.0 %copy-start.75 = (f32[128]{0:T(128)S(1)}, f32[128]{0:T(128)}, u32[]{:S(2)}) copy-start(f32[128]{0:T(128)} %param.33) | copy-start | bytes 1540
  380.8 46.4 %copy-start.57 = (f32[8,1,128]{2,1,0:T(1,128)}, f32[8,1,128]{2,1,0:T(1,128)S(1)}, u32[]{:S(2)}) copy-start(f32[8,1,128]{2,1,0:T(1,128)S(1)} %all-gather.3) | copy-start | bytes 12292
  440.6 23.6 %copy-start.76 = (pred[2,128]{1,0:T(4,128)(4,1)S(1)}, pred[2,128]{1,0:T(4,128)(4,1)}, u32[]{:S(2)}) copy-start(pred[2,128]{1,0:T(4,128)(4,1)} %get-tuple-element.371) | copy-start | bytes 772
  440.6 24.1 %copy-start.37 = (f32[2,128,2048]{2,1,0:T(8,128)S(1)}, f32[2,128,2048]{2,1,0:T(8,128)}, u32[]{:S(2)}) copy-start(f32[2,128,2048]{2,1,0:T(8,128)} %fusion.44) | copy-start | bytes 6291460
  483.3 167.6 %copy-start.3 = (f32[2,128,1024]{2,1,0:T(8,128)}, f32[2,128,1024]{2,1,0:T(8,128)S(1)}, u32[]{:S(2)}) copy-start(f32[2,128,1024]{2,1,0:T(8,128)S(1)} %get-tuple-element.354) | copy-start | bytes 3145732
  522.1 20.6 %copy-start = (f32[1024,4096]{1,0:T(8,128)S(1)}, f32[1024,4096]{1,0:T(8,128)}, u32[]{:S(2)}) copy-start(f32[1024,4096]{1,0:T(8,128)} %all-gather.20.cloned.1.call-done) | copy-start | bytes 50331652
  563.1 20.0 %copy-start.22 = (f32[2,128,1024]{2,1,0:T(8,128)}, f32[2,128,1024]{2,1,0:T(8,128)S(1)}, u32[]{:S(2)}) copy-start(f32[2,128,1024]{2,1,0:T(8,128)S(1)} %get-tuple-element.351) | copy-start | bytes 3145732
  564.0 19.2 %copy-start.16 = (f32[2,128,1024]{2,1,0:T(8,128)}, f32[2,128,1024]{2,1,0:T(8,128)S(1)}, u32[]{:S(2)}) copy-start(f32[2,128,1024]{2,1,0:T(8,128)S(1)} %fusion.95) | copy-start | bytes 3145732
  564.0 19.2 %slice-start.4 = ((s8[17301504]{0:T(1024)(128)(4,1)}), s8[4194304]{0:T(1024)(128)(4,1)S(1)}, s32[]{:S(2)}) async-start(s8[17301504]{0:T(1024)(128)(4,1)} %bitcast.164), calls=%async_computation.32 | async-start | bytes 8388608
  564.0 19.2 %slice-start.5 = ((s8[17301504]{0:T(1024)(128)(4,1)}), s8[4194304]{0:T(1024)(128)(4,1)S(1)}, s32[]{:S(2)}) async-start(s8[17301504]{0:T(1024)(128)(4,1)} %bitcast.164), calls=%async_computation.33 | async-start | bytes 8388608
  564.0 19.2 %slice-start.6 = ((s8[17301504]{0:T(1024)(128)(4,1)}), s8[4194304]{0:T(1024)(128)(4,1)S(1)}, s32[]{:S(2)}) async-start(s8[17301504]{0:T(1024)(128)(4,1)} %bitcast.164), calls=%async_computation.34 | async-start | bytes 8388608
  601.2 110.2 %copy-start.5 = (f32[1024,2,128]{2,1,0:T(2,128)}, f32[1024,2,128]{2,1,0:T(2,128)S(1)}, u32[]{:S(2)}) copy-start(f32[1024,2,128]{2,1,0:T(2,128)S(1)} %copy.259) | copy-start | bytes 3145732
  622.7 525.7 %reduce-scatter.21.cloned.1.call-start = ((), (), s32[]{:S(2)}) async-start(), calls=%async_computation.19 | async-start | bytes 9437184 | tf_op jit(solution)/shard_map/reduce_scatter | solution.py:262
  639.4 509.1 %reduce-scatter.25.cloned.1.call-start = ((), (), s32[]{:S(2)}) async-start(), calls=%async_computation.21 | async-start | bytes 9437184 | tf_op jit(solution)/shard_map/reduce_scatter | solution.py:265
  650.8 497.7 %reduce-scatter.27.cloned.1.call-start = ((), (), s32[]{:S(2)}) async-start(), calls=%async_computation.22 | async-start | bytes 18874368 | tf_op jit(solution)/shard_map/reduce_scatter | solution.py:267
  668.7 479.8 %reduce-scatter.29.cloned.1.call-start = ((), (), s32[]{:S(2)}) async-start(), calls=%async_computation.23 | async-start | bytes 18874368 | tf_op jit(solution)/shard_map/reduce_scatter | solution.py:268
  688.0 469.5 %reduce-scatter.23.cloned.1.call-start = ((), (), s32[]{:S(2)}) async-start(), calls=%async_computation.20 | async-start | bytes 19464192 | tf_op jit(solution)/shard_map/reduce_scatter | solution.py:263
  709.6 530.5 %reduce-scatter.31.cloned.1.call-start = ((), (), s32[]{:S(2)}) async-start(), calls=%async_computation.26 | async-start | bytes 73728
  711.4 110.4 %copy-start.62 = (f32[128]{0:T(128)S(1)}, f32[128]{0:T(128)}, u32[]{:S(2)}) copy-start(f32[128]{0:T(128)} %copy-done.61) | copy-start | bytes 1540
  711.4 224.8 %slice-start = ((s8[16777216]{0:T(1024)(128)(4,1)}), s8[4194304]{0:T(1024)(128)(4,1)S(1)}, s32[]{:S(2)}) async-start(s8[16777216]{0:T(1024)(128)(4,1)} %bitcast.162), calls=%async_computation.28 | async-start | bytes 8388608
  711.4 224.8 %slice-start.1 = ((s8[16777216]{0:T(1024)(128)(4,1)}), s8[4194304]{0:T(1024)(128)(4,1)S(1)}, s32[]{:S(2)}) async-start(s8[16777216]{0:T(1024)(128)(4,1)} %bitcast.162), calls=%async_computation.29 | async-start | bytes 8388608
  821.9 114.4 %slice-start.2 = ((s8[16777216]{0:T(1024)(128)(4,1)}), s8[4194304]{0:T(1024)(128)(4,1)S(1)}, s32[]{:S(2)}) async-start(s8[16777216]{0:T(1024)(128)(4,1)} %bitcast.162), calls=%async_computation.30 | async-start | bytes 8388608
  821.9 114.4 %slice-start.3 = ((s8[16777216]{0:T(1024)(128)(4,1)}), s8[4194304]{0:T(1024)(128)(4,1)S(1)}, s32[]{:S(2)}) async-start(s8[16777216]{0:T(1024)(128)(4,1)} %bitcast.162), calls=%async_computation.31 | async-start | bytes 8388608
  968.0 65.1 %copy-start.33 = (f32[1024,16]{1,0:T(8,128)S(1)}, f32[1024,16]{1,0:T(8,128)}, u32[]{:S(2)}) copy-start(f32[1024,16]{1,0:T(8,128)} %get-tuple-element.306) | copy-start | bytes 196612
  968.0 65.9 %copy-start.77 = (f32[128]{0:T(128)S(1)}, f32[128]{0:T(128)}, u32[]{:S(2)}) copy-start(f32[128]{0:T(128)} %get-tuple-element.308) | copy-start | bytes 1540
  968.0 65.9 %copy-start.78 = (f32[128]{0:T(128)S(1)}, f32[128]{0:T(128)}, u32[]{:S(2)}) copy-start(f32[128]{0:T(128)} %get-tuple-element.309) | copy-start | bytes 1540
  968.0 65.9 %copy-start.79 = (f32[128]{0:T(128)S(1)}, f32[128]{0:T(128)}, u32[]{:S(2)}) copy-start(f32[128]{0:T(128)} %get-tuple-element.314) | copy-start | bytes 1540
  1043.6 18.2 %copy-start.27 = (f32[2,1024,16]{2,0,1:T(2,128)S(1)}, f32[2,1024,16]{2,0,1:T(2,128)}, u32[]{:S(2)}) copy-start(f32[2,1024,16]{2,0,1:T(2,128)} %get-tuple-element.376) | copy-start | bytes 393220
  1043.6 246.6 %reduce-scatter.13.cloned.1.call-start = ((), (), s32[]{:S(2)}) async-start(), calls=%async_computation.15 | async-start | bytes 73728 | tf_op jit(solution)/shard_map/reduce_scatter | solution.py:257
  1061.8 23.5 %copy-start.18 = (f32[2,1024,16]{2,0,1:T(2,128)}, f32[2,1024,16]{2,0,1:T(2,128)S(1)}, u32[]{:S(2)}) copy-start(f32[2,1024,16]{2,0,1:T(2,128)S(1)} %copy.262) | copy-start | bytes 393220
  1114.2 31.6 %copy-start.44 = (f32[1024,16]{0,1:T(8,128)S(1)}, f32[1024,16]{0,1:T(8,128)}, u32[]{:S(2)}) copy-start(f32[1024,16]{0,1:T(8,128)} %copy-done.43) | copy-start | bytes 196612
  1114.2 31.6 %copy-start.46 = (f32[1024,16]{0,1:T(8,128)S(1)}, f32[1024,16]{0,1:T(8,128)}, u32[]{:S(2)}) copy-start(f32[1024,16]{0,1:T(8,128)} %copy-done.45) | copy-start | bytes 196612
  1114.2 31.6 %copy-start.48 = (f32[1024,16]{0,1:T(8,128)S(1)}, f32[1024,16]{0,1:T(8,128)}, u32[]{:S(2)}) copy-start(f32[1024,16]{0,1:T(8,128)} %copy-done.47) | copy-start | bytes 196612
  1114.2 31.6 %copy-start.50 = (f32[1024,16]{0,1:T(8,128)S(1)}, f32[1024,16]{0,1:T(8,128)}, u32[]{:S(2)}) copy-start(f32[1024,16]{0,1:T(8,128)} %copy-done.49) | copy-start | bytes 196612
  1114.2 31.6 %copy-start.51 = (f32[1024,16]{0,1:T(8,128)S(1)}, f32[1024,16]{0,1:T(8,128)}, u32[]{:S(2)}) copy-start(f32[1024,16]{0,1:T(8,128)} %copy.277) | copy-start | bytes 196612
  1146.6 143.6 %reduce-scatter.15.cloned.1.call-start = ((), (), s32[]{:S(2)}) async-start(), calls=%async_computation.16 | async-start | bytes 73728 | tf_op jit(solution)/shard_map/reduce_scatter | solution.py:258
  1147.3 151.1 %reduce-scatter.17.cloned.1.call-start = ((), (), s32[]{:S(2)}) async-start(), calls=%async_computation.17 | async-start | bytes 73728 | tf_op jit(solution)/shard_map/reduce_scatter | solution.py:259
  1147.8 185.2 %reduce-scatter.19.cloned.1.call-start = ((), (), s32[]{:S(2)}) async-start(), calls=%async_computation.18 | async-start | bytes 73728 | tf_op jit(solution)/shard_map/reduce_scatter | solution.py:260
  1148.4 483.9 %all-reduce.18.cloned.1.call-start = ((), (), s32[]{:S(2)}) async-start(), calls=%async_computation.27 | async-start | bytes 16908288 | tf_op jit(solution)/shard_map/psum | solution.py:270
  1158.8 62.3 %copy-start.4 = (f32[2,128,1024]{2,1,0:T(8,128)S(1)}, f32[2,128,1024]{2,1,0:T(8,128)}, u32[]{:S(2)}) copy-start(f32[2,128,1024]{2,1,0:T(8,128)} %copy-done.3) | copy-start | bytes 3145732
  1158.8 62.3 %copy-start.56 = (f32[2,128]{1,0:T(2,128)S(1)}, f32[2,128]{1,0:T(2,128)}, u32[]{:S(2)}) copy-start(f32[2,128]{1,0:T(2,128)} %copy-done.55) | copy-start | bytes 3076
  1221.0 19.8 %copy-start.19 = (f32[2,1024,16]{2,0,1:T(2,128)S(1)}, f32[2,1024,16]{2,0,1:T(2,128)}, u32[]{:S(2)}) copy-start(f32[2,1024,16]{2,0,1:T(2,128)} %copy-done.18) | copy-start | bytes 393220
  1251.7 35.7 %copy-start.21 = (f32[2,128,1024]{2,1,0:T(8,128)S(1)}, f32[2,128,1024]{2,1,0:T(8,128)}, u32[]{:S(2)}) copy-start(f32[2,128,1024]{2,1,0:T(8,128)} %copy-done.20) | copy-start | bytes 3145732
  (46 other events, 423.6 us)
Sparse Core Ops, SparseCore 0:
  106.3 23.7 all-gather.23
  132.0 54.3 all-gather.15
  188.3 92.0 all-gather.13
  282.2 54.3 all-gather.17
  338.4 92.0 all-gather.19
  432.2 89.8 all-gather.21
  622.9 23.4 all-gather.25
  649.9 71.2 reduce-scatter.20
  725.0 71.2 reduce-scatter.24
  799.7 115.9 reduce-scatter.26
  919.3 115.9 reduce-scatter.28
  1038.9 118.5 reduce-scatter.22
  1160.7 33.2 reduce-scatter.30
  1197.4 31.4 reduce-scatter.12
  1232.0 31.4 reduce-scatter.14
  1266.9 31.4 reduce-scatter.16
  1301.5 31.4 reduce-scatter.18
  1336.0 296.2 all-reduce.17
where the time goes:
time: 1660 us; the launch traced here: 1650 us
  matrix products  951 us (57%)
  waiting for transfers between devices  354 us (21%)
  blocking collectives  126 us (8%)
  local copies, waits for them, and re-layouts  113 us (7%)
  other arithmetic  86.8 us (5%)
    dot_general x3, matrix products, smoothing_tables(): toeplitz = jnp.einsum('tdn,sdn->dts', weighted, rising, precision=precise)  308 us
    dot_general x3, matrix products, front_part(): local_sum = jnp.einsum('dts,bsd->btd', toeplitz, normed, precision=precise)  281 us
    psum x1, waiting for transfers between devices, per_device(): lax.psum((shards[0], shards[1], shards[2], shards[3], shards[4], shards[5...  277 us
    dot_general x3, matrix products, attn_part(): jnp.einsum('tdn,bdn->btd', powers[1:] * (project_gain * out_scale)[None],...  64.6 us
    dot_general x3, matrix products, gated_mix(): jnp.einsum('bld,dk->blk', mixed_in, mix_weight, precision=precise)  58.3 us
    dot_general x3, matrix products, feed_forward(): jnp.einsum('blf,fd->bld', hidden, narrow_weight, precision=precise)  57.7 us
    dot_general x3, matrix products, feed_forward(): jnp.einsum('bld,df->blf', normed_two, widen_weight, precision=precise)  53.5 us
    dot_general x3, matrix products, front_part(): jnp.einsum('sdn,bsd->bdn', powers[:block_len][::-1], normed, precision=pr...  41.3 us
  transfers between devices with their start and end apart: 18, of which 5 were waited for; matrix products, arithmetic and copies ran while one was open for 59% of the time, Pallas kernels for 0%

commit v1 on v0

v1 whole, which is shorter than its diff:
```python
import functools

import jax
import jax.numpy as jnp
from jax import lax
from jax.experimental import pallas as pl
from jax.experimental.pallas import tpu as pltpu
from jax.sharding import PartitionSpec as P

exact = lax.Precision.HIGHEST
triple = lax.Precision.HIGH
norm_eps = 1e-05
masked_score = -1000000000.0
lanes = 128


def swap(value, bit):
    count = lax.axis_size("seq")
    return lax.ppermute(value, "seq", [(i, i ^ bit) for i in range(count)])


def gather_rows(shard):
    count = lax.axis_size("seq")
    if count != 8:
        return lax.all_gather(shard, "seq", axis=0, tiled=True)
    me = lax.axis_index("seq")
    rows, columns = shard.shape
    half = rows // 2
    across_x = swap(shard, 2)
    across_y = swap(shard, 4)
    corner_top = swap(across_x[:half], 4)
    corner_low = swap(across_y[half:], 2)
    full = jnp.zeros((count, 2, half, columns), shard.dtype)
    pieces = (
        (shard.reshape(2, half, columns), 0, 0),
        (across_x.reshape(2, half, columns), 2, 0),
        (across_y.reshape(2, half, columns), 4, 0),
        (corner_top[None], 6, 0),
        (corner_low[None], 6, 1),
    )
    for piece, bit, part in pieces:
        full = lax.dynamic_update_slice(full, piece[None], (me ^ bit, part, 0, 0))
    for piece, bit, part in pieces:
        full = lax.dynamic_update_slice(full, swap(piece, 1)[None], (me ^ bit ^ 1, part, 0, 0))
    return full.reshape(count * rows, columns)


def product_grad(left, right):
    return lax.dot_general(left, right, (((0,), (0,)), ((), ())), precision=triple)


def split(value):
    high = lax.reduce_precision(value, 8, 7)
    return high.astype(jnp.bfloat16), (value - high).astype(jnp.bfloat16)


def slot_of(count):
    table, chunk, left, right = [], 0, 0, 0
    for lefts, rights in count:
        table.append((chunk, left, right, rights))
        chunk, left, right = chunk + lefts * rights, left + lefts, right + rights
    return table, chunk


def reduce_body(
    count, left_high, left_low, right_high, right_low, extra, out,
    away, keep, got, got_x, got_y, got_xy, got_yx, part, from_edge, from_inner, sent, came,
):
    table, chunks = slot_of(count)
    depth, delay = away.shape[0], 2
    me, place = lax.axis_index("seq"), lax.axis_index("batch")
    core, along_x, along_y = me % 2, (me // 2) % 2, me // 4
    is_edge = (place == 0) | (place == 3)
    partner = jnp.where(place < 2, 1 - place, 5 - place)
    sibling, across_x, across_y = (
        {"seq": me + bit * (1 - 2 * own)} for bit, own in ((1, core), (2, along_x), (4, along_y))
    )

    barrier = pltpu.get_barrier_semaphore()
    for target in (sibling, across_x, across_y, {"batch": partner}):
        pl.semaphore_signal(barrier, inc=1, device_id=target, device_id_type=pl.DeviceIdType.MESH)

    @pl.when(jnp.logical_not(is_edge))
    def _():
        pl.semaphore_signal(
            barrier, inc=1, device_id={"batch": 3 - place}, device_id_type=pl.DeviceIdType.MESH
        )
        pl.semaphore_wait(barrier, 5)

    @pl.when(is_edge)
    def _():
        pl.semaphore_wait(barrier, 4)

    def copy(kind, slot, source, target, device):
        return pltpu.make_async_remote_copy(
            src_ref=source, dst_ref=target, send_sem=sent.at[kind, slot], recv_sem=came.at[kind, slot],
            device_id=device, device_id_type=pl.DeviceIdType.MESH,
        )

    def link(kind, chunk):
        slot = chunk % depth
        pairs = (
            lambda: (away.at[slot], got.at[slot], sibling),
            lambda: (keep.at[slot, :, 1 - along_x, 0], got_x.at[slot], across_x),
            lambda: (keep.at[slot, 1 - along_y, :, 1], got_y.at[slot], across_y),
            lambda: (got_x.at[slot, 1 - along_y], got_xy.at[slot], across_y),
            lambda: (got_y.at[slot, 1 - along_x], got_yx.at[slot], across_x),
            lambda: (part.at[slot], from_edge.at[slot], {"batch": partner}),
            lambda: (part.at[slot], from_inner.at[slot], {"batch": 3 - place}),
            lambda: (out.at[chunk], out.at[chunk], {"batch": partner}),
        )
        return copy(kind, slot, *pairs[kind]())

    def start(chunk):
        slot = chunk % depth
        to_sibling = link(0, chunk)

        @pl.when(chunk < chunks)
        def _():
            left, right = chunk * 0, chunk * 0
            for first, first_left, first_right, rights in table:
                inside = chunk >= first
                left = jnp.where(inside, first_left + (chunk - first) // rights, left)
                right = jnp.where(inside, first_right + (chunk - first) % rights, right)

            def product(parity):
                high, low = left_high[left, parity], left_low[left, parity]
                other = right_high[right]
                dot = functools.partial(jnp.dot, preferred_element_type=jnp.float32)
                total = dot(high, other) + (dot(low, other) + dot(high, right_low[right]))
                return total.reshape(away.shape[1:])

            away[slot] = product(1 - core)
            to_sibling.start()
            keep[slot] = product(core)

        @pl.when(chunk == chunks)
        def _():
            away[slot] = extra[1 - core].reshape(away.shape[1:])
            to_sibling.start()
            keep[slot] = extra[core].reshape(away.shape[1:])

    def with_sibling(chunk):
        slot = chunk % depth
        to_sibling, first, second = (link(kind, chunk) for kind in (0, 1, 2))
        to_sibling.wait()
        keep[slot] = keep[slot] + got[slot]
        first.start()
        second.start()

    def with_neighbour(chunk):
        slot = chunk % depth
        first, second, third, fourth = (link(kind, chunk) for kind in (1, 2, 3, 4))
        first.wait()
        second.wait()
        got_x[slot] = got_x[slot] + keep[slot, :, along_x, 0]
        got_y[slot] = got_y[slot] + keep[slot, along_y, :, 1]
        third.start()
        fourth.start()

    def with_corner(chunk):
        slot = chunk % depth
        third, fourth, to_inner = (link(kind, chunk) for kind in (3, 4, 5))
        third.wait()
        fourth.wait()
        part[slot, 0] = got_x[slot, along_y] + got_xy[slot]
        part[slot, 1] = got_y[slot, along_x] + got_yx[slot]

        @pl.when(is_edge)
        def _():
            to_inner.start()

    def inner_sum(chunk):
        slot = chunk % depth
        to_inner, across = (link(kind, chunk) for kind in (5, 6))

        @pl.when(is_edge)
        def _():
            to_inner.wait_send()

        @pl.when(jnp.logical_not(is_edge))
        def _():
            to_inner.wait_recv()
            part[slot] = part[slot] + from_edge[slot]
            across.start()

    def total_sum(chunk):
        slot = chunk % depth
        across, to_edge = (link(kind, chunk) for kind in (6, 7))

        @pl.when(jnp.logical_not(is_edge))
        def _():
            across.wait()
            out[chunk] = (part[slot] + from_inner[slot]).reshape(out.shape[1:])
            to_edge.start()

    def finish(chunk):
        to_edge = link(7, chunk)

        @pl.when(is_edge)
        def _():
            to_edge.wait_recv()

        @pl.when(jnp.logical_not(is_edge))
        def _():
            to_edge.wait_send()

    phases = (start, with_sibling, with_neighbour, with_corner, inner_sum, total_sum, finish)

    def step(at, carry):
        for number in range(len(phases) - 1, -1, -1):
            chunk = at - number * delay

            @pl.when((chunk >= 0) & (chunk <= chunks))
            def _():
                phases[number](chunk)

        return carry

    lax.fori_loop(0, chunks + 1 + (len(phases) - 1) * delay, step, 0)


def reduce_grads(products, extra, width=256):
    rows = products[0][0].shape[0]
    lefts, rights, count = [], [], []
    for left, right in products:
        blocks = left.shape[1] // (8 * lanes)
        cut = left.reshape(rows, 4, 2, blocks, lanes).transpose(3, 2, 1, 4, 0)
        lefts.append(cut.reshape(blocks, 2, 4 * lanes, rows))
        wide = right.shape[1] // width
        rights.append(right.reshape(rows, wide, width).transpose(1, 0, 2))
        count.append((blocks, wide))
    left_high, left_low = split(jnp.concatenate(lefts, axis=0))
    right_high, right_low = split(jnp.concatenate(rights, axis=0))
    _, chunks = slot_of(count)
    pairs = extra.reshape(4, 2, lanes, width).transpose(1, 0, 2, 3).reshape(2, 4 * lanes, width)
    depth, half = 8, lanes // 2
    vmem = pl.BlockSpec(memory_space=pltpu.VMEM)
    out = pl.pallas_call(
        functools.partial(reduce_body, tuple(count)),
        out_shape=jax.ShapeDtypeStruct((chunks + 1, 2, half, width), jnp.float32),
        in_specs=[vmem] * 5,
        out_specs=vmem,
        scratch_shapes=[pltpu.VMEM((depth, 2, 2, 2, half, width), jnp.float32)] * 3
        + [pltpu.VMEM((depth, 2, half, width), jnp.float32)] * 2
        + [pltpu.VMEM((depth, half, width), jnp.float32)] * 2
        + [pltpu.VMEM((depth, 2, half, width), jnp.float32)] * 3
        + [pltpu.SemaphoreType.DMA((8, depth))] * 2,
        compiler_params=pltpu.CompilerParams(
            collective_id=1, has_side_effects=True, vmem_limit_bytes=60 * 1024 * 1024
        ),
    )(left_high, left_low, right_high, right_low, pairs)
    out = out.reshape(chunks + 1, lanes, width)
    grads = []
    for (blocks, wide), (first, _, _, _) in zip(count, slot_of(count)[0]):
        piece = out[first : first + blocks * wide].reshape(blocks, wide, lanes, width)
        grads.append(piece.transpose(0, 2, 1, 3).reshape(blocks * lanes, wide * width))
    return grads, out[chunks]


def all_grads(products, packed, single):
    count = lax.axis_size("seq")
    rows, features = packed.shape
    blocks = packed.reshape(rows, count, features // count).transpose(1, 0, 2)
    last = product_grad(*single)
    if count != 8 or lax.axis_size("batch") != 4:

        def total(whole, tiled):
            part = lax.psum_scatter(whole, "seq", scatter_dimension=0, tiled=tiled)
            return lax.psum(part, "batch")

        wholes = [total(product_grad(*pair), True) for pair in products]
        return wholes, total(blocks, False), total(last, True)
    blocks = jnp.pad(blocks, ((0, 0), (0, lanes - rows), (0, 0)))
    extra = jnp.concatenate([last.reshape(count, lanes, -1), blocks], axis=2)
    wholes, rest = reduce_grads(products, extra)
    return wholes, rest[:rows, lanes:], rest[:, :lanes]


def tree_sum(terms):
    while len(terms) > 1:
        terms = [a + b for a, b in zip(terms[::2], terms[1::2])] + (
            [terms[-1]] if len(terms) % 2 else []
        )
    return terms[0]


def filter_body(reverse, decay_ref, weight_ref, signal_ref, out_ref, end_ref):
    sequences, length = signal_ref.shape[:2]
    states = decay_ref.shape[0]
    for s in range(sequences):

        def step(t, held):
            at = length - 1 - t if reverse else t
            entry = signal_ref[s, at]
            held = tuple(decay_ref[n] * held[n] + entry for n in range(states))
            out_ref[s, at] = tree_sum([weight_ref[n] * held[n] for n in range(states)])
            return held

        zero = jnp.zeros(signal_ref.shape[2:], jnp.float32)
        held = lax.fori_loop(0, length, step, (zero,) * states, unroll=4)
        for n in range(states):
            end_ref[s, n] = held[n]


def carried_body(reverse, decay_ref, weight_ref, enter_ref, local_ref, out_ref):
    sequences, length = local_ref.shape[:2]
    states = decay_ref.shape[0]
    for s in range(sequences):

        def step(t, held):
            at = length - 1 - t if reverse else t
            held = tuple(decay_ref[n] * held[n] for n in range(states))
            out_ref[s, at] = local_ref[s, at] + tree_sum(list(held))
            return held

        start = tuple(weight_ref[n] * enter_ref[s, n] for n in range(states))
        lax.fori_loop(0, length, step, start, unroll=4)


def moments_body(decay_ref, enter_ref, signal_ref, grad_ref, direct_ref, slope_ref, last_ref):
    sequences, length = signal_ref.shape[:2]
    states = decay_ref.shape[0]
    group = min(8, states)
    zero = jnp.zeros(signal_ref.shape[2:], jnp.float32)
    for low in range(0, states, group):
        span = range(low, min(low + group, states))
        sums = ((zero,) * len(span), (zero,) * len(span))
        for s in range(sequences):

            def step(t, carry):
                held, slope, direct, sloped = carry
                entry, grad = signal_ref[s, t], grad_ref[s, t]
                slope = tuple(decay_ref[n] * d + h for n, d, h in zip(span, slope, held))
                held = tuple(decay_ref[n] * h + entry for n, h in zip(span, held))
                direct = tuple(q + grad * h for q, h in zip(direct, held))
                sloped = tuple(q + grad * d for q, d in zip(sloped, slope))
                return held, slope, direct, sloped

            start = (tuple(enter_ref[s, n] for n in span), (zero,) * len(span)) + sums
            _, slope, direct, sloped = lax.fori_loop(0, length, step, start, unroll=2)
            sums = (direct, sloped)
            for n, d in zip(span, slope):
                last_ref[s, n] = d
        for n, q, d in zip(span, *sums):
            direct_ref[n] = q
            slope_ref[n] = d


def call_kernel(body, shapes, *operands):
    return pl.pallas_call(
        body,
        out_shape=[jax.ShapeDtypeStruct(shape, jnp.float32) for shape in shapes],
        in_specs=[pl.BlockSpec(memory_space=pltpu.VMEM)] * len(operands),
        out_specs=[pl.BlockSpec(memory_space=pltpu.VMEM)] * len(shapes),
        compiler_params=pltpu.CompilerParams(vmem_limit_bytes=32 * 1024 * 1024),
    )(*operands)


def entering(ends, block_decay, backward):
    count, mine = lax.axis_size("seq"), lax.axis_index("seq")
    pieces = lax.all_gather(ends, "seq")
    if backward:
        mine = count - 1 - mine
    total = jnp.zeros_like(ends)
    for position in range(count - 1):
        piece = pieces[count - 1 - position if backward else position]
        total = jnp.where(position < mine, block_decay * total + piece, total)
    return total


def silu(value):
    return value * jax.nn.sigmoid(value)


def silu_slope(value):
    gate = jax.nn.sigmoid(value)
    return gate * (1.0 + value * (1.0 - gate))


def normalise(signal):
    centre = jnp.mean(signal, axis=-1, keepdims=True)
    shifted = signal - centre
    spread = jnp.mean(shifted * shifted, axis=-1, keepdims=True)
    scale = lax.rsqrt(spread + norm_eps)
    return shifted * scale, scale


def normalise_back(grad, gain, hat, scale):
    inner = grad * gain
    return (
        inner
        - jnp.mean(inner, axis=-1, keepdims=True)
        - hat * jnp.mean(inner * hat, axis=-1, keepdims=True)
    ) * scale


def times(left, right):
    return jnp.dot(left, right, precision=triple)


def times_back(left, right):
    return lax.dot_general(left, right, (((1,), (1,)), ((), ())), precision=triple)


def per_device(
    tokens,
    lengths,
    out_grad,
    first_gain,
    smooth_alpha,
    smooth_delta,
    smooth_beta,
    smooth_gamma,
    smooth_omega,
    value_weight,
    mix_weight,
    query_affine,
    merge_weight,
    second_gain,
    widen_weight,
    narrow_weight,
):
    sequences, block_len, width = tokens.shape
    count = lax.axis_size("seq")
    states = smooth_alpha.shape[1]
    own = first_gain.shape[0]
    own_shared = query_affine.shape[0]
    rows = sequences * block_len
    value_dim = value_weight.shape[1]
    shared_dim = own_shared * count

    affine_row = jnp.pad(query_affine.reshape(-1), (0, own - 3 * own_shared))
    packed = jnp.concatenate(
        [
            smooth_alpha.T,
            smooth_delta.T,
            smooth_beta.T,
            smooth_gamma.T,
            jnp.stack([first_gain, smooth_omega, second_gain, affine_row]),
        ],
        axis=0,
    )
    small = lax.all_gather(packed, "seq").transpose(1, 0, 2)
    value_full = gather_rows(value_weight)
    mix_full = gather_rows(mix_weight)
    merge_full = gather_rows(merge_weight)
    widen_full = gather_rows(widen_weight)
    narrow_full = gather_rows(narrow_weight)

    tiles = (width // lanes, lanes)
    alpha_rate = jax.nn.sigmoid(small[:states].reshape(states, *tiles))
    damp_rate = jax.nn.sigmoid(small[states : 2 * states].reshape(states, *tiles))
    beta = small[2 * states : 3 * states].reshape(states, *tiles)
    gamma = small[3 * states : 4 * states].reshape(states, *tiles)
    gain_one = small[4 * states].reshape(1, width)
    omega = small[4 * states + 1].reshape(1, width)
    gain_two = small[4 * states + 2].reshape(1, width)
    affine = small[4 * states + 3, :, : 3 * own_shared].reshape(shared_dim, 3)
    out_scale = states ** (-0.5)
    decay = 1.0 - alpha_rate * damp_rate
    block_decay = jnp.exp(block_len * jnp.log1p(-alpha_rate * damp_rate))
    weight = alpha_rate * beta * gamma * out_scale

    offsets = lax.axis_index("seq") * block_len + lax.iota(jnp.int32, block_len)
    valid = (offsets[None, :] < lengths[:, None]).astype(jnp.float32)
    row_valid = valid.reshape(rows, 1)
    key_valid = valid.reshape(sequences, 1, block_len) > 0.5

    masked_in = tokens.reshape(rows, width) * row_valid
    hat_one, scale_one = normalise(masked_in)
    normed = hat_one * gain_one
    tiled = (sequences, block_len) + tiles
    ending = (sequences, states) + tiles
    signal = normed.reshape(tiled)
    local, ends = call_kernel(
        functools.partial(filter_body, False), [tiled, ending], decay, weight, signal
    )
    enter = entering(ends, block_decay, False)
    (smoothed,) = call_kernel(
        functools.partial(carried_body, False), [tiled], decay, weight, enter, local
    )
    mix_pre = smoothed.reshape(rows, width) + omega * normed
    mixed = silu(mix_pre)
    value_pre = times(normed, value_full)
    values = silu(value_pre)
    projected = times(mixed, mix_full)
    second_cut = width + shared_dim
    third_cut = second_cut + value_dim
    update = jax.nn.sigmoid(projected[:, :width])
    shared_pre = projected[:, width:second_cut]
    reset_pre = projected[:, second_cut:third_cut]
    shared = silu(shared_pre)
    reset_gate = silu(reset_pre)
    queries = (shared * affine[:, 0] + affine[:, 2]).reshape(sequences, block_len, shared_dim)
    key_rows = (shared * affine[:, 1]).reshape(sequences, block_len, shared_dim)
    score_scale = shared_dim ** (-0.5)
    scores = jnp.einsum("cqz,ckz->cqk", queries, key_rows, precision=exact) * score_scale
    scores = jnp.where(key_valid, scores, masked_score)
    soft = jax.nn.softmax(scores, axis=-1)
    values_cut = values.reshape(sequences, block_len, value_dim)
    attended = jnp.einsum("cqk,ckv->cqv", soft, values_cut, precision=triple)
    attended = attended.reshape(rows, value_dim)
    gated = attended * reset_gate
    cand_pre = projected[:, third_cut:] + times(gated, merge_full)
    candidate = silu(cand_pre)
    middle = masked_in + update * (candidate - masked_in)
    hat_two, scale_two = normalise(middle)
    normed_two = hat_two * gain_two
    wide_pre = times(normed_two, widen_full)
    hidden = silu(wide_pre)

    g_out = out_grad.reshape(rows, width) * row_valid
    g_wide = times_back(g_out, narrow_full) * silu_slope(wide_pre)
    g_normed_two = times_back(g_wide, widen_full)
    second_gain_sum = jnp.sum(g_normed_two * hat_two, axis=0)
    g_middle = g_out + normalise_back(g_normed_two, gain_two, hat_two, scale_two)

    g_cand = g_middle * update * silu_slope(cand_pre)
    g_gated = times_back(g_cand, merge_full)
    g_attended = (g_gated * reset_gate).reshape(sequences, block_len, value_dim)
    g_reset = g_gated * attended
    g_soft = jnp.einsum("cqv,ckv->cqk", g_attended, values_cut, precision=triple)
    g_values = jnp.einsum("cqk,cqv->ckv", soft, g_attended, precision=triple)
    g_scores = soft * (g_soft - jnp.sum(g_soft * soft, axis=-1, keepdims=True))
    g_scores = jnp.where(key_valid, g_scores, 0.0) * score_scale
    g_queries = jnp.einsum("cqk,ckz->cqz", g_scores, key_rows, precision=exact)
    g_keys = jnp.einsum("cqk,cqz->ckz", g_scores, queries, precision=exact)
    g_queries = g_queries.reshape(rows, shared_dim)
    g_keys = g_keys.reshape(rows, shared_dim)
    affine_sum = jnp.stack(
        [
            jnp.sum(g_queries * shared, axis=0),
            jnp.sum(g_keys * shared, axis=0),
            jnp.sum(g_queries, axis=0),
        ],
        axis=1,
    )
    g_shared = (g_queries * affine[:, 0] + g_keys * affine[:, 1]) * silu_slope(shared_pre)
    g_update = g_middle * (candidate - masked_in) * update * (1.0 - update)
    g_reset_pre = g_reset * silu_slope(reset_pre)
    g_projected = jnp.concatenate([g_update, g_shared, g_reset_pre, g_cand], axis=1)
    g_smooth = times_back(g_projected, mix_full) * silu_slope(mix_pre)
    g_val = g_values.reshape(rows, value_dim) * silu_slope(value_pre)
    g_from_values = times_back(g_val, value_full)

    smooth_tiled = g_smooth.reshape(tiled)
    back_local, back_ends = call_kernel(
        functools.partial(filter_body, True), [tiled, ending], decay, weight, smooth_tiled
    )
    back_enter = entering(back_ends, block_decay, True)
    direct, slope, last = call_kernel(
        moments_body,
        [(states,) + tiles, (states,) + tiles, ending],
        decay,
        enter,
        signal,
        smooth_tiled,
    )
    (back_full,) = call_kernel(
        functools.partial(carried_body, True), [tiled], decay, weight, back_enter, back_local
    )
    slope = slope + decay * jnp.sum(back_enter * last, axis=0)
    decay_grad = weight * slope
    alpha_grad = (beta * gamma * out_scale * direct - damp_rate * decay_grad) * (
        alpha_rate * (1.0 - alpha_rate)
    )
    delta_grad = -alpha_rate * decay_grad * damp_rate * (1.0 - damp_rate)
    beta_grad = alpha_rate * gamma * out_scale * direct
    gamma_grad = alpha_rate * beta * out_scale * direct

    g_normed = g_from_values + g_smooth * omega + back_full.reshape(rows, width)
    tokens_grad = (
        g_middle * (1.0 - update) + normalise_back(g_normed, gain_one, hat_one, scale_one)
    ) * row_valid
    first_gain_sum = jnp.sum(g_normed * hat_one, axis=0)
    omega_sum = jnp.sum(g_smooth * normed, axis=0)
    affine_rows = jnp.pad(
        affine_sum.reshape(count, 3 * own_shared), ((0, 0), (0, own - 3 * own_shared))
    )
    small_rows = [
        alpha_grad.reshape(states, width),
        delta_grad.reshape(states, width),
        beta_grad.reshape(states, width),
        gamma_grad.reshape(states, width),
        jnp.stack([first_gain_sum, omega_sum, second_gain_sum, affine_rows.reshape(width)]),
    ]
    wholes, small_grad, shared_grad = all_grads(
        (
            (hidden, g_out),
            (normed_two, g_wide),
            (gated, g_cand),
            (mixed, jnp.concatenate([g_update, g_reset_pre, g_cand], axis=1)),
            (normed, g_val),
        ),
        jnp.concatenate(small_rows, axis=0),
        (mixed, g_shared),
    )
    narrow_grad, widen_grad, merge_grad, mix_rest, value_grad = wholes
    mix_grad = jnp.concatenate([mix_rest[:, :width], shared_grad, mix_rest[:, width:]], axis=1)

    block_out = (middle + times(hidden, narrow_full)) * row_valid

    return (
        block_out.reshape(tokens.shape),
        tokens_grad.reshape(tokens.shape),
        small_grad[4 * states],
        small_grad[:states].T,
        small_grad[states : 2 * states].T,
        small_grad[2 * states : 3 * states].T,
        small_grad[3 * states : 4 * states].T,
        small_grad[4 * states + 1],
        value_grad,
        mix_grad,
        small_grad[4 * states + 3, : 3 * own_shared].reshape(own_shared, 3),
        merge_grad,
        small_grad[4 * states + 2],
        widen_grad,
        narrow_grad,
    )


def solution(mesh):
    rows = P("batch", "seq", None)
    split = P("seq", None)
    in_specs = (
        (rows, P("batch"), rows, P("seq"))
        + (split,) * 4
        + (P("seq"),)
        + (split,) * 4
        + (P("seq"),)
        + (split,) * 2
    )
    out_specs = (
        (rows, rows, P("seq"))
        + (split,) * 4
        + (P("seq"),)
        + (split,) * 4
        + (P("seq"),)
        + (split,) * 2
    )
    return jax.shard_map(
        per_device, mesh=mesh, in_specs=in_specs, out_specs=out_specs, check_vma=False
    )
```

time: 1660 us -> 1050 us (0.63)
  matrix products: 951 us -> 132 us
  Pallas kernels: 0 us -> 323 us
  waiting for transfers between devices: 354 us -> 202 us
  local copies, waits for them, and re-layouts: 113 us -> 236 us
  blocking collectives: 126 us -> 45.6 us
  starting transfers between devices: 0.72 us -> 24.5 us
  other arithmetic: 86.8 us -> 65.4 us
    dot_general x33 -> x17, matrix products: 951 us -> 132 us  [the longest x5 64.2 us: times_back(): lax.dot_general(left, right, (((1,), (1,)), ((), ())), precision=triple)]
    pallas_call x0 -> x6, Pallas kernels: none -> 323 us  [the longest x1 308 us: reduce_grads(): pl.pallas_call(functools.partial(reduce_body, tuple(count)), out_shape=ja...]
    psum x1 -> x0, waiting for transfers between devices: 277 us -> none  [per_device(): lax.psum((shards[0], shards[1], shards[2], shards[3], shards[4], shards[5...]
    ppermute x0 -> x45, waiting for transfers between devices: none -> 202 us  [swap(): return lax.ppermute(value, 'seq', [(i, i ^ bit) for i in range(count)])]
    dynamic_update_slice x0 -> x50, local copies, waits for them, and re-layouts: none -> 68.9 us  [the longest x25 34.9 us: gather_rows(): full = lax.dynamic_update_slice(full, piece[None], (me ^ bit, part, 0, 0))]
    reshape x0 -> x18, local copies, waits for them, and re-layouts: none -> 52.3 us  [the longest x6 24 us: reduce_grads(): cut = left.reshape(rows, 4, 2, blocks, lanes).transpose(3, 2, 1, 4, 0)]
    reduce_scatter x9 -> x0, waiting for transfers between devices: 51.8 us -> none  [the longest x1 34.6 us: per_device(): lax.psum_scatter(grad_gamma, 'seq', scatter_dimension=0, tiled=True)]
    reduce_sum x9 -> x5, other arithmetic: 40.3 us -> 3.7 us  [the longest x1 1.43 us: normalise(): centre = jnp.mean(signal, axis=-1, keepdims=True)]
  transfers between devices with their start and end apart: 18 -> 47, of which waited for: 5 -> 12; matrix products, arithmetic and copies ran while one was open for 59% -> 24% of each run, Pallas kernels for 0% -> 0%
where the time goes in v1:
time: 1050 us; the launch traced here: 1040 us
  Pallas kernels  323 us (31%)
  local copies, waits for them, and re-layouts  236 us (22%)
  waiting for transfers between devices  202 us (19%)
  matrix products  132 us (13%)
  other arithmetic  65.4 us (6%)
  blocking collectives  45.6 us (4%)
  starting transfers between devices  24.5 us (2%)
  between operations  15.3 us (1%)
    pallas_call x1, Pallas kernels, reduce_grads(): pl.pallas_call(functools.partial(reduce_body, tuple(count)), out_shape=ja...  308 us
    ppermute x45, waiting for transfers between devices, swap(): return lax.ppermute(value, 'seq', [(i, i ^ bit) for i in range(count)])  202 us
    dot_general x5, matrix products, times_back(): lax.dot_general(left, right, (((1,), (1,)), ((), ())), precision=triple)  64.2 us
    dot_general x5, matrix products, times(): return jnp.dot(left, right, precision=triple)  59.2 us
    all_gather x1, blocking collectives, per_device(): small = lax.all_gather(packed, 'seq').transpose(1, 0, 2)  45.6 us
    unnamed x157, local copies, waits for them, and re-layouts  35.3 us
    dynamic_update_slice x25, local copies, waits for them, and re-layouts, gather_rows(): full = lax.dynamic_update_slice(full, piece[None], (me ^ bit, part, 0, 0))  34.9 us
    dynamic_update_slice x25, local copies, waits for them, and re-layouts, gather_rows(): lax.dynamic_update_slice(full, swap(piece, 1)[None], (me ^ bit ^ 1, part,...  34 us
  transfers between devices with their start and end apart: 47, of which 12 were waited for; matrix products, arithmetic and copies ran while one was open for 24% of the time, Pallas kernels for 0%

profile of v1, /device:TPU:0, one launch (start us, length us, event | category | flops | bytes accessed | tf_op | source)
XLA Modules:
  0.0 1043.7 jit_solution(12014091516841623197)
XLA Ops:
  7.2 3.0 collective-permute-start.9
  13.2 3.5 concatenate.33
  16.7 45.6 %all-gather.3 = f32[8,68,128]{2,1,0:T(8,128)S(1)} all-gather(f32[1,68,128]{2,1,0:T(8,128)S(1)} %bitcast.452), channel_id=2, replica_groups=mesh['seq'=8,'batch'=4] {'seq'}, dimensions={0}, use_global_device_ids=true | all-gather | bytes 313344 | tf_op jit(solution)/shard_map/all_gather | solution.py:444
  66.4 2.7 broadcast_multiply_fusion
  72.2 3.3 shard_map.271
  79.2 2.7 reshape.619
  89.4 4.4 broadcast_in_dim.175
  94.8 4.3 broadcast_in_dim.183
  105.6 8.3 broadcast_in_dim.165
  115.4 3.1 constant_dynamic-update-slice_fusion.23
  141.0 7.4 collective-permute-done.20
  163.8 3.1 divide_multiply_fusion
  170.0 2.7 bitcast_dynamic-update-slice_fusion.26
  180.2 3.3 constant_dynamic-update-slice_fusion.10
  187.6 30.4 %collective-permute-done.37 = f32[512,1024]{1,0:T(8,128)S(1)} collective-permute-done((f32[512,1024]{1,0:T(8,128)}, f32[512,1024]{1,0:T(8,128)S(1)}, u32[]{:S(2)}, u32[]{:S(2)}) %collective-permute-start.37) | collective-permute-done | bytes 2097184 | tf_op jit(solution)/shard_map/ppermute | solution.py:19
  224.6 38.3 %collective-permute-done.28 = f32[128,4096]{1,0:T(8,128)S(1)} collective-permute-done((f32[128,4096]{1,0:T(8,128)S(1)}, f32[128,4096]{1,0:T(8,128)S(1)}, u32[]{:S(2)}, u32[]{:S(2)}) %collective-permute-start.28) | collective-permute-done | bytes 2097184 | tf_op jit(solution)/shard_map/ppermute | solution.py:19
  266.2 8.6 fusion.14
  277.9 31.4 %collective-permute-done.1 = f32[128,4224]{1,0:T(8,128)S(1)} collective-permute-done((f32[128,4224]{1,0:T(8,128)}, f32[128,4224]{1,0:T(8,128)S(1)}, u32[]{:S(2)}, u32[]{:S(2)}) %collective-permute-start.1) | collective-permute-done | bytes 2162720 | tf_op jit(solution)/shard_map/ppermute | solution.py:19
  311.6 20.3 %collective-permute-done.38 = f32[256,1024]{1,0:T(8,128)} collective-permute-done((f32[256,1024]{1,0:T(8,128)}, f32[256,1024]{1,0:T(8,128)}, u32[]{:S(2)}, u32[]{:S(2)}) %collective-permute-start.38) | collective-permute-done | bytes 1048608 | tf_op jit(solution)/shard_map/ppermute | solution.py:19
  335.9 17.8 %collective-permute-done.29 = f32[64,4096]{1,0:T(8,128)S(1)} collective-permute-done((f32[64,4096]{1,0:T(8,128)}, f32[64,4096]{1,0:T(8,128)S(1)}, u32[]{:S(2)}, u32[]{:S(2)}) %collective-permute-start.29) | collective-permute-done | bytes 1048608 | tf_op jit(solution)/shard_map/ppermute | solution.py:19
  353.8 6.1 collective-permute-done.30
  361.5 3.2 bitcast_dynamic-update-slice_fusion.8
  365.0 21.4 %collective-permute-done.2 = f32[64,4224]{1,0:T(8,128)S(1)} collective-permute-done((f32[64,4224]{1,0:T(8,128)S(1)}, f32[64,4224]{1,0:T(8,128)S(1)}, u32[]{:S(2)}, u32[]{:S(2)}) %collective-permute-start.2) | collective-permute-done | bytes 1081376 | tf_op jit(solution)/shard_map/ppermute | solution.py:19
  388.0 23.1 %collective-permute-done.3 = f32[64,4224]{1,0:T(8,128)S(1)} collective-permute-done((f32[64,4224]{1,0:T(8,128)S(1)}, f32[64,4224]{1,0:T(8,128)S(1)}, u32[]{:S(2)}, u32[]{:S(2)}) %collective-permute-start.3) | collective-permute-done | bytes 1081376 | tf_op jit(solution)/shard_map/ppermute | solution.py:19
  412.7 3.1 bitcast_dynamic-update-slice_fusion.4
  432.8 14.2 %fusion.25 = f32[256,4224]{1,0:T(8,128)} fusion(f32[1024,4224]{1,0:T(8,128)} %bitcast.29, f32[32,8,8,128]{3,2,1,0:T(8,128)S(1)} %bitcast.412), kind=kOutput, calls=%fused_computation.56 | convolution fusion | flops 6643777536 | bytes 22675456 | tf_op jit(solution)/shard_map/dot_general | solution.py:399
  449.7 3.0 bitcast_multiply_fusion.2
  452.7 9.9 fusion.83
  464.7 14.7 %fusion.11 = (f32[256,4096]{1,0:T(8,128)}, f32[256,4096]{1,0:T(8,128)}) fusion(f32[256,1024]{1,0:T(8,128)} %fusion.37, f32[1024,4096]{1,0:T(8,128)S(1)} %bitcast.370), kind=kOutput, calls=%fused_computation.20 | convolution fusion | flops 6446645248 | bytes 26214400 | tf_op jit(solution)/shard_map/dot_general | solution.py:399
  479.4 13.0 %convolution_multiply_fusion = f32[256,4096]{1,0:T(8,128)} fusion(f32[256,1024]{1,0:T(8,128)} %bitcast.433, f32[4096,1024]{1,0:T(8,128)} %bitcast.379, f32[256,4096]{1,0:T(8,128)} %get-tuple-element.162), kind=kOutput, calls=%fused_computation.7 | convolution fusion | flops 6450839552 | bytes 26214400 | tf_op jit(solution)/shard_map/dot_general | solution.py:403
  492.5 20.9 %multiply_reduce_fusion = (f32[1024]{0:T(1024)}, f32[256]{0:T(256)S(1)}, f32[256]{0:T(256)S(1)}, f32[256,1024]{1,0:T(8,128)}) fusion(f32[256,1024]{1,0:T(8,128)} %copy-done.3, f32[256]{0:T(256)S(1)} %add_rsqrt_fusion, f32[256]{0:T(256)S(1)} %broadcast_multiply_fusion.7, f32[1024]{0:T(1024)S(1)} %get-tuple-element.136, ...), kind=kOutput, calls=%fused_computation.92 | convolution fusion | flops 6444546560 | bytes 23080960 | tf_op jit(solution)/shard_map/dot_general | solution.py:403
  513.4 4.9 multiply_multiply_fusion.1
  520.0 8.7 fusion.12
  531.9 12.4 %fusion.15 = f32[256,1024]{1,0:T(8,128)S(1)} fusion(f32[1024,4224]{1,0:T(8,128)} %bitcast.29, f32[256,1024]{1,0:T(8,128)S(1)} %multiply_multiply_fusion.2, f32[256,2048]{1,0:T(8,128)} %get-tuple-element.124, f32[256,128]{1,0:T(8,128)S(1)} %get-tuple-element.126, f32[256,1024]{1,0:T(8,128)} %get-tuple-element.109, f32[256,1024]{1,0:T(8,128)} %get-tuple-element.130, ...), kind=kOutput, calls=%fused_computation.40 | convolution fusion | flops 6649905152 | bytes 24780800 | tf_op jit(solution)/shard_map/dot_general | solution.py:403
  544.5 5.9 shard_map.275
  550.4 3.3 shard_map.273
  556.1 3.1 reshape.611
  559.2 4.0 reshape.613
  563.2 5.6 copy.127
  570.1 4.3 pad_maximum_fusion
  574.4 6.0 reshape.609
  580.4 5.4 copy.119
  585.7 4.5 constant_dynamic-update-slice_fusion.4
  591.7 4.1 copy.121
  595.9 5.4 copy.128
  603.8 5.6 copy.131
  609.4 5.3 copy.132
  614.7 4.3 bitcast_multiply_fusion
  619.0 2.9 copy.133
  621.9 3.3 copy.134
  625.3 4.8 bitcast_dynamic-update-slice_fusion.1
  636.3 11.9 %fusion.1 = (bf16[48,256,256]{2,1,0:T(8,128)(2,1)}, bf16[48,256,256]{2,1,0:T(8,128)(2,1)}) fusion(f32[48,256,256]{2,1,0:T(8,128)} %bitcast_dynamic-update-slice_fusion.5), kind=kLoop, calls=%fused_computation.5 | loop fusion | flops 12582912 | bytes 25165824 | tf_op jit(solution)/shard_map/convert_element_type | solution.py:54
  648.5 2.5 copy.151
  654.4 3.0 constant_dynamic-update-slice_fusion.2
  662.0 9.4 fusion.2
  671.4 11.8 %fusion.18 = f32[256,1024]{1,0:T(8,128)} fusion(f32[256,1024]{1,0:T(8,128)S(1)} %copy-done.4, f32[4096,1024]{1,0:T(8,128)} %bitcast.380, f32[256]{0:T(256)S(1)} %copy-done.48, f32[256,4096]{1,0:T(8,128)S(1)} %copy-done.24), kind=kOutput, calls=%fused_computation.42 | convolution fusion | flops 6447169536 | bytes 23069696 | tf_op jit(solution)/shard_map/dot_general | solution.py:399
  686.2 9.3 multiply_reduce_fusion.2
  697.4 2.5 copy.139
  700.0 307.5 %shard_map.276 = f32[65,2,64,256]{3,2,1,0:T(8,128)} custom-call(bf16[9,2,512,256]{3,2,1,0:T(8,128)(2,1)} %get-tuple-element.118.left_high, bf16[9,2,512,256]{3,2,1,0:T(8,128)(2,1)} %get-tuple-element.117.left_low, bf16[48,256,256]{2,1,0:T(8,128)(2,1)} %get-tuple-element.116.right_high, bf16[48,256,256]{2,1,0:T(8,128)(2,1)} %get-tuple-element.115.right_low, ...), custom_call_target="tpu_custom_call" | custom-call | tf_op jit(solution)/shard_map/pallas_call | solution.py:239
  1009.5 2.7 fusion.85
  1012.3 5.6 fusion.84
  1024.5 3.3 copy.161
  1027.8 2.9 copy.144
  1032.5 2.7 add_multiply_fusion
  (368 shorter events, 172.7 us)
Async XLA Ops:
  7.2 70.2 %copy-start.1 = (f32[2,128,1024]{2,1,0:T(8,128)S(1)}, f32[2,128,1024]{2,1,0:T(8,128)}, u32[]{:S(2)}) copy-start(f32[2,128,1024]{2,1,0:T(8,128)} %param.16) | copy-start | bytes 3145732
  7.2 150.7 %all-gather.7.cloned.1.call-start = ((), (), s32[]{:S(2)}) async-start(), calls=%async_computation | async-start | bytes 1179648 | tf_op jit(solution)/shard_map/all_gather | solution.py:362
  7.2 113.6 %collective-permute-start.9 = (f32[128,2048]{1,0:T(8,128)}, f32[128,2048]{1,0:T(8,128)}, u32[]{:S(2)}, u32[]{:S(2)}) collective-permute-start(f32[128,2048]{1,0:T(8,128)} %param.25), channel_id=1, source_target_pairs={{0,8},{4,12},{8,0},{12,4},{16,24},{20,28},{24,16},{28,20},{1,9},{5... | collective-permute-start | bytes 3145736 | tf_op jit(solution)/shard_map/ppermute | solution.py:19
  10.2 112.3 %collective-permute-start.10 = (f32[128,2048]{1,0:T(8,128)}, f32[128,2048]{1,0:T(8,128)}, u32[]{:S(2)}, u32[]{:S(2)}) collective-permute-start(f32[128,2048]{1,0:T(8,128)} %param.25), channel_id=1, source_target_pairs={{0,16},{4,20},{8,24},{12,28},{16,0},{20,4},{24,8},{28,12},{1,17},{... | collective-permute-start | bytes 3145736 | tf_op jit(solution)/shard_map/ppermute | solution.py:19
  11.8 113.9 %collective-permute-start.18 = (f32[256,1024]{1,0:T(8,128)}, f32[256,1024]{1,0:T(8,128)}, u32[]{:S(2)}, u32[]{:S(2)}) collective-permute-start(f32[256,1024]{1,0:T(8,128)} %param.28), channel_id=1, source_target_pairs={{0,8},{4,12},{8,0},{12,4},{16,24},{20,28},{24,16},{28,20},{1,9},{5... | collective-permute-start | bytes 3145736 | tf_op jit(solution)/shard_map/ppermute | solution.py:19
  12.3 122.3 %collective-permute-start.19 = (f32[256,1024]{1,0:T(8,128)}, f32[256,1024]{1,0:T(8,128)}, u32[]{:S(2)}, u32[]{:S(2)}) collective-permute-start(f32[256,1024]{1,0:T(8,128)} %param.28), channel_id=1, source_target_pairs={{0,16},{4,20},{8,24},{12,28},{16,0},{20,4},{24,8},{28,12},{1,17},{... | collective-permute-start | bytes 3145736 | tf_op jit(solution)/shard_map/ppermute | solution.py:19
  62.4 95.5 %copy-start.38 = (f32[16,8,128]{2,1,0:T(8,128)}, f32[16,8,128]{2,1,0:T(8,128)S(1)}, u32[]{:S(2)}) copy-start(f32[16,8,128]{2,1,0:T(8,128)S(1)} %get-tuple-element.113) | copy-start | bytes 196612
  62.4 95.4 %copy-start.40 = (f32[16,8,128]{2,1,0:T(8,128)}, f32[16,8,128]{2,1,0:T(8,128)S(1)}, u32[]{:S(2)}) copy-start(f32[16,8,128]{2,1,0:T(8,128)S(1)} %get-tuple-element.114) | copy-start | bytes 196612
  75.5 607.7 %all-gather.9.cloned.1.call-start = ((), (), s32[]{:S(2)}) async-start(), calls=%async_computation.1 | async-start | bytes 1179648 | tf_op jit(solution)/shard_map/all_gather | solution.py:362
  76.0 103.7 %collective-permute-start.36 = (f32[512,1024]{1,0:T(8,128)}, f32[512,1024]{1,0:T(8,128)}, u32[]{:S(2)}, u32[]{:S(2)}) collective-permute-start(f32[512,1024]{1,0:T(8,128)} %param.31), channel_id=1, source_target_pairs={{0,8},{4,12},{8,0},{12,4},{16,24},{20,28},{24,16},{28,20},{1,9},{5... | collective-permute-start | bytes 6291464 | tf_op jit(solution)/shard_map/ppermute | solution.py:19
  120.5 27.8 %copy-start.33 = (f32[256,1024]{1,0:T(8,128)S(1)}, f32[256,1024]{1,0:T(8,128)}, u32[]{:S(2)}) copy-start(f32[256,1024]{1,0:T(8,128)} %param.28) | copy-start | bytes 3145732
  120.8 34.3 %copy-start = (f32[8,2,64,4096]{3,2,1,0:T(8,128)}, f32[8,2,64,4096]{3,2,1,0:T(8,128)S(1)}, u32[]{:S(2)}) copy-start(f32[8,2,64,4096]{3,2,1,0:T(8,128)S(1)} %constant_dynamic-update-slice_fusion.14) | copy-start | bytes 50331652
  120.8 34.3 %collective-permute-start.13 = (f32[2,64,2048]{2,1,0:T(8,128)S(1)}, f32[2,64,2048]{2,1,0:T(8,128)S(1)}, u32[]{:S(2)}, u32[]{:S(2)}) collective-permute-start(f32[2,64,2048]{2,1,0:T(8,128)S(1)} %bitcast.436), channel_id=1, source_target_pairs={{0,4},{4,0},{8,12},{12,8},{16,20},{20,16},{24,28},{28,24},{1,5},{5... | collective-permute-start | bytes 3145736 | tf_op jit(solution)/shard_map/ppermute | solution.py:19
  122.5 16.9 %collective-permute-start.11 = (f32[64,2048]{1,0:T(8,128)S(1)}, f32[64,2048]{1,0:T(8,128)S(1)}, u32[]{:S(2)}, u32[]{:S(2)}) collective-permute-start(f32[64,2048]{1,0:T(8,128)S(1)} %slice.277), channel_id=1, source_target_pairs={{0,16},{4,20},{8,24},{12,28},{16,0},{20,4},{24,8},{28,12},{1,17},{... | collective-permute-start | bytes 1572872 | tf_op jit(solution)/shard_map/ppermute | solution.py:19
  125.6 28.1 %collective-permute-start.12 = (f32[64,2048]{1,0:T(8,128)S(1)}, f32[64,2048]{1,0:T(8,128)S(1)}, u32[]{:S(2)}, u32[]{:S(2)}) collective-permute-start(f32[64,2048]{1,0:T(8,128)S(1)} %slice.278), channel_id=1, source_target_pairs={{0,8},{4,12},{8,0},{12,4},{16,24},{20,28},{24,16},{28,20},{1,9},{5... | collective-permute-start | bytes 1572872 | tf_op jit(solution)/shard_map/ppermute | solution.py:19
  134.6 13.7 %collective-permute-start.20 = (f32[128,1024]{1,0:T(8,128)S(1)}, f32[128,1024]{1,0:T(8,128)}, u32[]{:S(2)}, u32[]{:S(2)}) collective-permute-start(f32[128,1024]{1,0:T(8,128)S(1)} %slice.280), channel_id=1, source_target_pairs={{0,16},{4,20},{8,24},{12,28},{16,0},{20,4},{24,8},{28,12},{1,17},{... | collective-permute-start | bytes 1572872 | tf_op jit(solution)/shard_map/ppermute | solution.py:19
  139.4 13.4 %collective-permute-start.21 = (f32[128,1024]{1,0:T(8,128)S(1)}, f32[128,1024]{1,0:T(8,128)S(1)}, u32[]{:S(2)}, u32[]{:S(2)}) collective-permute-start(f32[128,1024]{1,0:T(8,128)S(1)} %slice.281), channel_id=1, source_target_pairs={{0,8},{4,12},{8,0},{12,4},{16,24},{20,28},{24,16},{28,20},{1,9},{5... | collective-permute-start | bytes 1572872 | tf_op jit(solution)/shard_map/ppermute | solution.py:19
  148.4 7.9 collective-permute-start.22
  152.8 19.9 %collective-permute-start.14 = (f32[2,64,2048]{2,1,0:T(8,128)}, f32[2,64,2048]{2,1,0:T(8,128)}, u32[]{:S(2)}, u32[]{:S(2)}) collective-permute-start(f32[2,64,2048]{2,1,0:T(8,128)} %bitcast.41), channel_id=1, source_target_pairs={{0,4},{4,0},{8,12},{12,8},{16,20},{20,16},{24,28},{28,24},{1,5},{5... | collective-permute-start | bytes 3145736 | tf_op jit(solution)/shard_map/ppermute | solution.py:19
  153.7 13.1 %collective-permute-start.23 = (f32[2,128,1024]{2,1,0:T(8,128)}, f32[2,128,1024]{2,1,0:T(8,128)}, u32[]{:S(2)}, u32[]{:S(2)}) collective-permute-start(f32[2,128,1024]{2,1,0:T(8,128)} %bitcast.59), channel_id=1, source_target_pairs={{0,4},{4,0},{8,12},{12,8},{16,20},{20,16},{24,28},{28,24},{1,5},{5... | collective-permute-start | bytes 3145736 | tf_op jit(solution)/shard_map/ppermute | solution.py:19
  155.1 14.3 %collective-permute-start.24 = (f32[2,128,1024]{2,1,0:T(8,128)}, f32[2,128,1024]{2,1,0:T(8,128)}, u32[]{:S(2)}, u32[]{:S(2)}) collective-permute-start(f32[2,128,1024]{2,1,0:T(8,128)} %bitcast.61), channel_id=1, source_target_pairs={{0,4},{4,0},{8,12},{12,8},{16,20},{20,16},{24,28},{28,24},{1,5},{5... | collective-permute-start | bytes 3145736 | tf_op jit(solution)/shard_map/ppermute | solution.py:19
  156.3 17.6 %collective-permute-start.25 = (f32[1,128,1024]{2,1,0:T(8,128)}, f32[1,128,1024]{2,1,0:T(8,128)}, u32[]{:S(2)}, u32[]{:S(2)}) collective-permute-start(f32[1,128,1024]{2,1,0:T(8,128)} %bitcast.63), channel_id=1, source_target_pairs={{0,4},{4,0},{8,12},{12,8},{16,20},{20,16},{24,28},{28,24},{1,5},{5... | collective-permute-start | bytes 1572872 | tf_op jit(solution)/shard_map/ppermute | solution.py:19
  163.7 100.3 %slice-start = ((s8[16777216]{0:T(1024)(128)(4,1)}), s8[4194304]{0:T(1024)(128)(4,1)S(1)}, s32[]{:S(2)}) async-start(s8[16777216]{0:T(1024)(128)(4,1)} %bitcast.368), calls=%async_computation.2 | async-start | bytes 8388608
  166.8 51.2 %copy-start.43 = (f32[64,2048]{1,0:T(8,128)S(1)}, f32[64,2048]{1,0:T(8,128)}, u32[]{:S(2)}) copy-start(f32[64,2048]{1,0:T(8,128)} %copy-done.42) | copy-start | bytes 1572868
  166.9 7.8 collective-permute-start.26
  169.3 94.7 %slice-start.1 = ((s8[16777216]{0:T(1024)(128)(4,1)}), s8[4194304]{0:T(1024)(128)(4,1)S(1)}, s32[]{:S(2)}) async-start(s8[16777216]{0:T(1024)(128)(4,1)} %bitcast.368), calls=%async_computation.3 | async-start | bytes 8388608
  169.4 48.7 %collective-permute-start.37 = (f32[512,1024]{1,0:T(8,128)}, f32[512,1024]{1,0:T(8,128)S(1)}, u32[]{:S(2)}, u32[]{:S(2)}) collective-permute-start(f32[512,1024]{1,0:T(8,128)} %param.31), channel_id=1, source_target_pairs={{0,16},{4,20},{8,24},{12,28},{16,0},{20,4},{24,8},{28,12},{1,17},{... | collective-permute-start | bytes 6291464 | tf_op jit(solution)/shard_map/ppermute | solution.py:19
  172.7 50.2 %collective-permute-start.27 = (f32[128,4096]{1,0:T(8,128)S(1)}, f32[128,4096]{1,0:T(8,128)S(1)}, u32[]{:S(2)}, u32[]{:S(2)}) collective-permute-start(f32[128,4096]{1,0:T(8,128)S(1)} %copy-done.29), channel_id=1, source_target_pairs={{0,8},{4,12},{8,0},{12,4},{16,24},{20,28},{24,16},{28,20},{1,9},{5... | collective-permute-start | bytes 6291464 | tf_op jit(solution)/shard_map/ppermute | solution.py:19
  173.8 89.1 %collective-permute-start.28 = (f32[128,4096]{1,0:T(8,128)S(1)}, f32[128,4096]{1,0:T(8,128)S(1)}, u32[]{:S(2)}, u32[]{:S(2)}) collective-permute-start(f32[128,4096]{1,0:T(8,128)S(1)} %copy-done.29), channel_id=1, source_target_pairs={{0,16},{4,20},{8,24},{12,28},{16,0},{20,4},{24,8},{28,12},{1,17},{... | collective-permute-start | bytes 6291464 | tf_op jit(solution)/shard_map/ppermute | solution.py:19
  174.6 8.8 collective-permute-start.15
  179.7 5.9 collective-permute-start.16
  180.2 83.9 %slice-start.2 = ((s8[16777216]{0:T(1024)(128)(4,1)}), s8[4194304]{0:T(1024)(128)(4,1)S(1)}, s32[]{:S(2)}) async-start(s8[16777216]{0:T(1024)(128)(4,1)} %bitcast.368), calls=%async_computation.4 | async-start | bytes 8388608
  183.5 91.4 %collective-permute-start = (f32[128,4224]{1,0:T(8,128)}, f32[128,4224]{1,0:T(8,128)S(1)}, u32[]{:S(2)}, u32[]{:S(2)}) collective-permute-start(f32[128,4224]{1,0:T(8,128)} %param.26), channel_id=1, source_target_pairs={{0,8},{4,12},{8,0},{12,4},{16,24},{20,28},{24,16},{28,20},{1,9},{5... | collective-permute-start | bytes 6488072 | tf_op jit(solution)/shard_map/ppermute | solution.py:19
  185.7 123.7 %collective-permute-start.1 = (f32[128,4224]{1,0:T(8,128)}, f32[128,4224]{1,0:T(8,128)S(1)}, u32[]{:S(2)}, u32[]{:S(2)}) collective-permute-start(f32[128,4224]{1,0:T(8,128)} %param.26), channel_id=1, source_target_pairs={{0,16},{4,20},{8,24},{12,28},{16,0},{20,4},{24,8},{28,12},{1,17},{... | collective-permute-start | bytes 6488072 | tf_op jit(solution)/shard_map/ppermute | solution.py:19
  218.0 46.3 %collective-permute-start.17 = (f32[1,64,2048]{2,1,0:T(8,128)S(1)}, f32[1,64,2048]{2,1,0:T(8,128)S(1)}, u32[]{:S(2)}, u32[]{:S(2)}) collective-permute-start(f32[1,64,2048]{2,1,0:T(8,128)S(1)} %bitcast.444), channel_id=1, source_target_pairs={{0,4},{4,0},{8,12},{12,8},{16,20},{20,16},{24,28},{28,24},{1,5},{5... | collective-permute-start | bytes 1572872 | tf_op jit(solution)/shard_map/ppermute | solution.py:19
  219.5 44.6 %slice-start.3 = ((s8[16777216]{0:T(1024)(128)(4,1)}), s8[4194304]{0:T(1024)(128)(4,1)S(1)}, s32[]{:S(2)}) async-start(s8[16777216]{0:T(1024)(128)(4,1)} %bitcast.368), calls=%async_computation.5 | async-start | bytes 8388608
  221.9 44.3 %copy-start.27 = (f32[2,128,1024]{2,1,0:T(8,128)S(1)}, f32[2,128,1024]{2,1,0:T(8,128)}, u32[]{:S(2)}) copy-start(f32[2,128,1024]{2,1,0:T(8,128)} %multiply_multiply_fusion.3) | copy-start | bytes 3145732
  223.0 43.2 %copy-start.22 = (f32[128,4096]{1,0:T(8,128)}, f32[128,4096]{1,0:T(8,128)S(1)}, u32[]{:S(2)}) copy-start(f32[128,4096]{1,0:T(8,128)S(1)} %collective-permute-done.27) | copy-start | bytes 6291460
  223.0 189.2 %collective-permute-start.4 = (f32[2,64,4224]{2,1,0:T(8,128)}, f32[2,64,4224]{2,1,0:T(8,128)}, u32[]{:S(2)}, u32[]{:S(2)}) collective-permute-start(f32[2,64,4224]{2,1,0:T(8,128)} %bitcast.19), channel_id=1, source_target_pairs={{0,4},{4,0},{8,12},{12,8},{16,20},{20,16},{24,28},{28,24},{1,5},{5... | collective-permute-start | bytes 6488072 | tf_op jit(solution)/shard_map/ppermute | solution.py:19
  263.0 97.1 %collective-permute-start.40 = (f32[2,256,1024]{2,1,0:T(8,128)}, f32[2,256,1024]{2,1,0:T(8,128)}, u32[]{:S(2)}, u32[]{:S(2)}) collective-permute-start(f32[2,256,1024]{2,1,0:T(8,128)} %bitcast.90), channel_id=1, source_target_pairs={{0,4},{4,0},{8,12},{12,8},{16,20},{20,16},{24,28},{28,24},{1,5},{5... | collective-permute-start | bytes 6291464 | tf_op jit(solution)/shard_map/ppermute | solution.py:19
  264.4 67.5 %collective-permute-start.38 = (f32[256,1024]{1,0:T(8,128)}, f32[256,1024]{1,0:T(8,128)}, u32[]{:S(2)}, u32[]{:S(2)}) collective-permute-start(f32[256,1024]{1,0:T(8,128)} %slice.285), channel_id=1, source_target_pairs={{0,16},{4,20},{8,24},{12,28},{16,0},{20,4},{24,8},{28,12},{1,17},{... | collective-permute-start | bytes 3145736 | tf_op jit(solution)/shard_map/ppermute | solution.py:19
  274.8 173.7 %copy-start.8 = (f32[256,2048]{1,0:T(8,128)}, f32[256,2048]{1,0:T(8,128)S(1)}, u32[]{:S(2)}) copy-start(f32[256,2048]{1,0:T(8,128)S(1)} %get-tuple-element.156) | copy-start | bytes 6291460
  274.8 57.1 %copy-start.30 = (f32[128,4096]{1,0:T(8,128)S(1)}, f32[128,4096]{1,0:T(8,128)}, u32[]{:S(2)}) copy-start(f32[128,4096]{1,0:T(8,128)} %param.30) | copy-start | bytes 6291460
  274.8 59.4 %copy-start.37 = (f32[64,4096]{1,0:T(8,128)S(1)}, f32[64,4096]{1,0:T(8,128)}, u32[]{:S(2)}) copy-start(f32[64,4096]{1,0:T(8,128)} %slice.284) | copy-start | bytes 3145732
  274.8 59.4 %collective-permute-start.39 = (f32[256,1024]{1,0:T(8,128)}, f32[256,1024]{1,0:T(8,128)S(1)}, u32[]{:S(2)}, u32[]{:S(2)}) collective-permute-start(f32[256,1024]{1,0:T(8,128)} %slice.286), channel_id=1, source_target_pairs={{0,8},{4,12},{8,0},{12,4},{16,24},{20,28},{24,16},{28,20},{1,9},{5... | collective-permute-start | bytes 3145736 | tf_op jit(solution)/shard_map/ppermute | solution.py:19
  309.3 44.4 %collective-permute-start.29 = (f32[64,4096]{1,0:T(8,128)}, f32[64,4096]{1,0:T(8,128)S(1)}, u32[]{:S(2)}, u32[]{:S(2)}) collective-permute-start(f32[64,4096]{1,0:T(8,128)} %slice.283), channel_id=1, source_target_pairs={{0,16},{4,20},{8,24},{12,28},{16,0},{20,4},{24,8},{28,12},{1,17},{... | collective-permute-start | bytes 3145736 | tf_op jit(solution)/shard_map/ppermute | solution.py:19
  310.1 54.7 %copy-start.23 = (f32[128,4096]{1,0:T(8,128)S(1)}, f32[128,4096]{1,0:T(8,128)}, u32[]{:S(2)}) copy-start(f32[128,4096]{1,0:T(8,128)} %copy-done.22) | copy-start | bytes 6291460
  331.9 32.8 %collective-permute-start.31 = (f32[2,64,4096]{2,1,0:T(8,128)S(1)}, f32[2,64,4096]{2,1,0:T(8,128)S(1)}, u32[]{:S(2)}, u32[]{:S(2)}) collective-permute-start(f32[2,64,4096]{2,1,0:T(8,128)S(1)} %bitcast.424), channel_id=1, source_target_pairs={{0,4},{4,0},{8,12},{12,8},{16,20},{20,16},{24,28},{28,24},{1,5},{5... | collective-permute-start | bytes 6291464 | tf_op jit(solution)/shard_map/ppermute | solution.py:19
  334.2 25.8 %copy-start.34 = (f32[256,1024]{1,0:T(8,128)}, f32[256,1024]{1,0:T(8,128)S(1)}, u32[]{:S(2)}) copy-start(f32[256,1024]{1,0:T(8,128)S(1)} %collective-permute-done.39) | copy-start | bytes 3145732
  334.2 25.7 %collective-permute-start.30 = (f32[64,4096]{1,0:T(8,128)S(1)}, f32[64,4096]{1,0:T(8,128)S(1)}, u32[]{:S(2)}, u32[]{:S(2)}) collective-permute-start(f32[64,4096]{1,0:T(8,128)S(1)} %copy-done.37), channel_id=1, source_target_pairs={{0,8},{4,12},{8,0},{12,4},{16,24},{20,28},{24,16},{28,20},{1,9},{5... | collective-permute-start | bytes 3145736 | tf_op jit(solution)/shard_map/ppermute | solution.py:19
  353.7 62.1 %collective-permute-start.41 = (f32[2,256,1024]{2,1,0:T(8,128)}, f32[2,256,1024]{2,1,0:T(8,128)S(1)}, u32[]{:S(2)}, u32[]{:S(2)}) collective-permute-start(f32[2,256,1024]{2,1,0:T(8,128)} %bitcast.92), channel_id=1, source_target_pairs={{0,4},{4,0},{8,12},{12,8},{16,20},{20,16},{24,28},{28,24},{1,5},{5... | collective-permute-start | bytes 6291464 | tf_op jit(solution)/shard_map/ppermute | solution.py:19
  359.9 57.4 %collective-permute-start.42 = (f32[2,256,1024]{2,1,0:T(8,128)S(1)}, f32[2,256,1024]{2,1,0:T(8,128)S(1)}, u32[]{:S(2)}, u32[]{:S(2)}) collective-permute-start(f32[2,256,1024]{2,1,0:T(8,128)S(1)} %bitcast.409), channel_id=1, source_target_pairs={{0,4},{4,0},{8,12},{12,8},{16,20},{20,16},{24,28},{28,24},{1,5},{5... | collective-permute-start | bytes 6291464 | tf_op jit(solution)/shard_map/ppermute | solution.py:19
  360.9 25.5 %collective-permute-start.2 = (f32[64,4224]{1,0:T(8,128)S(1)}, f32[64,4224]{1,0:T(8,128)S(1)}, u32[]{:S(2)}, u32[]{:S(2)}) collective-permute-start(f32[64,4224]{1,0:T(8,128)S(1)} %slice.268), channel_id=1, source_target_pairs={{0,16},{4,20},{8,24},{12,28},{16,0},{20,4},{24,8},{28,12},{1,17},{... | collective-permute-start | bytes 3244040 | tf_op jit(solution)/shard_map/ppermute | solution.py:19
  364.7 54.5 %collective-permute-start.32 = (f32[2,64,4096]{2,1,0:T(8,128)S(1)}, f32[2,64,4096]{2,1,0:T(8,128)}, u32[]{:S(2)}, u32[]{:S(2)}) collective-permute-start(f32[2,64,4096]{2,1,0:T(8,128)S(1)} %bitcast.411), channel_id=1, source_target_pairs={{0,4},{4,0},{8,12},{12,8},{16,20},{20,16},{24,28},{28,24},{1,5},{5... | collective-permute-start | bytes 6291464 | tf_op jit(solution)/shard_map/ppermute | solution.py:19
  386.4 24.7 %collective-permute-start.3 = (f32[64,4224]{1,0:T(8,128)S(1)}, f32[64,4224]{1,0:T(8,128)S(1)}, u32[]{:S(2)}, u32[]{:S(2)}) collective-permute-start(f32[64,4224]{1,0:T(8,128)S(1)} %slice.269), channel_id=1, source_target_pairs={{0,8},{4,12},{8,0},{12,4},{16,24},{20,28},{24,16},{28,20},{1,9},{5... | collective-permute-start | bytes 3244040 | tf_op jit(solution)/shard_map/ppermute | solution.py:19
  411.1 13.3 %collective-permute-start.33 = (f32[2,64,4096]{2,1,0:T(8,128)S(1)}, f32[2,64,4096]{2,1,0:T(8,128)S(1)}, u32[]{:S(2)}, u32[]{:S(2)}) collective-permute-start(f32[2,64,4096]{2,1,0:T(8,128)S(1)} %bitcast.407), channel_id=1, source_target_pairs={{0,4},{4,0},{8,12},{12,8},{16,20},{20,16},{24,28},{28,24},{1,5},{5... | collective-permute-start | bytes 6291464 | tf_op jit(solution)/shard_map/ppermute | solution.py:19
  412.2 15.5 %collective-permute-start.5 = (f32[2,64,4224]{2,1,0:T(8,128)S(1)}, f32[2,64,4224]{2,1,0:T(8,128)S(1)}, u32[]{:S(2)}, u32[]{:S(2)}) collective-permute-start(f32[2,64,4224]{2,1,0:T(8,128)S(1)} %bitcast.403), channel_id=1, source_target_pairs={{0,4},{4,0},{8,12},{12,8},{16,20},{20,16},{24,28},{28,24},{1,5},{5... | collective-permute-start | bytes 6488072 | tf_op jit(solution)/shard_map/ppermute | solution.py:19
  415.8 13.4 %collective-permute-start.6 = (f32[2,64,4224]{2,1,0:T(8,128)S(1)}, f32[2,64,4224]{2,1,0:T(8,128)S(1)}, u32[]{:S(2)}, u32[]{:S(2)}) collective-permute-start(f32[2,64,4224]{2,1,0:T(8,128)S(1)} %bitcast.405), channel_id=1, source_target_pairs={{0,4},{4,0},{8,12},{12,8},{16,20},{20,16},{24,28},{28,24},{1,5},{5... | collective-permute-start | bytes 6488072 | tf_op jit(solution)/shard_map/ppermute | solution.py:19
  417.3 5.9 collective-permute-start.43
  419.2 5.7 collective-permute-start.44
  423.1 3.1 collective-permute-start.34
  424.4 3.3 collective-permute-start.35
  425.0 5.7 collective-permute-start.7
  426.3 5.5 collective-permute-start.8
  (52 other events, 472.1 us)
Sparse Core Ops, SparseCore 0:
  75.6 28.2 all-gather.6
  574.5 23.9 all-gather.8

commit v2 on v1

--- a/solution.py
+++ b/solution.py
@@ -14,35 +14,8 @@
 lanes = 128
 
 
-def swap(value, bit):
-    count = lax.axis_size("seq")
-    return lax.ppermute(value, "seq", [(i, i ^ bit) for i in range(count)])
-
-
 def gather_rows(shard):
-    count = lax.axis_size("seq")
-    if count != 8:
-        return lax.all_gather(shard, "seq", axis=0, tiled=True)
-    me = lax.axis_index("seq")
-    rows, columns = shard.shape
-    half = rows // 2
-    across_x = swap(shard, 2)
-    across_y = swap(shard, 4)
-    corner_top = swap(across_x[:half], 4)
-    corner_low = swap(across_y[half:], 2)
-    full = jnp.zeros((count, 2, half, columns), shard.dtype)
-    pieces = (
-        (shard.reshape(2, half, columns), 0, 0),
-        (across_x.reshape(2, half, columns), 2, 0),
-        (across_y.reshape(2, half, columns), 4, 0),
-        (corner_top[None], 6, 0),
-        (corner_low[None], 6, 1),
-    )
-    for piece, bit, part in pieces:
-        full = lax.dynamic_update_slice(full, piece[None], (me ^ bit, part, 0, 0))
-    for piece, bit, part in pieces:
-        full = lax.dynamic_update_slice(full, swap(piece, 1)[None], (me ^ bit ^ 1, part, 0, 0))
-    return full.reshape(count * rows, columns)
+    return lax.all_gather(shard, "seq", axis=0, tiled=True)
 
 
 def product_grad(left, right):
@@ -54,19 +27,528 @@
     return high.astype(jnp.bfloat16), (value - high).astype(jnp.bfloat16)
 
 
-def slot_of(count):
-    table, chunk, left, right = [], 0, 0, 0
-    for lefts, rights in count:
-        table.append((chunk, left, right, rights))
-        chunk, left, right = chunk + lefts * rights, left + lefts, right + rights
-    return table, chunk
-
-
-def reduce_body(
-    count, left_high, left_low, right_high, right_low, extra, out,
-    away, keep, got, got_x, got_y, got_xy, got_yx, part, from_edge, from_inner, sent, came,
+def halves(value):
+    high = value.astype(jnp.bfloat16)
+    return high, (value - high.astype(jnp.float32)).astype(jnp.bfloat16)
+
+
+def contract(left, right, left_dim, right_dim, precision=None):
+    return lax.dot_general(
+        left, right, (((left_dim,), (right_dim,)), ((), ())),
+        precision=precision, preferred_element_type=jnp.float32,
+    )
+
+
+def turned(left, right):
+    return contract(left, right, 0, 0)
+
+
+def three(left, right, left_dim, right_dim):
+    (high, low), (other, rest) = left, right
+    return contract(high, other, left_dim, right_dim) + (
+        contract(low, other, left_dim, right_dim) + contract(high, rest, left_dim, right_dim)
+    )
+
+
+def place_of(device):
+    return (device % 2) * 4 + device // 2
+
+
+gather_shapes = ((1, 8), (1, 16), (2, 4), (1, 16), (4, 4))
+
+
+def forward_body(
+    value_ref, mix_ref, merge_ref, widen_ref, narrow_ref,
+    normed_h, normed_l, mixed_h, mixed_l, shared_w, affine, key_valid, row_valid, masked, g_out, gain_two,
+    w_high, w_low, value_pre, attended, projected, shared_pre, soft, cand_pre, middle, block_out,
+    two_h, two_l, gated_h, gated_l, hidden_h, hidden_l, g_wide,
+    buf, stage_h, stage_l, g_hidden, loaded, sent, came, stored,
 ):
-    table, chunks = slot_of(count)
+    weights = (value_ref, mix_ref, merge_ref, widen_ref, narrow_ref)
+    firsts, chunks = chunk_table(gather_shapes)
+    depth, delay = buf.shape[0], 2
+    width = buf.shape[-1]
+    half = lanes * 4
+    me, level = lax.axis_index("seq"), lax.axis_index("batch")
+    core, along_x, along_y = me % 2, (me // 2) % 2, me // 4
+    id_sibling = me + 1 - 2 * core
+    id_x, id_y = me + 2 - 4 * along_x, me + 4 - 8 * along_y
+    id_corner = id_x + 4 - 8 * along_y
+    mine, at_x, at_y, at_corner = (place_of(device) for device in (me, id_x, id_y, id_corner))
+    above, below = (level + 1) % 4, (level + 3) % 4
+    quarter, eighth = lanes // 4, lanes // 8
+
+    barrier = pltpu.get_barrier_semaphore()
+    for target in (
+        {"seq": id_sibling}, {"seq": id_x}, {"seq": id_y}, {"batch": above}, {"batch": below}
+    ):
+        pl.semaphore_signal(barrier, inc=1, **on_other(**target))
+    pl.semaphore_wait(barrier, 5)
+
+    def link(kind, chunk):
+        slot = chunk % depth
+
+        def rows(place, start, count):
+            return buf.at[slot, place, pl.ds(pl.multiple_of(start, 8), count)]
+
+        piece, target = (
+            lambda: (buf.at[slot, mine], {"seq": id_x}),
+            lambda: (buf.at[slot, mine], {"seq": id_y}),
+            lambda: (buf.at[slot, mine], {"seq": id_sibling}),
+            lambda: (rows(at_x, level * quarter, eighth), {"seq": id_y}),
+            lambda: (rows(at_y, level * quarter + eighth, eighth), {"seq": id_x}),
+            lambda: (buf.at[slot, at_x], {"seq": id_sibling}),
+            lambda: (buf.at[slot, at_y], {"seq": id_sibling}),
+            lambda: (rows(at_corner, level * quarter, quarter), {"batch": above}),
+            lambda: (rows(at_corner, ((level + 3) % 4) * quarter, quarter), {"batch": above}),
+            lambda: (rows(at_corner, ((level + 2) % 4) * quarter, quarter), {"batch": above}),
+            lambda: (buf.at[slot, at_corner], {"seq": id_sibling}),
+        )[kind]()
+        return pltpu.make_async_remote_copy(
+            src_ref=piece, dst_ref=piece, send_sem=sent.at[kind, slot], recv_sem=came.at[kind, slot],
+            **on_other(**target),
+        )
+
+    def load(chunk):
+        slot = chunk % depth
+        for number, ((blocks, wide), first, weight) in enumerate(
+            zip(gather_shapes, firsts, weights)
+        ):
+
+            @pl.when((chunk >= first) & (chunk < first + blocks * wide))
+            def _(number=number, first=first, wide=wide, weight=weight):
+                row = ((chunk - first) // wide) * lanes
+                column = ((chunk - first) % wide) * width
+                if number == 1:
+                    column = column + jnp.where(column >= weights[2].shape[1], lanes, 0)
+                source = weight.at[
+                    pl.ds(pl.multiple_of(row, lanes), lanes),
+                    pl.ds(pl.multiple_of(column, lanes), width),
+                ]
+                pltpu.make_async_copy(source, buf.at[slot, mine], loaded.at[slot]).start()
+
+    def exchange(done, begun):
+        def phase(chunk):
+            for kind in done:
+                link(kind, chunk).wait()
+            for kind in begun:
+                link(kind, chunk).start()
+
+        return phase
+
+    def send(chunk):
+        slot = chunk % depth
+        first = value_ref.at[pl.ds(0, lanes), pl.ds(0, width)]
+        pltpu.make_async_copy(first, buf.at[slot, mine], loaded.at[slot]).wait()
+        for kind in (0, 1, 2):
+            link(kind, chunk).start()
+
+    def store(chunk, kind):
+        return pltpu.make_async_copy(
+            (stage_h, stage_l)[kind].at[chunk % 2],
+            (w_high, w_low)[kind].at[chunk],
+            stored.at[kind, chunk % 2],
+        )
+
+    def product(left_h, left_l, right):
+        return three((left_h[0], left_l[0]), (right[0][0], right[1][0]), 1, 0) + three(
+            (left_h[1], left_l[1]), (right[0][1], right[1][1]), 1, 0
+        )
+
+    sequences, block_len = soft.shape[:2]
+
+    def attention():
+        shared_full = halves(shared_w[...])
+        total = three(
+            (mixed_h[0], mixed_l[0]), (shared_full[0][:, :half], shared_full[1][:, :half]), 1, 1
+        ) + three(
+            (mixed_h[1], mixed_l[1]), (shared_full[0][:, half:], shared_full[1][:, half:]), 1, 1
+        )
+        shared_pre[...] = total
+        shared = total * jax.nn.sigmoid(total)
+        queries = shared * affine[0:1] + affine[2:3]
+        keys = shared * affine[1:2]
+        for s in range(sequences):
+            span = slice(s * block_len, (s + 1) * block_len)
+            scores = contract(queries[span], keys[span], 1, 1, exact) * shared.shape[1] ** (-0.5)
+            scores = jnp.where(key_valid[s] > 0.5, scores, masked_score)
+            weight = jnp.exp(scores - jnp.max(scores, axis=1, keepdims=True))
+            soft[s] = weight / jnp.sum(weight, axis=1, keepdims=True)
+
+    def put(target_h, target_l, index, column, value):
+        high, low = halves(value)
+        target_h[(*index, slice(None), pl.ds(pl.multiple_of(column, lanes), lanes))] = high
+        target_l[(*index, slice(None), pl.ds(pl.multiple_of(column, lanes), lanes))] = low
+
+    def complete(chunk):
+        slot = chunk % depth
+        link(10, chunk).wait()
+
+        @pl.when(chunk >= 2)
+        def _():
+            store(chunk - 2, 0).wait()
+            store(chunk - 2, 1).wait()
+
+        right = halves(buf[slot].reshape(2, half, width))
+        stage_h[chunk % 2] = right[0]
+        stage_l[chunk % 2] = right[1]
+        store(chunk, 0).start()
+        store(chunk, 1).start()
+
+        def among(number):
+            blocks, wide = gather_shapes[number]
+            return (chunk >= firsts[number]) & (chunk < firsts[number] + blocks * wide)
+
+        @pl.when(among(0))
+        def _():
+            total = product(normed_h, normed_l, right)
+            value_pre[chunk] = total
+            values = total * jax.nn.sigmoid(total)
+            for s in range(sequences):
+                span = slice(s * block_len, (s + 1) * block_len)
+                attended[chunk, span] = contract(soft[s], values[span], 1, 0, exact)
+
+        @pl.when(among(1))
+        def _():
+            tile = chunk - firsts[1]
+            total = product(mixed_h, mixed_l, right)
+            projected[tile] = total
+
+            @pl.when((tile >= 4) & (tile < 12))
+            def _():
+                block = tile - 4
+                gated = attended[block] * total * jax.nn.sigmoid(total)
+                for j in range(2):
+                    cut = gated[:, j * lanes : (j + 1) * lanes]
+                    put(gated_h, gated_l, (j, block % 2), (block // 2) * lanes, cut)
+
+        @pl.when(among(2))
+        def _():
+            j, tile = (chunk - firsts[2]) // 4, (chunk - firsts[2]) % 4
+            total = product(gated_h.at[j], gated_l.at[j], right)
+
+            @pl.when(j == 0)
+            def _():
+                cand_pre[tile] = projected[12 + tile] + total
+
+            @pl.when(j == 1)
+            def _():
+                cand_pre[tile] = cand_pre[tile] + total
+
+            @pl.when(chunk == firsts[3] - 1)
+            def _():
+                tiles = middle.shape[0]
+                features = tiles * width
+                total = 0.0
+                for k in range(tiles):
+                    cand = cand_pre[k]
+                    cand = cand * jax.nn.sigmoid(cand)
+                    value = masked[k] + jax.nn.sigmoid(projected[k]) * (cand - masked[k])
+                    middle[k] = value
+                    total = total + jnp.sum(value, axis=1, keepdims=True)
+                centre = total / features
+                total = 0.0
+                for k in range(tiles):
+                    shifted = middle[k] - centre
+                    total = total + jnp.sum(shifted * shifted, axis=1, keepdims=True)
+                scale = lax.rsqrt(total / features + norm_eps)
+                for k in range(tiles):
+                    value = (middle[k] - centre) * scale * gain_two[k]
+                    for parity in range(2):
+                        cut = value[:, parity * lanes : (parity + 1) * lanes]
+                        put(two_h, two_l, (parity,), k * lanes, cut)
+                    block_out[k] = jnp.zeros(block_out.shape[1:], jnp.float32)
+                g_hidden[...] = jnp.zeros(g_hidden.shape, jnp.float32)
+
+        @pl.when(among(3))
+        def _():
+            tile = chunk - firsts[3]
+            total = product(two_h, two_l, right)
+            g_wide[tile] = total
+            hidden = total * jax.nn.sigmoid(total)
+            for i in range(2):
+                cut = hidden[:, i * lanes : (i + 1) * lanes]
+                index = (2 * (tile % 2) + i, (tile // 2) % 2)
+                put(hidden_h, hidden_l, index, (tile // 4) * lanes, cut)
+
+        @pl.when(among(4))
+        def _():
+            j, tile = (chunk - firsts[4]) // 4, (chunk - firsts[4]) % 4
+            block_out[tile] = block_out[tile] + product(hidden_h.at[j], hidden_l.at[j], right)
+            grad = halves(g_out[tile])
+            for parity in range(2):
+                back = three(grad, (right[0][parity], right[1][parity]), 1, 1)
+                g_hidden[j, parity] = g_hidden[j, parity] + back
+
+    phases = (
+        (0, load),
+        (1, send),
+        (1 + delay, exchange((0, 1, 2), (3, 4, 5, 6))),
+        (1 + 2 * delay, exchange((3, 4, 5, 6), (7,))),
+        (1 + 3 * delay, exchange((7,), (8,))),
+        (1 + 4 * delay, exchange((8,), (9,))),
+        (1 + 5 * delay, exchange((9,), (10,))),
+        (1 + 6 * delay, complete),
+    )
+
+    def step(at, carry):
+        for after, phase in phases[-2:0:-1]:
+
+            @pl.when((at >= after) & (at < after + chunks))
+            def _(after=after, phase=phase):
+                phase(at - after)
+
+        pl.when(at < chunks)(lambda: load(at))
+        pl.when(at == 2)(attention)
+
+        @pl.when(at >= phases[-1][0])
+        def _():
+            complete(at - phases[-1][0])
+
+        return carry
+
+    lax.fori_loop(0, chunks + phases[-1][0], step, 0)
+    for chunk in (chunks - 2, chunks - 1):
+        for kind in range(2):
+            store(chunk, kind).wait()
+    for k in range(middle.shape[0]):
+        block_out[k] = (middle[k] + block_out[k]) * row_valid[...]
+    for k in range(g_wide.shape[0]):
+        for i in range(2):
+            span = slice(i * lanes, (i + 1) * lanes)
+            back = g_hidden[2 * (k % 2) + i, (k // 2) % 2, :, (k // 4) * lanes : (k // 4 + 1) * lanes]
+            wide = g_wide[k, :, span]
+            g_wide[k, :, span] = back * silu_slope(wide)
+
+
+def call_forward(weights, operands, rows, sequences):
+    width = 256
+    _, chunks = chunk_table(gather_shapes)
+    vmem, anywhere = pl.BlockSpec(memory_space=pltpu.VMEM), pl.BlockSpec(memory_space=pl.ANY)
+
+    def f32(*shape):
+        return jax.ShapeDtypeStruct(shape, jnp.float32)
+
+    def b16(*shape):
+        return jax.ShapeDtypeStruct(shape, jnp.bfloat16)
+
+    half, block_len = 4 * lanes, rows // sequences
+    shapes = [b16(chunks, 2, half, width)] * 2 + [
+        f32(8, rows, width), f32(8, rows, width), f32(16, rows, width), f32(rows, lanes),
+        f32(sequences, block_len, block_len), f32(4, rows, width), f32(4, rows, width), f32(4, rows, width),
+        b16(2, rows, half), b16(2, rows, half), b16(2, 2, rows, half), b16(2, 2, rows, half),
+        b16(4, 2, rows, half), b16(4, 2, rows, half), f32(16, rows, width),
+    ]
+    depth = 16
+    return pl.pallas_call(
+        forward_body,
+        out_shape=shapes,
+        in_specs=[anywhere] * len(weights) + [vmem] * len(operands),
+        out_specs=[anywhere] * 2 + [vmem] * (len(shapes) - 2),
+        scratch_shapes=[
+            pltpu.VMEM((depth, 8, lanes, width), jnp.float32),
+            pltpu.VMEM((2, 2, half, width), jnp.bfloat16),
+            pltpu.VMEM((2, 2, half, width), jnp.bfloat16),
+            pltpu.VMEM((4, 2, rows, half), jnp.float32),
+            pltpu.SemaphoreType.DMA((depth,)),
+            pltpu.SemaphoreType.DMA((11, depth)),
+            pltpu.SemaphoreType.DMA((11, depth)),
+            pltpu.SemaphoreType.DMA((2, 2)),
+        ],
+        compiler_params=pltpu.CompilerParams(
+            collective_id=2, has_side_effects=True, vmem_limit_bytes=60 * 1024 * 1024
+        ),
+    )(*weights, *operands)
+
+
+def backward_body(
+    w_high, w_low, g_wide, value_pre, attended, projected, shared_pre, soft, cand_pre, middle, masked, g_out,
+    gain_two, shared_w, affine, key_valid,
+    g_projected, g_val, g_shared, g_mixed, g_normed, g_rest, gain_sum, affine_sum,
+    buf_h, buf_l, g_two, g_gated, fetched,
+):
+    firsts, _ = chunk_table(gather_shapes)
+    steps = 48
+    tiles, rows, width = masked.shape
+    half = 4 * lanes
+    features = tiles * width
+    sequences, block_len = soft.shape[:2]
+
+    def fetch(step, kind):
+        chunk = jnp.where(
+            step < 16, firsts[3] + step, jnp.where(step < 24, step + 8, jnp.where(step < 40, step - 16, step - 40))
+        )
+        slot = step % 4
+        return pltpu.make_async_copy(
+            (w_high, w_low)[kind].at[chunk], (buf_h, buf_l)[kind].at[slot], fetched.at[kind, slot]
+        )
+
+    def both(step, call):
+        for kind in range(2):
+            getattr(fetch(step, kind), call)()
+
+    for step in range(3):
+        both(step, "start")
+
+    def back(grad, slot, parity):
+        return three(halves(grad), (buf_h[slot, parity], buf_l[slot, parity]), 1, 1)
+
+    def norm_two_back():
+        total = 0.0
+        for k in range(tiles):
+            total = total + jnp.sum(middle[k], axis=1, keepdims=True)
+        centre = total / features
+        total = 0.0
+        for k in range(tiles):
+            shifted = middle[k] - centre
+            total = total + jnp.sum(shifted * shifted, axis=1, keepdims=True)
+        scale = lax.rsqrt(total / features + norm_eps)
+
+        def grad_of(k):
+            span = slice(k * lanes, (k + 1) * lanes)
+            return jnp.concatenate([g_two[0, :, span], g_two[1, :, span]], axis=1)
+
+        plain, crossed = 0.0, 0.0
+        for k in range(tiles):
+            grad, hat = grad_of(k), (middle[k] - centre) * scale
+            gain_sum[k] = jnp.sum(grad * hat, axis=0, keepdims=True)
+            inner = grad * gain_two[k]
+            plain = plain + jnp.sum(inner, axis=1, keepdims=True)
+            crossed = crossed + jnp.sum(inner * hat, axis=1, keepdims=True)
+        plain, crossed = plain / features, crossed / features
+        for k in range(tiles):
+            inner, hat = grad_of(k) * gain_two[k], (middle[k] - centre) * scale
+            g_middle = g_out[k] + (inner - plain - hat * crossed) * scale
+            update = jax.nn.sigmoid(projected[k])
+            pre = cand_pre[k]
+            gate = jax.nn.sigmoid(pre)
+            g_rest[k] = g_middle * (1.0 - update)
+            g_projected[k] = g_middle * (pre * gate - masked[k]) * update * (1.0 - update)
+            g_projected[12 + k] = g_middle * update * (gate * (1.0 + pre * (1.0 - gate)))
+
+    def attention_back():
+        g_soft = [0.0] * sequences
+        for m in range(8):
+            span = slice((m // 2) * lanes, (m // 2 + 1) * lanes)
+            grad = jnp.concatenate([g_gated[0, m % 2, :, span], g_gated[1, m % 2, :, span]], axis=1)
+            pre = projected[4 + m]
+            gate = jax.nn.sigmoid(pre)
+            g_attended = grad * pre * gate
+            g_projected[4 + m] = grad * attended[m] * (gate * (1.0 + pre * (1.0 - gate)))
+            pre = value_pre[m]
+            gate = jax.nn.sigmoid(pre)
+            values, slope = pre * gate, gate * (1.0 + pre * (1.0 - gate))
+            for s in range(sequences):
+                part = slice(s * block_len, (s + 1) * block_len)
+                own = halves(g_attended[part])
+                g_soft[s] = g_soft[s] + three(own, halves(values[part]), 1, 1)
+                g_val[m, part] = three(halves(soft[s]), own, 0, 0) * slope[part]
+        pre = shared_pre[...]
+        gate = jax.nn.sigmoid(pre)
+        shared, slope = pre * gate, gate * (1.0 + pre * (1.0 - gate))
+        score_scale = shared.shape[1] ** (-0.5)
+        queries = shared * affine[0:1] + affine[2:3]
+        keys = shared * affine[1:2]
+        sums = [0.0, 0.0, 0.0]
+        for s in range(sequences):
+            part = slice(s * block_len, (s + 1) * block_len)
+            weight = soft[s]
+            g_scores = weight * (g_soft[s] - jnp.sum(g_soft[s] * weight, axis=1, keepdims=True))
+            g_scores = jnp.where(key_valid[s] > 0.5, g_scores, 0.0) * score_scale
+            g_queries = contract(g_scores, keys[part], 1, 0, exact)
+            g_keys = contract(g_scores, queries[part], 0, 0, exact)
+            g_shared[part] = (g_queries * affine[0:1] + g_keys * affine[1:2]) * slope[part]
+            for number, term in enumerate((g_queries * shared[part], g_keys * shared[part], g_queries)):
+                sums[number] = sums[number] + jnp.sum(term, axis=0, keepdims=True)
+        for number in range(3):
+            affine_sum[number : number + 1] = sums[number]
+        own, full = halves(g_shared[...]), halves(shared_w[...])
+        for parity in range(2):
+            span = slice(parity * half, (parity + 1) * half)
+            g_mixed[parity] = three(own, (full[0][:, span], full[1][:, span]), 1, 0)
+
+    g_two[...] = jnp.zeros(g_two.shape, jnp.float32)
+    g_gated[...] = jnp.zeros(g_gated.shape, jnp.float32)
+    g_normed[...] = jnp.zeros(g_normed.shape, jnp.float32)
+
+    def work(step, carry):
+        slot = step % 4
+        pl.when(step + 3 < steps)(lambda: both(step + 3, "start"))
+        both(step, "wait")
+        pl.when(step == 16)(norm_two_back)
+        pl.when(step == 24)(attention_back)
+
+        @pl.when(step < 16)
+        def _():
+            for parity in range(2):
+                g_two[parity] = g_two[parity] + back(g_wide[step], slot, parity)
+
+        @pl.when((step >= 16) & (step < 24))
+        def _():
+            j = (step - 16) // 4
+            for parity in range(2):
+                more = back(g_projected[12 + step % 4], slot, parity)
+                g_gated[j, parity] = g_gated[j, parity] + more
+
+        @pl.when((step >= 24) & (step < 40))
+        def _():
+            for parity in range(2):
+                g_mixed[parity] = g_mixed[parity] + back(g_projected[step - 24], slot, parity)
+
+        @pl.when(step >= 40)
+        def _():
+            for parity in range(2):
+                g_normed[parity] = g_normed[parity] + back(g_val[step - 40], slot, parity)
+
+        return carry
+
+    lax.fori_loop(0, steps, work, 0)
+
+
+def call_backward(w_high, w_low, *operands):
+    masked = operands[8]
+    tiles, rows, width = masked.shape
+    half = 4 * lanes
+    vmem, anywhere = pl.BlockSpec(memory_space=pltpu.VMEM), pl.BlockSpec(memory_space=pl.ANY)
+    shapes = [
+        (16, rows, width), (8, rows, width), (rows, lanes), (2, rows, half), (2, rows, half),
+        (tiles, rows, width), (tiles, 1, width), (3, lanes),
+    ]
+    return pl.pallas_call(
+        backward_body,
+        out_shape=[jax.ShapeDtypeStruct(shape, jnp.float32) for shape in shapes],
+        in_specs=[anywhere] * 2 + [vmem] * len(operands),
+        out_specs=[vmem] * len(shapes),
+        scratch_shapes=[
+            pltpu.VMEM((4, 2, half, width), jnp.bfloat16),
+            pltpu.VMEM((4, 2, half, width), jnp.bfloat16),
+            pltpu.VMEM((2, rows, half), jnp.float32),
+            pltpu.VMEM((2, 2, rows, half), jnp.float32),
+            pltpu.SemaphoreType.DMA((2, 4)),
+        ],
+        compiler_params=pltpu.CompilerParams(vmem_limit_bytes=60 * 1024 * 1024),
+    )(w_high, w_low, *operands)
+
+
+def on_other(**coordinate):
+    return dict(device_id=coordinate, device_id_type=pl.DeviceIdType.MESH)
+
+
+def chunk_table(shapes):
+    firsts, chunk = [], 0
+    for blocks, wide in shapes:
+        firsts.append(chunk)
+        chunk += blocks * wide
+    return firsts, chunk
+
+
+def reduce_body(shapes, offsets, *refs):
+    highs, refs = refs[: len(shapes)], refs[len(shapes) :]
+    lows, refs = refs[: len(shapes)], refs[len(shapes) :]
+    rights, refs = refs[: len(shapes)], refs[len(shapes) :]
+    extra, out, away, keep, got, got_x, got_y, got_xy, got_yx, part = refs[:10]
+    from_edge, from_inner, sent, came = refs[10:]
+    firsts, chunks = chunk_table(shapes)
     depth, delay = away.shape[0], 2
     me, place = lax.axis_index("seq"), lax.axis_index("batch")
     core, along_x, along_y = me % 2, (me // 2) % 2, me // 4
@@ -115,24 +597,23 @@
         slot = chunk % depth
         to_sibling = link(0, chunk)
 
-        @pl.when(chunk < chunks)
-        def _():
-            left, right = chunk * 0, chunk * 0
-            for first, first_left, first_right, rights in table:
-                inside = chunk >= first
-                left = jnp.where(inside, first_left + (chunk - first) // rights, left)
-                right = jnp.where(inside, first_right + (chunk - first) % rights, right)
-
-            def product(parity):
-                high, low = left_high[left, parity], left_low[left, parity]
-                other = right_high[right]
-                dot = functools.partial(jnp.dot, preferred_element_type=jnp.float32)
-                total = dot(high, other) + (dot(low, other) + dot(high, right_low[right]))
-                return total.reshape(away.shape[1:])
-
-            away[slot] = product(1 - core)
-            to_sibling.start()
-            keep[slot] = product(core)
+        for (blocks, wide), first, shift, high, low, right in zip(
+            shapes, firsts, offsets, highs, lows, rights
+        ):
+
+            @pl.when((chunk >= first) & (chunk < first + blocks * wide))
+            def _(first=first, wide=wide, shift=shift, high=high, low=low, right=right):
+                block = (chunk - first) // wide
+                other, rest = halves(right[shift + (chunk - first) % wide])
+
+                def product(parity):
+                    top, under = high[block, parity], low[block, parity]
+                    total = turned(top, other) + (turned(under, other) + turned(top, rest))
+                    return total.reshape(away.shape[1:])
+
+                away[slot] = product(1 - core)
+                to_sibling.start()
+                keep[slot] = product(core)
 
         @pl.when(chunk == chunks)
         def _():
@@ -220,26 +701,16 @@
     lax.fori_loop(0, chunks + 1 + (len(phases) - 1) * delay, step, 0)
 
 
-def reduce_grads(products, extra, width=256):
-    rows = products[0][0].shape[0]
-    lefts, rights, count = [], [], []
-    for left, right in products:
-        blocks = left.shape[1] // (8 * lanes)
-        cut = left.reshape(rows, 4, 2, blocks, lanes).transpose(3, 2, 1, 4, 0)
-        lefts.append(cut.reshape(blocks, 2, 4 * lanes, rows))
-        wide = right.shape[1] // width
-        rights.append(right.reshape(rows, wide, width).transpose(1, 0, 2))
-        count.append((blocks, wide))
-    left_high, left_low = split(jnp.concatenate(lefts, axis=0))
-    right_high, right_low = split(jnp.concatenate(rights, axis=0))
-    _, chunks = slot_of(count)
-    pairs = extra.reshape(4, 2, lanes, width).transpose(1, 0, 2, 3).reshape(2, 4 * lanes, width)
+def reduce_grads(products, extra):
+    shapes = tuple((item[0].shape[0], item[4]) for item in products)
+    width = extra.shape[-1]
+    _, chunks = chunk_table(shapes)
     depth, half = 8, lanes // 2
     vmem = pl.BlockSpec(memory_space=pltpu.VMEM)
     out = pl.pallas_call(
-        functools.partial(reduce_body, tuple(count)),
+        functools.partial(reduce_body, shapes, tuple(item[3] for item in products)),
         out_shape=jax.ShapeDtypeStruct((chunks + 1, 2, half, width), jnp.float32),
-        in_specs=[vmem] * 5,
+        in_specs=[vmem] * (3 * len(products) + 1),
         out_specs=vmem,
         scratch_shapes=[pltpu.VMEM((depth, 2, 2, 2, half, width), jnp.float32)] * 3
         + [pltpu.VMEM((depth, 2, half, width), jnp.float32)] * 2
@@ -249,32 +720,18 @@
         compiler_params=pltpu.CompilerParams(
             collective_id=1, has_side_effects=True, vmem_limit_bytes=60 * 1024 * 1024
         ),
-    )(left_high, left_low, right_high, right_low, pairs)
+    )(
+        *[item[0] for item in products],
+        *[item[1] for item in products],
+        *[item[2] for item in products],
+        extra,
+    )
     out = out.reshape(chunks + 1, lanes, width)
     grads = []
-    for (blocks, wide), (first, _, _, _) in zip(count, slot_of(count)[0]):
+    for (blocks, wide), first in zip(shapes, chunk_table(shapes)[0]):
         piece = out[first : first + blocks * wide].reshape(blocks, wide, lanes, width)
         grads.append(piece.transpose(0, 2, 1, 3).reshape(blocks * lanes, wide * width))
     return grads, out[chunks]
-
-
-def all_grads(products, packed, single):
-    count = lax.axis_size("seq")
-    rows, features = packed.shape
-    blocks = packed.reshape(rows, count, features // count).transpose(1, 0, 2)
-    last = product_grad(*single)
-    if count != 8 or lax.axis_size("batch") != 4:
-
-        def total(whole, tiled):
-            part = lax.psum_scatter(whole, "seq", scatter_dimension=0, tiled=tiled)
-            return lax.psum(part, "batch")
-
-        wholes = [total(product_grad(*pair), True) for pair in products]
-        return wholes, total(blocks, False), total(last, True)
-    blocks = jnp.pad(blocks, ((0, 0), (0, lanes - rows), (0, 0)))
-    extra = jnp.concatenate([last.reshape(count, lanes, -1), blocks], axis=2)
-    wholes, rest = reduce_grads(products, extra)
-    return wholes, rest[:rows, lanes:], rest[:, :lanes]
 
 
 def tree_sum(terms):
@@ -401,6 +858,164 @@
 
 def times_back(left, right):
     return lax.dot_general(left, right, (((1,), (1,)), ((), ())), precision=triple)
+
+
+def plain_layer(masked_in, normed, mix_pre, g_out, row_valid, key_valid, affine, gain_two, weights):
+    value_full, mix_full, merge_full, widen_full, narrow_full = (gather_rows(w) for w in weights)
+    rows, width = masked_in.shape
+    sequences, _, block_len = key_valid.shape
+    value_dim, shared_dim = value_full.shape[1], affine.shape[0]
+    mixed = silu(mix_pre)
+    value_pre = times(normed, value_full)
+    values = silu(value_pre)
+    projected = times(mixed, mix_full)
+    second_cut = width + shared_dim
+    third_cut = second_cut + value_dim
+    update = jax.nn.sigmoid(projected[:, :width])
+    shared_pre = projected[:, width:second_cut]
+    reset_pre = projected[:, second_cut:third_cut]
+    shared = silu(shared_pre)
+    reset_gate = silu(reset_pre)
+    queries = (shared * affine[:, 0] + affine[:, 2]).reshape(sequences, block_len, shared_dim)
+    key_rows = (shared * affine[:, 1]).reshape(sequences, block_len, shared_dim)
+    score_scale = shared_dim ** (-0.5)
+    scores = jnp.einsum("cqz,ckz->cqk", queries, key_rows, precision=exact) * score_scale
+    scores = jnp.where(key_valid > 0.5, scores, masked_score)
+    soft = jax.nn.softmax(scores, axis=-1)
+    values_cut = values.reshape(sequences, block_len, value_dim)
+    attended = jnp.einsum("cqk,ckv->cqv", soft, values_cut, precision=triple)
+    attended = attended.reshape(rows, value_dim)
+    gated = attended * reset_gate
+    cand_pre = projected[:, third_cut:] + times(gated, merge_full)
+    candidate = silu(cand_pre)
+    middle = masked_in + update * (candidate - masked_in)
+    hat_two, scale_two = normalise(middle)
+    normed_two = hat_two * gain_two
+    wide_pre = times(normed_two, widen_full)
+    hidden = silu(wide_pre)
+    block_out = (middle + times(hidden, narrow_full)) * row_valid
+
+    g_wide = times_back(g_out, narrow_full) * silu_slope(wide_pre)
+    g_normed_two = times_back(g_wide, widen_full)
+    gain_sum = jnp.sum(g_normed_two * hat_two, axis=0)
+    g_middle = g_out + normalise_back(g_normed_two, gain_two, hat_two, scale_two)
+    g_cand = g_middle * update * silu_slope(cand_pre)
+    g_gated = times_back(g_cand, merge_full)
+    g_attended = (g_gated * reset_gate).reshape(sequences, block_len, value_dim)
+    g_soft = jnp.einsum("cqv,ckv->cqk", g_attended, values_cut, precision=triple)
+    g_values = jnp.einsum("cqk,cqv->ckv", soft, g_attended, precision=triple)
+    g_scores = soft * (g_soft - jnp.sum(g_soft * soft, axis=-1, keepdims=True))
+    g_scores = jnp.where(key_valid > 0.5, g_scores, 0.0) * score_scale
+    g_queries = jnp.einsum("cqk,ckz->cqz", g_scores, key_rows, precision=exact)
+    g_keys = jnp.einsum("cqk,cqz->ckz", g_scores, queries, precision=exact)
+    g_queries = g_queries.reshape(rows, shared_dim)
+    g_keys = g_keys.reshape(rows, shared_dim)
+    terms = (g_queries * shared, g_keys * shared, g_queries)
+    affine_sum = jnp.stack([jnp.sum(term, axis=0) for term in terms])
+    g_shared = (g_queries * affine[:, 0] + g_keys * affine[:, 1]) * silu_slope(shared_pre)
+    g_update = g_middle * (candidate - masked_in) * update * (1.0 - update)
+    g_reset = g_gated * attended * silu_slope(reset_pre)
+    g_projected = jnp.concatenate([g_update, g_shared, g_reset, g_cand], axis=1)
+    g_mixed = times_back(g_projected, mix_full)
+    g_val = g_values.reshape(rows, value_dim) * silu_slope(value_pre)
+    g_from_values = times_back(g_val, value_full)
+
+    def total(packed):
+        count = lax.axis_size("seq")
+        features = packed.shape[1] // count
+
+        def reduced(whole, tiled=True):
+            part = lax.psum_scatter(whole, "seq", scatter_dimension=0, tiled=tiled)
+            return lax.psum(part, "batch")
+
+        pairs = (
+            (normed, g_val),
+            (mixed, g_projected),
+            (gated, g_cand),
+            (normed_two, g_wide),
+            (hidden, g_out),
+        )
+        grads = tuple(reduced(product_grad(*pair)) for pair in pairs)
+        blocks = packed.reshape(-1, count, features).transpose(1, 0, 2)
+        return grads + (reduced(blocks, False),)
+
+    return block_out, g_mixed, g_from_values, g_middle * (1.0 - update), gain_sum, affine_sum, total
+
+
+def to_tiles(value):
+    return value.reshape(value.shape[0], -1, 2 * lanes).transpose(1, 0, 2)
+
+
+def from_tiles(value):
+    return value.transpose(1, 0, 2).reshape(value.shape[1], -1)
+
+
+def to_places(value):
+    rows, columns = value.shape
+    return value.reshape(rows, 4, 2, columns // 8).transpose(2, 0, 1, 3).reshape(2, rows, -1)
+
+
+def from_places(value):
+    _, rows, columns = value.shape
+    return value.reshape(2, rows, 4, columns // 4).transpose(1, 2, 0, 3).reshape(rows, -1)
+
+
+def plane_layer(
+    masked_in, normed, mix_pre, g_out, row_valid, key_valid, affine, gain_two, weights, shared_full
+):
+    rows, width = masked_in.shape
+    sequences = key_valid.shape[0]
+    mixed = silu(mix_pre)
+    normed_split, mixed_split = split(to_places(normed)), split(to_places(mixed))
+    shared_w = shared_full.reshape(lanes, 4, 2, lanes).transpose(0, 2, 1, 3).reshape(lanes, width)
+    affine_rows = affine.T
+    valid = key_valid.astype(jnp.float32)
+    masked, grad_tiles = to_tiles(masked_in), to_tiles(g_out)
+    gain_tiles = to_tiles(gain_two)
+    (
+        w_high, w_low, value_pre, attended, projected, shared_pre, soft, cand_pre, middle, block_out,
+        two_h, two_l, gated_h, gated_l, hidden_h, hidden_l, g_wide,
+    ) = call_forward(
+        weights,
+        (*normed_split, *mixed_split, shared_w, affine_rows, valid, row_valid, masked, grad_tiles, gain_tiles),
+        rows,
+        sequences,
+    )
+    g_projected, g_val, g_shared, g_mixed, g_normed, g_rest, gain_sum, affine_sum = call_backward(
+        w_high, w_low, g_wide, value_pre, attended, projected, shared_pre, soft, cand_pre, middle,
+        masked, grad_tiles, gain_tiles, shared_w, affine_rows, valid,
+    )
+
+    def total(packed):
+        blocks = packed.reshape(-1, 8, lanes).transpose(1, 0, 2)
+        used = blocks.shape[1]
+        blocks = jnp.pad(blocks, ((0, 0), (0, lanes - used), (0, 0)))
+        last = product_grad(mixed, g_shared)
+        extra = jnp.concatenate([last.reshape(8, lanes, lanes), blocks], axis=2)
+        extra = extra.reshape(4, 2, lanes, -1).transpose(1, 0, 2, 3).reshape(2, 4 * lanes, -1)
+        grads, rest = reduce_grads(
+            (
+                (hidden_h, hidden_l, grad_tiles, 0, 4),
+                (two_h[None], two_l[None], g_wide, 0, 16),
+                (gated_h, gated_l, g_projected, 12, 4),
+                (mixed_split[0][None], mixed_split[1][None], g_projected, 0, 16),
+                (normed_split[0][None], normed_split[1][None], g_val, 0, 8),
+            ),
+            extra,
+        )
+        narrow, widen, merge, mix, value = grads
+        mix = jnp.concatenate([mix[:, :width], rest[:, :lanes], mix[:, width:]], axis=1)
+        return value, mix, merge, widen, narrow, rest[:used, lanes:]
+
+    return (
+        from_tiles(block_out),
+        from_places(g_mixed),
+        from_places(g_normed),
+        from_tiles(g_rest),
+        gain_sum.reshape(width),
+        affine_sum,
+        total,
+    )
 
 
 def per_device(
@@ -427,26 +1042,20 @@
     own = first_gain.shape[0]
     own_shared = query_affine.shape[0]
     rows = sequences * block_len
-    value_dim = value_weight.shape[1]
     shared_dim = own_shared * count
+    plane = count == 8 and lax.axis_size("batch") == 4
 
     affine_row = jnp.pad(query_affine.reshape(-1), (0, own - 3 * own_shared))
-    packed = jnp.concatenate(
-        [
-            smooth_alpha.T,
-            smooth_delta.T,
-            smooth_beta.T,
-            smooth_gamma.T,
-            jnp.stack([first_gain, smooth_omega, second_gain, affine_row]),
-        ],
-        axis=0,
-    )
-    small = lax.all_gather(packed, "seq").transpose(1, 0, 2)
-    value_full = gather_rows(value_weight)
-    mix_full = gather_rows(mix_weight)
-    merge_full = gather_rows(merge_weight)
-    widen_full = gather_rows(widen_weight)
-    narrow_full = gather_rows(narrow_weight)
+    packed = [
+        smooth_alpha.T,
+        smooth_delta.T,
+        smooth_beta.T,
+        smooth_gamma.T,
+        jnp.stack([first_gain, smooth_omega, second_gain, affine_row]),
+    ]
+    if plane:
+        packed.append(mix_weight[:, width : width + shared_dim].T)
+    small = lax.all_gather(jnp.concatenate(packed, axis=0), "seq").transpose(1, 0, 2)
 
     tiles = (width // lanes, lanes)
     alpha_rate = jax.nn.sigmoid(small[:states].reshape(states, *tiles))
@@ -465,9 +1074,10 @@
     offsets = lax.axis_index("seq") * block_len + lax.iota(jnp.int32, block_len)
     valid = (offsets[None, :] < lengths[:, None]).astype(jnp.float32)
     row_valid = valid.reshape(rows, 1)
-    key_valid = valid.reshape(sequences, 1, block_len) > 0.5
+    key_valid = valid.reshape(sequences, 1, block_len)
 
     masked_in = tokens.reshape(rows, width) * row_valid
+    g_out = out_grad.reshape(rows, width) * row_valid
     hat_one, scale_one = normalise(masked_in)
     normed = hat_one * gain_one
     tiled = (sequences, block_len) + tiles
@@ -481,68 +1091,15 @@
         functools.partial(carried_body, False), [tiled], decay, weight, enter, local
     )
     mix_pre = smoothed.reshape(rows, width) + omega * normed
-    mixed = silu(mix_pre)
-    value_pre = times(normed, value_full)
-    values = silu(value_pre)
-    projected = times(mixed, mix_full)
-    second_cut = width + shared_dim
-    third_cut = second_cut + value_dim
-    update = jax.nn.sigmoid(projected[:, :width])
-    shared_pre = projected[:, width:second_cut]
-    reset_pre = projected[:, second_cut:third_cut]
-    shared = silu(shared_pre)
-    reset_gate = silu(reset_pre)
-    queries = (shared * affine[:, 0] + affine[:, 2]).reshape(sequences, block_len, shared_dim)
-    key_rows = (shared * affine[:, 1]).reshape(sequences, block_len, shared_dim)
-    score_scale = shared_dim ** (-0.5)
-    scores = jnp.einsum("cqz,ckz->cqk", queries, key_rows, precision=exact) * score_scale
-    scores = jnp.where(key_valid, scores, masked_score)
-    soft = jax.nn.softmax(scores, axis=-1)
-    values_cut = values.reshape(sequences, block_len, value_dim)
-    attended = jnp.einsum("cqk,ckv->cqv", soft, values_cut, precision=triple)
-    attended = attended.reshape(rows, value_dim)
-    gated = attended * reset_gate
-    cand_pre = projected[:, third_cut:] + times(gated, merge_full)
-    candidate = silu(cand_pre)
-    middle = masked_in + update * (candidate - masked_in)
-    hat_two, scale_two = normalise(middle)
-    normed_two = hat_two * gain_two
-    wide_pre = times(normed_two, widen_full)
-    hidden = silu(wide_pre)
-
-    g_out = out_grad.reshape(rows, width) * row_valid
-    g_wide = times_back(g_out, narrow_full) * silu_slope(wide_pre)
-    g_normed_two = times_back(g_wide, widen_full)
-    second_gain_sum = jnp.sum(g_normed_two * hat_two, axis=0)
-    g_middle = g_out + normalise_back(g_normed_two, gain_two, hat_two, scale_two)
-
-    g_cand = g_middle * update * silu_slope(cand_pre)
-    g_gated = times_back(g_cand, merge_full)
-    g_attended = (g_gated * reset_gate).reshape(sequences, block_len, value_dim)
-    g_reset = g_gated * attended
-    g_soft = jnp.einsum("cqv,ckv->cqk", g_attended, values_cut, precision=triple)
-    g_values = jnp.einsum("cqk,cqv->ckv", soft, g_attended, precision=triple)
-    g_scores = soft * (g_soft - jnp.sum(g_soft * soft, axis=-1, keepdims=True))
-    g_scores = jnp.where(key_valid, g_scores, 0.0) * score_scale
-    g_queries = jnp.einsum("cqk,ckz->cqz", g_scores, key_rows, precision=exact)
-    g_keys = jnp.einsum("cqk,cqz->ckz", g_scores, queries, precision=exact)
-    g_queries = g_queries.reshape(rows, shared_dim)
-    g_keys = g_keys.reshape(rows, shared_dim)
-    affine_sum = jnp.stack(
-        [
-            jnp.sum(g_queries * shared, axis=0),
-            jnp.sum(g_keys * shared, axis=0),
-            jnp.sum(g_queries, axis=0),
-        ],
-        axis=1,
-    )
-    g_shared = (g_queries * affine[:, 0] + g_keys * affine[:, 1]) * silu_slope(shared_pre)
-    g_update = g_middle * (candidate - masked_in) * update * (1.0 - update)
-    g_reset_pre = g_reset * silu_slope(reset_pre)
-    g_projected = jnp.concatenate([g_update, g_shared, g_reset_pre, g_cand], axis=1)
-    g_smooth = times_back(g_projected, mix_full) * silu_slope(mix_pre)
-    g_val = g_values.reshape(rows, value_dim) * silu_slope(value_pre)
-    g_from_values = times_back(g_val, value_full)
+
+    weights = (value_weight, mix_weight, merge_weight, widen_weight, narrow_weight)
+    operands = (masked_in, normed, mix_pre, g_out, row_valid, key_valid, affine, gain_two, weights)
+    if plane:
+        results = plane_layer(*operands, small[4 * states + 4 :])
+    else:
+        results = plain_layer(*operands)
+    block_out, g_mixed, g_from_values, g_rest, second_gain_sum, affine_sum, total = results
+    g_smooth = g_mixed * silu_slope(mix_pre)
 
     smooth_tiled = g_smooth.reshape(tiled)
     back_local, back_ends = call_kernel(
@@ -570,13 +1127,11 @@
     gamma_grad = alpha_rate * beta * out_scale * direct
 
     g_normed = g_from_values + g_smooth * omega + back_full.reshape(rows, width)
-    tokens_grad = (
-        g_middle * (1.0 - update) + normalise_back(g_normed, gain_one, hat_one, scale_one)
-    ) * row_valid
+    tokens_grad = (g_rest + normalise_back(g_normed, gain_one, hat_one, scale_one)) * row_valid
     first_gain_sum = jnp.sum(g_normed * hat_one, axis=0)
     omega_sum = jnp.sum(g_smooth * normed, axis=0)
     affine_rows = jnp.pad(
-        affine_sum.reshape(count, 3 * own_shared), ((0, 0), (0, own - 3 * own_shared))
+        affine_sum.T.reshape(count, 3 * own_shared), ((0, 0), (0, own - 3 * own_shared))
     )
     small_rows = [
         alpha_grad.reshape(states, width),
@@ -585,21 +1140,9 @@
         gamma_grad.reshape(states, width),
         jnp.stack([first_gain_sum, omega_sum, second_gain_sum, affine_rows.reshape(width)]),
     ]
-    wholes, small_grad, shared_grad = all_grads(
-        (
-            (hidden, g_out),
-            (normed_two, g_wide),
-            (gated, g_cand),
-            (mixed, jnp.concatenate([g_update, g_reset_pre, g_cand], axis=1)),
-            (normed, g_val),
-        ),
-        jnp.concatenate(small_rows, axis=0),
-        (mixed, g_shared),
-    )
-    narrow_grad, widen_grad, merge_grad, mix_rest, value_grad = wholes
-    mix_grad = jnp.concatenate([mix_rest[:, :width], shared_grad, mix_rest[:, width:]], axis=1)
-
-    block_out = (middle + times(hidden, narrow_full)) * row_valid
+    value_grad, mix_grad, merge_grad, widen_grad, narrow_grad, small_grad = total(
+        jnp.concatenate(small_rows, axis=0)
+    )
 
     return (
         block_out.reshape(tokens.shape),

time: 1050 us -> 767 us (0.73)
  Pallas kernels: 323 us -> 611 us
  waiting for transfers between devices: 202 us -> 6.14 us
  local copies, waits for them, and re-layouts: 236 us -> 81.4 us
  matrix products: 132 us -> 3.16 us
  blocking collectives: 45.6 us -> 12 us
  other arithmetic: 65.4 us -> 32.2 us
  starting transfers between devices: 24.5 us -> 0.08 us
    pallas_call x1 -> x3, Pallas kernels: 308 us -> 595 us  [the longest x1 308 us: reduce_grads(): pl.pallas_call(functools.partial(reduce_body, shapes, tuple((item[3] for...]
    ppermute x45 -> x0, waiting for transfers between devices: 202 us -> none  [swap(): return lax.ppermute(value, 'seq', [(i, i ^ bit) for i in range(count)])]
    dot_general x16 -> x0, matrix products: 130 us -> none  [the longest x5 64.2 us: times_back(): lax.dot_general(left, right, (((1,), (1,)), ((), ())), precision=triple)]
    dynamic_update_slice x50 -> x0, local copies, waits for them, and re-layouts: 68.9 us -> none  [the longest x25 34.9 us: gather_rows(): full = lax.dynamic_update_slice(full, piece[None], (me ^ bit, part, 0, 0))]
    all_gather x1, blocking collectives: 45.6 us -> 12 us  [per_device(): lax.all_gather(jnp.concatenate(packed, axis=0), 'seq').transpose(1, 0, 2)]
    ppermute x45 -> x0, starting transfers between devices: 23.9 us -> none  [swap(): return lax.ppermute(value, 'seq', [(i, i ^ bit) for i in range(count)])]
    reshape x13 -> x12, local copies, waits for them, and re-layouts: 44.8 us -> 20.9 us  [the longest x4 10.5 us: from_places(): value.reshape(2, rows, 4, columns // 4).transpose(1, 2, 0, 3)]
    unnamed x157 -> x124, local copies, waits for them, and re-layouts: 35.3 us -> 12 us
  transfers between devices with their start and end apart: 47 -> 2, of which waited for: 12 -> 1; matrix products, arithmetic and copies ran while one was open for 24% -> 7% of each run, Pallas kernels for 0% -> 1%
where the time goes in v2:
time: 767 us; the launch traced here: 761 us
  Pallas kernels  611 us (80%)
  local copies, waits for them, and re-layouts  81.4 us (11%)
  other arithmetic  32.2 us (4%)
  between operations  15 us (2%)
  blocking collectives  12 us (2%)
    pallas_call x1, Pallas kernels, reduce_grads(): pl.pallas_call(functools.partial(reduce_body, shapes, tuple((item[3] for...  308 us
    pallas_call x1, Pallas kernels, call_forward(): pl.pallas_call(forward_body, out_shape=shapes, in_specs=[anywhere] * len(...  240 us
    pallas_call x1, Pallas kernels, call_backward(): pl.pallas_call(backward_body, out_shape=[jax.ShapeDtypeStruct(shape, jnp....  47.7 us
    pallas_call x5, Pallas kernels, call_kernel(): pl.pallas_call(body, out_shape=[jax.ShapeDtypeStruct(shape, jnp.float32)...  16.1 us
  transfers between devices with their start and end apart: 2, of which 1 were waited for; matrix products, arithmetic and copies ran while one was open for 7% of the time, Pallas kernels for 1%

profile of v2, /device:TPU:0, one launch (start us, length us, event | category | flops | bytes accessed | tf_op | source)
XLA Modules:
  0.0 761.5 jit_solution(9917488371286830034)
XLA Ops:
  7.3 0.9 slice.138
  8.3 0.8 copy.149
  9.1 3.7 concatenate.21
  12.9 12.0 %all-gather.3 = f32[8,196,128]{2,1,0:T(8,128)S(1)} all-gather(f32[1,196,128]{2,1,0:T(8,128)S(1)} %bitcast.235), channel_id=2, replica_groups=mesh['seq'=8,'batch'=4] {'seq'}, dimensions={0}, use_global_device_ids=true | all-gather | bytes 903168 | tf_op jit(solution)/shard_map/all_gather | solution.py:1058
  25.0 0.7 slice_bitcast_fusion.8
  28.1 1.0 fusion.18.signal_ref
  29.1 3.3 shard_map.271
  32.4 1.9 reshape.676
  34.3 1.4 reshape.684
  35.7 1.9 slice.206
  38.3 2.8 reshape.685
  41.1 0.8 copy.159.row_valid
  41.9 2.0 copy.155
  43.8 2.1 reshape.683.shared_w
  47.3 3.0 fusion.12
  50.3 6.1 all-gather.7.cloned.1.call-done
  56.4 1.4 fusion.26.enter_ref
  57.8 1.6 shard_map.272
  60.2 1.5 fusion
  61.7 239.6 %shard_map.273 = (bf16[64,2,512,256]{3,2,1,0:T(8,128)(2,1)}, bf16[64,2,512,256]{3,2,1,0:T(8,128)(2,1)}, f32[8,256,256]{2,1,0:T(8,128)}, f32[8,256,256]{2,1,0:T(8...) custom-call(f32[128,2048]{1,0:T(8,128)} %value_ref.1, ...), custom_call_target="tpu_custom_call" | custom-call | tf_op jit(solution)/shard_map/pallas_call | solution.py:343
  301.3 47.7 %shard_map.274 = (f32[16,256,256]{2,1,0:T(8,128)}, f32[8,256,256]{2,1,0:T(8,128)}, f32[256,128]{1,0:T(8,128)}, f32[2,256,512]{2,1,0:T(8,128)}, f32[2,256,512]{2,...) custom-call(bf16[64,2,512,256]{3,2,1,0:T(8,128)(2,1)} %get-tuple-element.50.w_high, ...), custom_call_target="tpu_custom_call" | custom-call | tf_op jit(solution)/shard_map/pallas_call | solution.py:517
  349.1 1.4 bitcast_bitcast_fusion
  350.5 0.8 copy.166
  351.3 1.0 copy-done.12
  352.3 1.0 multiply_multiply_fusion.signal_ref.grad_ref
  353.3 3.3 shard_map.275
  356.6 1.0 copy-done
  357.6 6.3 shard_map.277
  364.6 3.0 reshape.690
  367.7 1.1 reshape.691
  368.8 2.6 reshape.687
  371.5 3.0 copy.250
  375.3 1.5 multiply_bitcast_fusion
  376.8 2.6 copy.170
  379.5 3.6 multiply_reduce_fusion
  384.2 3.0 copy.154
  387.2 2.6 reshape.695
  389.8 1.8 reshape.688
  391.6 1.9 copy.163
  393.5 1.6 reshape.686
  395.2 1.9 copy.161
  397.1 1.5 reshape_reshape.3
  398.6 3.2 fusion.10
  401.8 1.1 fusion.3
  402.9 1.1 fusion.2
  404.1 1.4 multiply_reduce_fusion.6
  405.7 1.6 shard_map.276
  407.4 7.4 multiply_reduce_fusion.1
  415.6 1.3 copy.176
  416.9 308.0 %shard_map.278 = f32[65,2,64,256]{3,2,1,0:T(8,128)} custom-call(bf16[4,2,256,512]{3,2,1,0:T(8,128)(2,1)} %get-tuple-element.65.refs_0_, bf16[1,2,256,512]{3,2,1,0:T(8,128)(2,1)} %bitcast.232, bf16[2,2,256,512]{3,2,1,0:T(8,128)(2,1)} %get-tuple-element.67.refs_2_, bf16[1,2,256,512]{3,2,1,0:T(8,128)(2,1)} %get-tuple-element.176.refs_3_, ...), custom_call_target="tpu_custom_call" | custom-call | tf_op jit(solution)/shard_map/pallas_call | solution.py:710
  724.9 4.8 fusion.50
  729.9 1.3 slice.224
  731.1 0.8 slice.222
  732.0 0.9 slice.162
  732.9 3.1 fusion.51
  737.1 1.1 reshape.693
  738.2 2.9 copy.181
  741.2 1.8 copy.198
  743.0 1.5 copy.197
  745.2 1.2 copy.196
  746.4 1.1 copy.194
  748.3 1.5 pad_maximum_fusion
  749.8 0.8 copy-done.20
  751.2 3.2 add_multiply_fusion
  (155 shorter events, 12.5 us)
Async XLA Ops:
  7.2 18.9 %copy-start.55 = (s32[2]{0:T(128)S(1)}, s32[2]{0:T(128)}, u32[]{:S(2)}) copy-start(s32[2]{0:T(128)} %param.17) | copy-start | bytes 28
  7.2 19.0 %copy-start.4 = (f32[2,128,1024]{2,1,0:T(8,128)S(1)}, f32[2,128,1024]{2,1,0:T(8,128)}, u32[]{:S(2)}) copy-start(f32[2,128,1024]{2,1,0:T(8,128)} %param.16) | copy-start | bytes 3145732
  7.2 49.2 %all-gather.7.cloned.1.call-start = ((), (), s32[]{:S(2)}) async-start(), calls=%async_computation | async-start | bytes 1179648 | tf_op jit(solution)/shard_map/all_gather | solution.py:819
  25.0 0.9 copy-start.15
  26.1 30.4 %copy-start.28 = (f32[16,8,128]{2,1,0:T(8,128)}, f32[16,8,128]{2,1,0:T(8,128)S(1)}, u32[]{:S(2)}) copy-start(f32[16,8,128]{2,1,0:T(8,128)S(1)} %get-tuple-element.161) | copy-start | bytes 196612
  26.1 30.4 %copy-start.30 = (f32[16,8,128]{2,1,0:T(8,128)}, f32[16,8,128]{2,1,0:T(8,128)S(1)}, u32[]{:S(2)}) copy-start(f32[16,8,128]{2,1,0:T(8,128)S(1)} %get-tuple-element.162) | copy-start | bytes 196612
  26.2 21.1 %copy-start.40 = (f32[256]{0:T(256)}, f32[256]{0:T(256)S(1)}, u32[]{:S(2)}) copy-start(f32[256]{0:T(256)S(1)} %get-tuple-element.203) | copy-start | bytes 3076
  27.9 1.2 copy-start.43
  28.1 1.0 copy-start.7
  32.4 371.6 %all-gather.9.cloned.1.call-start = ((), (), s32[]{:S(2)}) async-start(), calls=%async_computation.1 | async-start | bytes 1179648 | tf_op jit(solution)/shard_map/all_gather | solution.py:819
  38.3 9.0 %copy-start.18 = (f32[256,4,256]{2,1,0:T(4,128)S(1)}, f32[256,4,256]{2,1,0:T(4,128)}, u32[]{:S(2)}) copy-start(f32[256,4,256]{2,1,0:T(4,128)} %reshape.684) | copy-start | bytes 3145732
  56.4 3.1 copy-start.13
  56.4 3.1 copy-start.36
  56.4 3.1 copy-start.38
  56.4 3.1 copy-start.41
  56.4 3.1 copy-start.47
  56.4 3.1 copy-start.49
  349.1 3.2 copy-start.8
  349.1 3.2 copy-start.34
  349.1 3.2 copy-start.44
  351.3 1.0 copy-start.12
  356.6 1.0 copy-start
  364.0 0.6 copy-start.2
  368.8 5.7 copy-start.54
  368.8 6.5 copy-start.5
  368.8 6.5 copy-start.32
  368.8 6.5 copy-start.42
  368.8 6.5 copy-start.48
  368.8 6.4 copy-start.50
  375.3 4.2 copy-start.37
  375.3 4.2 copy-start.39
  376.8 2.6 copy-start.14
  384.2 5.6 copy-start.10
  395.1 3.5 copy-start.31
  398.6 4.3 copy-start.19
  401.8 2.3 copy-start.3
  401.8 2.3 copy-start.29
  402.9 2.6 copy-start.16
  402.9 2.8 copy-start.1
  405.4 1.9 copy-start.9
  405.4 1.9 copy-start.11
  405.4 1.9 copy-start.35
  405.5 1.9 copy-start.45
  407.3 7.5 copy-start.51
  407.3 7.5 copy-start.53
  407.3 7.5 copy-start.52
  407.4 7.5 copy-start.26
  743.0 1.6 copy-start.25
  744.5 1.9 copy-start.24
  745.2 3.0 copy-start.17
  745.2 3.0 copy-start.27
  746.4 3.4 copy-start.23
  748.2 1.6 copy-start.6
  748.2 2.3 copy-start.20
  748.3 2.6 copy-start.21
  748.3 2.9 copy-start.22
  748.3 2.9 copy-start.33
  748.3 2.9 copy-start.46
Sparse Core Ops, SparseCore 0:
  32.5 23.8 all-gather.6
  357.7 22.1 all-gather.8

commit v3 on v2

v3 whole, which is shorter than its diff:
```python
import functools

import jax
import jax.numpy as jnp
from jax import lax
from jax.experimental import pallas as pl
from jax.experimental.pallas import tpu as pltpu
from jax.sharding import PartitionSpec as P

exact = lax.Precision.HIGHEST
triple = lax.Precision.HIGH
norm_eps = 1e-05
masked_score = -1000000000.0
lanes = 128


def gather_rows(shard):
    return lax.all_gather(shard, "seq", axis=0, tiled=True)


def product_grad(left, right):
    return lax.dot_general(left, right, (((0,), (0,)), ((), ())), precision=triple)


def halves(value):
    high = value.astype(jnp.bfloat16)
    return high, (value - high.astype(jnp.float32)).astype(jnp.bfloat16)


def contract(left, right, left_dim, right_dim, precision=None):
    return lax.dot_general(
        left, right, (((left_dim,), (right_dim,)), ((), ())),
        precision=precision, preferred_element_type=jnp.float32,
    )


def turned(left, right):
    return contract(left, right, 0, 0)


def three(left, right, left_dim, right_dim):
    (high, low), (other, rest) = left, right
    return contract(high, other, left_dim, right_dim) + (
        contract(low, other, left_dim, right_dim) + contract(high, rest, left_dim, right_dim)
    )


def place_of(device):
    return (device % 2) * 4 + device // 2


def tree_sum(terms):
    while len(terms) > 1:
        terms = [a + b for a, b in zip(terms[::2], terms[1::2])] + (
            [terms[-1]] if len(terms) % 2 else []
        )
    return terms[0]


def run_filter(reverse, s, decay_ref, weight_ref, signal_ref, out_ref, end_ref):
    length, states = signal_ref.shape[1], decay_ref.shape[0]

    def step(t, held):
        at = length - 1 - t if reverse else t
        entry = signal_ref[s, at]
        held = tuple(decay_ref[n] * held[n] + entry for n in range(states))
        out_ref[s, at] = tree_sum([weight_ref[n] * held[n] for n in range(states)])
        return held

    zero = jnp.zeros(signal_ref.shape[2:], jnp.float32)
    held = lax.fori_loop(0, length, step, (zero,) * states, unroll=4)
    for n in range(states):
        end_ref[s, n] = held[n]


def run_carried(reverse, s, decay_ref, weight_ref, enter_ref, local_ref, out_ref):
    length, states = local_ref.shape[1], decay_ref.shape[0]

    def step(t, held):
        at = length - 1 - t if reverse else t
        held = tuple(decay_ref[n] * held[n] for n in range(states))
        out_ref[s, at] = local_ref[s, at] + tree_sum(list(held))
        return held

    start = tuple(weight_ref[n] * enter_ref[s, n] for n in range(states))
    lax.fori_loop(0, length, step, start, unroll=4)


def run_moments(s, low, high, decay_ref, enter_ref, signal_ref, grad_ref, direct_ref, slope_ref, last_ref):
    length, span = signal_ref.shape[1], range(low, high)
    zero = jnp.zeros(signal_ref.shape[2:], jnp.float32)

    def step(t, carry):
        held, slope, direct, sloped = carry
        entry, grad = signal_ref[s, t], grad_ref[s, t]
        slope = tuple(decay_ref[n] * d + h for n, d, h in zip(span, slope, held))
        held = tuple(decay_ref[n] * h + entry for n, h in zip(span, held))
        direct = tuple(q + grad * h for q, h in zip(direct, held))
        sloped = tuple(q + grad * d for q, d in zip(sloped, slope))
        return held, slope, direct, sloped

    zeros = (zero,) * len(span)
    if s:
        sums = (tuple(direct_ref[n] for n in span), tuple(slope_ref[n] for n in span))
    else:
        sums = (zeros, zeros)
    start = (tuple(enter_ref[s, n] for n in span), zeros) + sums
    _, slope, direct, sloped = lax.fori_loop(0, length, step, start, unroll=2)
    for k, n in enumerate(span):
        last_ref[s, n], direct_ref[n], slope_ref[n] = slope[k], direct[k], sloped[k]


def filter_body(reverse, decay_ref, weight_ref, signal_ref, out_ref, end_ref):
    for s in range(signal_ref.shape[0]):
        run_filter(reverse, s, decay_ref, weight_ref, signal_ref, out_ref, end_ref)


def carried_body(reverse, decay_ref, weight_ref, enter_ref, local_ref, out_ref):
    for s in range(local_ref.shape[0]):
        run_carried(reverse, s, decay_ref, weight_ref, enter_ref, local_ref, out_ref)


def moments_body(decay_ref, enter_ref, signal_ref, grad_ref, *outs):
    states = decay_ref.shape[0]
    for low in range(0, states, 8):
        for s in range(signal_ref.shape[0]):
            run_moments(s, low, min(low + 8, states), decay_ref, enter_ref, signal_ref, grad_ref, *outs)


def run_entering(reverse, s, block_ref, ends_ref, me, enter_ref):
    count = ends_ref.shape[0]
    mine = count - 1 - me if reverse else me

    def one(n, carry):
        total = jnp.zeros(block_ref.shape[1:], jnp.float32)
        for position in range(count - 1):
            piece = ends_ref[count - 1 - position if reverse else position, s, n]
            total = jnp.where(position < mine, block_ref[n] * total + piece, total)
        enter_ref[s, n] = total
        return carry

    lax.fori_loop(0, block_ref.shape[0], one, 0)


def on_other(**coordinate):
    return dict(device_id=coordinate, device_id_type=pl.DeviceIdType.MESH)


def chunk_table(shapes):
    firsts, chunk = [], 0
    for blocks, wide in shapes:
        firsts.append(chunk)
        chunk += blocks * wide
    return firsts, chunk


def to_peers(source, target, sent, came):
    me = lax.axis_index("seq")
    for k in range(1, 8):
        yield pltpu.make_async_remote_copy(
            src_ref=source, dst_ref=target, send_sem=sent.at[k - 1], recv_sem=came.at[k - 1],
            **on_other(seq=(me // 4 + k // 4) % 2 * 4 + (me // 2 + k // 2) % 2 * 2 + (me + k) % 2),
        )


gather_shapes = ((1, 8), (1, 16), (2, 4), (1, 16), (4, 4))


def forward_body(
    value_ref, mix_ref, merge_ref, widen_ref, narrow_ref, packed, tokens, out_grad, row_valid, key_valid,
    w_high, w_low, value_pre, attended, projected, shared_pre, soft, cand_pre, middle, block_out,
    two_h, two_l, gated_h, gated_l, hidden_h, hidden_l, g_wide,
    normed_h, normed_l, mixed_h, mixed_l, masked, g_out, signal, enter, mix_pre, small, shared_w,
    buf, stage_h, stage_l, g_hidden, smoothed, ends, tables, loaded, sent, came, stored, near, sent_all, came_all,
):
    weights = (value_ref, mix_ref, merge_ref, widen_ref, narrow_ref)
    firsts, chunks = chunk_table(gather_shapes)
    depth, delay = buf.shape[0], 2
    width = buf.shape[-1]
    half = lanes * 4
    me, level = lax.axis_index("seq"), lax.axis_index("batch")
    core, along_x, along_y = me % 2, (me // 2) % 2, me // 4
    id_sibling = me + 1 - 2 * core
    id_x, id_y = me + 2 - 4 * along_x, me + 4 - 8 * along_y
    id_corner = id_x + 4 - 8 * along_y
    mine, at_x, at_y, at_corner = (place_of(device) for device in (me, id_x, id_y, id_corner))
    above, below = (level + 1) % 4, (level + 3) % 4
    quarter, eighth = lanes // 4, lanes // 8

    barrier = pltpu.get_barrier_semaphore()
    for other in range(1, 8):
        pl.semaphore_signal(barrier, inc=1, **on_other(seq=(me + other) % 8))
    for target in (above, below):
        pl.semaphore_signal(barrier, inc=1, **on_other(batch=target))
    pl.semaphore_wait(barrier, 9)

    def link(kind, chunk):
        slot = chunk % depth

        def rows(place, start, count):
            return buf.at[slot, place, pl.ds(pl.multiple_of(start, 8), count)]

        piece, target = (
            lambda: (buf.at[slot, mine], {"seq": id_x}),
            lambda: (buf.at[slot, mine], {"seq": id_y}),
            lambda: (buf.at[slot, mine], {"seq": id_sibling}),
            lambda: (rows(at_x, level * quarter, eighth), {"seq": id_y}),
            lambda: (rows(at_y, level * quarter + eighth, eighth), {"seq": id_x}),
            lambda: (buf.at[slot, at_x], {"seq": id_sibling}),
            lambda: (buf.at[slot, at_y], {"seq": id_sibling}),
            lambda: (rows(at_corner, level * quarter, quarter), {"batch": above}),
            lambda: (rows(at_corner, ((level + 3) % 4) * quarter, quarter), {"batch": above}),
            lambda: (rows(at_corner, ((level + 2) % 4) * quarter, quarter), {"batch": above}),
            lambda: (buf.at[slot, at_corner], {"seq": id_sibling}),
        )[kind]()
        return pltpu.make_async_remote_copy(
            src_ref=piece, dst_ref=piece, send_sem=sent.at[kind, slot], recv_sem=came.at[kind, slot],
            **on_other(**target),
        )

    def load(chunk):
        slot = chunk % depth
        for number, ((blocks, wide), first, weight) in enumerate(
            zip(gather_shapes, firsts, weights)
        ):

            @pl.when((chunk >= first) & (chunk < first + blocks * wide))
            def _(number=number, first=first, wide=wide, weight=weight):
                row = ((chunk - first) // wide) * lanes
                column = ((chunk - first) % wide) * width
                if number == 1:
                    column = column + jnp.where(column >= weights[2].shape[1], lanes, 0)
                source = weight.at[
                    pl.ds(pl.multiple_of(row, lanes), lanes),
                    pl.ds(pl.multiple_of(column, lanes), width),
                ]
                pltpu.make_async_copy(source, buf.at[slot, mine], loaded.at[slot]).start()

    def exchange(done, begun):
        def phase(chunk):
            for kind in done:
                link(kind, chunk).wait()
            for kind in begun:
                link(kind, chunk).start()

        return phase

    def send(chunk):
        slot = chunk % depth
        first = value_ref.at[pl.ds(0, lanes), pl.ds(0, width)]
        pltpu.make_async_copy(first, buf.at[slot, mine], loaded.at[slot]).wait()
        for kind in (0, 1, 2):
            link(kind, chunk).start()

    def store(chunk, kind):
        return pltpu.make_async_copy(
            (stage_h, stage_l)[kind].at[chunk % 2],
            (w_high, w_low)[kind].at[chunk],
            stored.at[kind, chunk % 2],
        )

    def product(left_h, left_l, right):
        return three((left_h[0], left_l[0]), (right[0][0], right[1][0]), 1, 0) + three(
            (left_h[1], left_l[1]), (right[0][1], right[1][1]), 1, 0
        )

    sequences, block_len = soft.shape[:2]
    states = tables.shape[1]
    decay, weight, block_decay = (tables.at[kind] for kind in range(3))
    features = tokens.shape[1]
    tiles = features // width

    def share(kind):
        if kind == 0:
            source = target = small.at[me]
        elif kind == 1:
            source = mix_ref.at[:, pl.ds(features, lanes)]
            target = shared_w.at[mine]
        else:
            source = target = ends.at[me]
        return list(to_peers(source, target, sent_all.at[kind], came_all.at[kind]))

    def own_shared():
        return pltpu.make_async_copy(mix_ref.at[:, pl.ds(features, lanes)], shared_w.at[mine], near)

    def row_of(number, k):
        return jnp.concatenate(
            [small[2 * k, number : number + 1], small[2 * k + 1, number : number + 1]], axis=1
        )

    def hand_out():
        small[me] = packed[...]
        for kind in (0, 1):
            for item in share(kind):
                item.start()
        own_shared().start()

    def norm_one():
        for kind in (0, 1):
            for item in share(kind):
                item.wait()
        own_shared().wait()
        for kind in range(3):
            for n in range(states):
                tables[kind, n] = small[:, kind * states + n]
        keep = row_valid[...]
        value = tokens[...] * keep
        centre = jnp.mean(value, axis=1, keepdims=True)
        shifted = value - centre
        scale = lax.rsqrt(jnp.mean(shifted * shifted, axis=1, keepdims=True) + norm_eps)
        gain = jnp.concatenate([row_of(3 * states, k) for k in range(tiles)], axis=1)
        normed = shifted * scale * gain
        for k in range(tiles):
            span = slice(k * width, (k + 1) * width)
            masked[k] = value[:, span]
            g_out[k] = out_grad[:, span] * keep
            for parity in range(2):
                start = k * width + parity * lanes
                put(normed_h, normed_l, (parity,), k * lanes, normed[:, start : start + lanes])
        for s in range(sequences):
            rows = normed[s * block_len : (s + 1) * block_len]
            signal[s] = rows.reshape(signal.shape[1:])

    def filter_one(s):
        run_filter(False, s, decay, weight, signal, smoothed, ends.at[me])
        if s == sequences - 1:
            for item in share(2):
                item.start()

    def carry_one(s):
        if s == 0:
            for item in share(2):
                item.wait()
        run_entering(False, s, block_decay, ends, me, enter)
        run_carried(False, s, decay, weight, enter, smoothed, smoothed)

    def mix_in():
        for s in range(sequences):
            span = slice(s * block_len, (s + 1) * block_len)
            skip = jnp.concatenate([row_of(3 * states + 1, k) for k in range(tiles)], axis=1)
            normed = signal[s].reshape(block_len, features)
            value = smoothed[s].reshape(block_len, features) + skip * normed
            mixed = value * jax.nn.sigmoid(value)
            for block in range(8):
                cut = slice(block * lanes, (block + 1) * lanes)
                to = (block % 2, span, slice(block // 2 * lanes, (block // 2 + 1) * lanes))
                mix_pre[to] = value[:, cut]
                mixed_h[to], mixed_l[to] = halves(mixed[:, cut])

    def attention():
        shared_full = halves(shared_w[...].reshape(2, half, lanes))
        total = product(mixed_h, mixed_l, shared_full)
        affine = tree_sum([small[k, 3 * states + 3 : 3 * states + 6] for k in range(8)])
        shared_pre[...] = total
        shared = total * jax.nn.sigmoid(total)
        queries = shared * affine[0:1] + affine[2:3]
        keys = shared * affine[1:2]
        for s in range(sequences):
            span = slice(s * block_len, (s + 1) * block_len)
            scores = contract(queries[span], keys[span], 1, 1, exact) * shared.shape[1] ** (-0.5)
            scores = jnp.where(key_valid[s] > 0.5, scores, masked_score)
            weight = jnp.exp(scores - jnp.max(scores, axis=1, keepdims=True))
            soft[s] = weight / jnp.sum(weight, axis=1, keepdims=True)

    def put(target_h, target_l, index, column, value):
        high, low = halves(value)
        target_h[(*index, slice(None), pl.ds(pl.multiple_of(column, lanes), lanes))] = high
        target_l[(*index, slice(None), pl.ds(pl.multiple_of(column, lanes), lanes))] = low

    def complete(chunk):
        slot = chunk % depth
        link(10, chunk).wait()

        @pl.when(chunk >= 2)
        def _():
            store(chunk - 2, 0).wait()
            store(chunk - 2, 1).wait()

        right = halves(buf[slot].reshape(2, half, width))
        stage_h[chunk % 2] = right[0]
        stage_l[chunk % 2] = right[1]
        store(chunk, 0).start()
        store(chunk, 1).start()

        def among(number):
            blocks, wide = gather_shapes[number]
            return (chunk >= firsts[number]) & (chunk < firsts[number] + blocks * wide)

        @pl.when(among(0))
        def _():
            total = product(normed_h, normed_l, right)
            value_pre[chunk] = total
            values = total * jax.nn.sigmoid(total)
            for s in range(sequences):
                span = slice(s * block_len, (s + 1) * block_len)
                attended[chunk, span] = contract(soft[s], values[span], 1, 0, exact)

        @pl.when(among(1))
        def _():
            tile = chunk - firsts[1]
            total = product(mixed_h, mixed_l, right)
            projected[tile] = total

            @pl.when((tile >= 4) & (tile < 12))
            def _():
                block = tile - 4
                gated = attended[block] * total * jax.nn.sigmoid(total)
                for j in range(2):
                    cut = gated[:, j * lanes : (j + 1) * lanes]
                    put(gated_h, gated_l, (j, block % 2), (block // 2) * lanes, cut)

        @pl.when(among(2))
        def _():
            j, tile = (chunk - firsts[2]) // 4, (chunk - firsts[2]) % 4
            total = product(gated_h.at[j], gated_l.at[j], right)

            @pl.when(j == 0)
            def _():
                cand_pre[tile] = projected[12 + tile] + total

            @pl.when(j == 1)
            def _():
                cand_pre[tile] = cand_pre[tile] + total

            @pl.when(chunk == firsts[3] - 1)
            def _():
                total = 0.0
                for k in range(tiles):
                    cand = cand_pre[k]
                    cand = cand * jax.nn.sigmoid(cand)
                    value = masked[k] + jax.nn.sigmoid(projected[k]) * (cand - masked[k])
                    middle[k] = value
                    total = total + jnp.sum(value, axis=1, keepdims=True)
                centre = total / features
                total = 0.0
                for k in range(tiles):
                    shifted = middle[k] - centre
                    total = total + jnp.sum(shifted * shifted, axis=1, keepdims=True)
                scale = lax.rsqrt(total / features + norm_eps)
                for k in range(tiles):
                    value = (middle[k] - centre) * scale * row_of(3 * states + 2, k)
                    for parity in range(2):
                        cut = value[:, parity * lanes : (parity + 1) * lanes]
                        put(two_h, two_l, (parity,), k * lanes, cut)
                block_out[...] = jnp.zeros(block_out.shape, jnp.float32)
                g_hidden[...] = jnp.zeros(g_hidden.shape, jnp.float32)

        @pl.when(among(3))
        def _():
            tile = chunk - firsts[3]
            total = product(two_h, two_l, right)
            g_wide[tile] = total
            hidden = total * jax.nn.sigmoid(total)
            for i in range(2):
                cut = hidden[:, i * lanes : (i + 1) * lanes]
                index = (2 * (tile % 2) + i, (tile // 2) % 2)
                put(hidden_h, hidden_l, index, (tile // 4) * lanes, cut)

        @pl.when(among(4))
        def _():
            j, tile = (chunk - firsts[4]) // 4, (chunk - firsts[4]) % 4
            to = (slice(None), pl.ds(pl.multiple_of(tile * width, width), width))
            block_out[to] = block_out[to] + product(hidden_h.at[j], hidden_l.at[j], right)
            grad = halves(g_out[tile])
            for parity in range(2):
                back = three(grad, (right[0][parity], right[1][parity]), 1, 1)
                g_hidden[j, parity] = g_hidden[j, parity] + back

    phases = (
        (0, load),
        (1, send),
        (1 + delay, exchange((0, 1, 2), (3, 4, 5, 6))),
        (1 + 2 * delay, exchange((3, 4, 5, 6), (7,))),
        (1 + 3 * delay, exchange((7,), (8,))),
        (1 + 4 * delay, exchange((8,), (9,))),
        (1 + 5 * delay, exchange((9,), (10,))),
        (1 + 6 * delay, complete),
    )

    def step(at, carry):
        for after, phase in phases[-2:0:-1]:

            @pl.when((at >= after) & (at < after + chunks))
            def _(after=after, phase=phase):
                phase(at - after)

        pl.when(at < chunks)(lambda: load(at))
        pl.when(at == 0)(hand_out)
        pl.when(at == 1)(norm_one)
        for s in range(sequences):
            pl.when(at == 2 + s)(functools.partial(filter_one, s))
            pl.when(at == 5 + s)(functools.partial(carry_one, s))
        pl.when(at == 8)(mix_in)
        pl.when(at == 9)(attention)

        @pl.when(at >= phases[-1][0])
        def _():
            complete(at - phases[-1][0])

        return carry

    lax.fori_loop(0, chunks + phases[-1][0], step, 0)
    for chunk in (chunks - 2, chunks - 1):
        for kind in range(2):
            store(chunk, kind).wait()
    for k in range(tiles):
        span = slice(k * width, (k + 1) * width)
        block_out[:, span] = (middle[k] + block_out[:, span]) * row_valid[...]
    for k in range(g_wide.shape[0]):
        for i in range(2):
            span = slice(i * lanes, (i + 1) * lanes)
            back = g_hidden[2 * (k % 2) + i, (k // 2) % 2, :, (k // 4) * lanes : (k // 4 + 1) * lanes]
            wide = g_wide[k, :, span]
            g_wide[k, :, span] = back * silu_slope(wide)


def f32(*shape):
    return jax.ShapeDtypeStruct(shape, jnp.float32)


def b16(*shape):
    return jax.ShapeDtypeStruct(shape, jnp.bfloat16)


def call_forward(weights, packed, tokens, out_grad, row_valid, key_valid, states):
    width, half = 2 * lanes, 4 * lanes
    rows, features = tokens.shape
    sequences = key_valid.shape[0]
    block_len = rows // sequences
    _, chunks = chunk_table(gather_shapes)
    vmem, anywhere = pl.BlockSpec(memory_space=pltpu.VMEM), pl.BlockSpec(memory_space=pl.ANY)
    line = (sequences, block_len, 8, lanes)
    shapes = [b16(chunks, 2, half, width)] * 2 + [
        f32(8, rows, width), f32(8, rows, width), f32(16, rows, width), f32(rows, lanes),
        f32(sequences, block_len, block_len), f32(4, rows, width), f32(4, rows, width), f32(rows, features),
        b16(2, rows, half), b16(2, rows, half), b16(2, 2, rows, half), b16(2, 2, rows, half),
        b16(4, 2, rows, half), b16(4, 2, rows, half), f32(16, rows, width),
        b16(2, rows, half), b16(2, rows, half), b16(2, rows, half), b16(2, rows, half),
        f32(4, rows, width), f32(4, rows, width), f32(*line), f32(sequences, states, 8, lanes),
        f32(2, rows, half), f32(8, *packed.shape), f32(8, lanes, lanes),
    ]
    depth = 16
    return pl.pallas_call(
        forward_body,
        out_shape=shapes,
        in_specs=[anywhere] * len(weights) + [vmem] * 5,
        out_specs=[anywhere] * 2 + [vmem] * (len(shapes) - 2),
        scratch_shapes=[
            pltpu.VMEM((depth, 8, lanes, width), jnp.float32),
            pltpu.VMEM((2, 2, half, width), jnp.bfloat16),
            pltpu.VMEM((2, 2, half, width), jnp.bfloat16),
            pltpu.VMEM((4, 2, rows, half), jnp.float32),
            pltpu.VMEM(line, jnp.float32),
            pltpu.VMEM((8, sequences, states, 8, lanes), jnp.float32),
            pltpu.VMEM((3, states, 8, lanes), jnp.float32),
            pltpu.SemaphoreType.DMA((depth,)),
            pltpu.SemaphoreType.DMA((11, depth)),
            pltpu.SemaphoreType.DMA((11, depth)),
            pltpu.SemaphoreType.DMA((2, 2)),
            pltpu.SemaphoreType.DMA,
            pltpu.SemaphoreType.DMA((3, 7)),
            pltpu.SemaphoreType.DMA((3, 7)),
        ],
        compiler_params=pltpu.CompilerParams(
            collective_id=2, has_side_effects=True, vmem_limit_bytes=62 * 1024 * 1024
        ),
    )(*weights, packed, tokens, out_grad, row_valid, key_valid)


reduce_shapes = ((4, 4), (1, 16), (2, 4), (1, 16), (1, 8))


def backward_body(
    w_high, w_low, value_src, projected_src, middle_src, g_wide, attended, shared_pre, soft, cand_pre,
    two_h, two_l, gated_h, gated_l, hidden_h, hidden_l, normed_h, normed_l, mixed_h, mixed_l,
    masked, g_out, signal, enter, mix_pre, small, shared_w, row_valid, key_valid,
    tokens_grad, narrow_grad, widen_grad, merge_grad, mix_grad, value_grad, small_grad,
    away, keep, got, got_x, got_y, got_xy, got_yx, part, from_edge, from_inner, done,
    value_pre, projected, middle, buf_h, buf_l, g_two, g_gated, g_mixed, g_normed, g_soft, g_shared,
    smooth, back, ends, back_enter, tables, direct, slope, last, small_sum,
    fetched, read, sent, came, written, sent_all, came_all,
):
    lefts = (
        (hidden_h, hidden_l), (two_h, two_l), (gated_h, gated_l), (mixed_h, mixed_l), (normed_h, normed_l)
    )
    rights = ((g_out, 0), (g_wide, 0), (projected, 12), (projected, 0), (value_pre, 0))
    grads = (narrow_grad, widen_grad, merge_grad, mix_grad, value_grad)
    firsts, chunks = chunk_table(reduce_shapes)
    gathered, _ = chunk_table(gather_shapes)
    delay = 2
    tiles, rows, width = masked.shape
    half, features = 4 * lanes, tiles * width
    sequences, block_len = soft.shape[:2]
    states = tables.shape[1]
    decay, weight, block_decay = (tables.at[kind] for kind in range(3))
    me, level = lax.axis_index("seq"), lax.axis_index("batch")
    core, along_x, along_y = me % 2, (me // 2) % 2, me // 4
    is_edge = (level == 0) | (level == 3)
    partner = jnp.where(level < 2, 1 - level, 5 - level)
    sibling, across_x, across_y = (
        {"seq": me + bit * (1 - 2 * own)} for bit, own in ((1, core), (2, along_x), (4, along_y))
    )

    copies_in = [
        pltpu.make_async_copy(source, target, read.at[number])
        for number, (source, target) in enumerate(
            ((middle_src, middle), (projected_src, projected), (value_src, value_pre))
        )
    ]
    for item in copies_in:
        item.start()

    barrier = pltpu.get_barrier_semaphore()
    for other in range(1, 8):
        pl.semaphore_signal(barrier, inc=1, **on_other(seq=(me + other) % 8))
    pl.semaphore_signal(barrier, inc=1, **on_other(batch=partner))

    @pl.when(jnp.logical_not(is_edge))
    def _():
        pl.semaphore_signal(barrier, inc=1, **on_other(batch=3 - level))
        pl.semaphore_wait(barrier, 9)

    @pl.when(is_edge)
    def _():
        pl.semaphore_wait(barrier, 8)

    def slot_in(ref, chunk):
        return chunk % ref.shape[0]

    def link(kind, chunk):
        def at(ref, *index):
            return ref.at[(slot_in(ref, chunk), *index)]

        source, target, device = (
            lambda: (at(away), at(got), sibling),
            lambda: (at(keep, slice(None), 1 - along_x, 0), at(got_x), across_x),
            lambda: (at(keep, 1 - along_y, slice(None), 1), at(got_y), across_y),
            lambda: (at(got_x, 1 - along_y), at(got_xy), across_y),
            lambda: (at(got_y, 1 - along_x), at(got_yx), across_x),
            lambda: (at(part), at(from_edge), {"batch": partner}),
            lambda: (at(part), at(from_inner), {"batch": 3 - level}),
        )[kind]()
        slot = chunk % sent.shape[1]
        return pltpu.make_async_remote_copy(
            src_ref=source, dst_ref=target, send_sem=sent.at[kind, slot], recv_sem=came.at[kind, slot],
            **on_other(**device),
        )

    def results(chunk, call):
        slot, at = slot_in(done, chunk), chunk % sent.shape[1]

        def pieces(number, source, target):
            yield lambda: pltpu.make_async_copy(source, target, written.at[number, at])
            yield lambda: pltpu.make_async_remote_copy(
                src_ref=source, dst_ref=target,
                send_sem=sent.at[7 + number, at], recv_sem=came.at[7 + number, at],
                **on_other(batch=partner),
            )

        for number, ((blocks, wide), first, grad) in enumerate(zip(reduce_shapes, firsts, grads)):

            @pl.when((chunk >= first) & (chunk < first + blocks * wide))
            def _(number=number, first=first, wide=wide, grad=grad):
                row = ((chunk - first) // wide) * lanes
                column = ((chunk - first) % wide) * width
                if number == 3:
                    column = column + jnp.where(column >= features, lanes, 0)
                target = grad.at[
                    pl.ds(pl.multiple_of(row, lanes), lanes),
                    pl.ds(pl.multiple_of(column, lanes), width),
                ]
                call(*pieces(0, done.at[slot], target))

        @pl.when(chunk == chunks)
        def _():
            target = mix_grad.at[:, pl.ds(features, lanes)]
            call(*pieces(0, done.at[slot, :, pl.ds(0, lanes)], target))
            call(*pieces(1, done.at[slot, :, pl.ds(lanes, lanes)], small_grad))

    def begin(chunk):
        slot, to = slot_in(away, chunk), slot_in(keep, chunk)
        for (blocks, wide), first, (high, low), (right, shift) in zip(
            reduce_shapes, firsts, lefts, rights
        ):

            @pl.when((chunk >= first) & (chunk < first + blocks * wide))
            def _(first=first, wide=wide, shift=shift, high=high, low=low, right=right):
                block = (chunk - first) // wide
                other, rest = halves(right[shift + (chunk - first) % wide])

                def product(parity):
                    top, under = (
                        (high[block, parity], low[block, parity])
                        if len(high.shape) == 4
                        else (high[parity], low[parity])
                    )
                    total = turned(top, other) + (turned(under, other) + turned(top, rest))
                    return total.reshape(away.shape[1:])

                away[slot] = product(1 - core)
                link(0, chunk).start()
                keep[to] = product(core)

        @pl.when(chunk == chunks)
        def _():
            right = halves(g_shared[...])

            def fill(ref, at, parity):
                total = three((mixed_h[parity], mixed_l[parity]), right, 0, 0)
                total = total.reshape(*away.shape[1:-1], lanes)
                sums = [small_sum[2 * q + parity].reshape(2, -1, lanes) for q in range(4)]
                sums = jnp.stack(sums, axis=0).reshape(total.shape)
                ref[at] = jnp.concatenate([total, sums], axis=-1)

            fill(away, slot, 1 - core)
            link(0, chunk).start()
            fill(keep, to, core)

    def with_sibling(chunk):
        slot = slot_in(keep, chunk)
        link(0, chunk).wait()
        keep[slot] = keep[slot] + got[slot_in(got, chunk)]
        link(1, chunk).start()
        link(2, chunk).start()

    def with_neighbour(chunk):
        slot = slot_in(got_x, chunk)
        link(1, chunk).wait()
        link(2, chunk).wait()
        from_slot = slot_in(keep, chunk)
        got_x[slot] = got_x[slot] + keep[from_slot, :, along_x, 0]
        got_y[slot] = got_y[slot] + keep[from_slot, along_y, :, 1]
        link(3, chunk).start()
        link(4, chunk).start()

    def with_corner(chunk):
        slot = slot_in(part, chunk)
        link(3, chunk).wait()
        link(4, chunk).wait()
        part[slot, 0] = got_x[slot, along_y] + got_xy[slot]
        part[slot, 1] = got_y[slot, along_x] + got_yx[slot]
        pl.when(is_edge)(lambda: link(5, chunk).start())

    def inner_sum(chunk):
        slot = slot_in(part, chunk)
        pl.when(is_edge)(lambda: link(5, chunk).wait_send())

        @pl.when(jnp.logical_not(is_edge))
        def _():
            link(5, chunk).wait_recv()
            part[slot] = part[slot] + from_edge[slot]
            link(6, chunk).start()

    def total_sum(chunk):
        slot = slot_in(part, chunk)

        @pl.when(jnp.logical_not(is_edge))
        def _():
            link(6, chunk).wait()
            done[slot] = (part[slot] + from_inner[slot]).reshape(done.shape[1:])

            def start(stay, go):
                stay().start()
                go().start()

            results(chunk, start)

    def finish(chunk):
        def receive(stay, go):
            go().wait_recv()

        def release(stay, go):
            stay().wait()
            go().wait_send()

        pl.when(is_edge)(lambda: results(chunk, receive))
        pl.when(jnp.logical_not(is_edge))(lambda: results(chunk, release))

    steps = 48

    def fetch(step, call):
        chunk = jnp.where(
            step < 16, gathered[3] + step, jnp.where(step < 24, step + 8, jnp.where(step < 40, step - 16, step - 40))
        )
        slot = slot_in(buf_h, step)
        for kind, (source, target) in enumerate(((w_high, buf_h), (w_low, buf_l))):
            item = pltpu.make_async_copy(source.at[chunk], target.at[slot], fetched.at[kind, slot])
            getattr(item, call)()

    def back_product(grad, step, parity):
        slot = slot_in(buf_h, step)
        return three(halves(grad), (buf_h[slot, parity], buf_l[slot, parity]), 1, 1)

    def row_of(number, k):
        return jnp.concatenate(
            [small[2 * k, number : number + 1], small[2 * k + 1, number : number + 1]], axis=1
        )

    def put_row(number, k, value):
        for i in range(2):
            small_sum[2 * k + i, number : number + 1] = value[:, i * lanes : (i + 1) * lanes]

    def statistics(ref):
        total = 0.0
        for k in range(tiles):
            total = total + jnp.sum(ref[k], axis=1, keepdims=True)
        centre = total / features
        total = 0.0
        for k in range(tiles):
            shifted = ref[k] - centre
            total = total + jnp.sum(shifted * shifted, axis=1, keepdims=True)
        return centre, lax.rsqrt(total / features + norm_eps)

    def norm_two_back():
        for item in copies_in:
            item.wait()
        centre, scale = statistics(middle)

        def grad_of(k):
            span = slice(k * lanes, (k + 1) * lanes)
            return jnp.concatenate([g_two[0, :, span], g_two[1, :, span]], axis=1)

        plain, crossed = 0.0, 0.0
        for k in range(tiles):
            grad, hat = grad_of(k), (middle[k] - centre) * scale
            put_row(2 * states + 2, k, jnp.sum(grad * hat, axis=0, keepdims=True))
            inner = grad * row_of(3 * states + 2, k)
            plain = plain + jnp.sum(inner, axis=1, keepdims=True)
            crossed = crossed + jnp.sum(inner * hat, axis=1, keepdims=True)
        plain, crossed = plain / features, crossed / features
        for k in range(tiles):
            inner, hat = grad_of(k) * row_of(3 * states + 2, k), (middle[k] - centre) * scale
            g_middle = g_out[k] + (inner - plain - hat * crossed) * scale
            update = jax.nn.sigmoid(projected[k])
            pre = cand_pre[k]
            gate = jax.nn.sigmoid(pre)
            middle[k] = g_middle * (1.0 - update)
            projected[k] = g_middle * (pre * gate - masked[k]) * update * (1.0 - update)
            projected[12 + k] = g_middle * update * (gate * (1.0 + pre * (1.0 - gate)))

    def attention_back(m):
        parity, start = m % 2, pl.multiple_of((m // 2) * lanes, lanes)
        grad = jnp.concatenate(
            [g_gated[0, parity, :, pl.ds(start, lanes)], g_gated[1, parity, :, pl.ds(start, lanes)]], axis=1
        )
        pre = projected[4 + m]
        gate = jax.nn.sigmoid(pre)
        g_attended = grad * pre * gate
        projected[4 + m] = grad * attended[m] * (gate * (1.0 + pre * (1.0 - gate)))
        pre = value_pre[m]
        gate = jax.nn.sigmoid(pre)
        values, bend = pre * gate, gate * (1.0 + pre * (1.0 - gate))
        g_values = []
        for s in range(sequences):
            span = slice(s * block_len, (s + 1) * block_len)
            own = halves(g_attended[span])
            g_soft[s] = g_soft[s] + three(own, halves(values[span]), 1, 1)
            g_values.append(three(halves(soft[s]), own, 0, 0) * bend[span])
        value_pre[m] = jnp.concatenate(g_values, axis=0)

    def scores_back():
        affine = tree_sum([small[k, 3 * states + 3 : 3 * states + 6] for k in range(8)])
        pre = shared_pre[...]
        gate = jax.nn.sigmoid(pre)
        shared, bend = pre * gate, gate * (1.0 + pre * (1.0 - gate))
        score_scale = shared.shape[1] ** (-0.5)
        queries = shared * affine[0:1] + affine[2:3]
        keys = shared * affine[1:2]
        sums = [0.0, 0.0, 0.0]
        for s in range(sequences):
            span = slice(s * block_len, (s + 1) * block_len)
            soft_weight, grad = soft[s], g_soft[s]
            g_scores = soft_weight * (grad - jnp.sum(grad * soft_weight, axis=1, keepdims=True))
            g_scores = jnp.where(key_valid[s] > 0.5, g_scores, 0.0) * score_scale
            g_queries = contract(g_scores, keys[span], 1, 0, exact)
            g_keys = contract(g_scores, queries[span], 0, 0, exact)
            g_shared[span] = (g_queries * affine[0:1] + g_keys * affine[1:2]) * bend[span]
            terms = (g_queries * shared[span], g_keys * shared[span], g_queries)
            for number, term in enumerate(terms):
                sums[number] = sums[number] + jnp.sum(term, axis=0, keepdims=True)
        for number in range(3):
            for k in range(8):
                row = 2 * states + 3 + number
                small_sum[k, row : row + 1] = sums[number]
        own, full = halves(g_shared[...]), halves(shared_w[...].reshape(2, half, lanes))
        for parity in range(2):
            g_mixed[parity] = three(own, (full[0][parity], full[1][parity]), 1, 1)

    def smooth_back():
        for kind in range(3):
            for n in range(states):
                tables[kind, n] = small[:, kind * states + n]
        for parity in range(2):
            pre = mix_pre[parity]
            g_mixed[parity] = g_mixed[parity] * silu_slope(pre)
        for s in range(sequences):
            span = slice(s * block_len, (s + 1) * block_len)
            blocks = [
                g_mixed[block % 2, span, block // 2 * lanes : (block // 2 + 1) * lanes]
                for block in range(8)
            ]
            smooth[s] = jnp.concatenate(blocks, axis=1).reshape(smooth.shape[1:])

    def share():
        return list(to_peers(ends.at[me], ends.at[me], sent_all, came_all))

    def filter_one(s):
        run_filter(True, s, decay, weight, smooth, back, ends.at[me])
        if s == sequences - 1:
            for item in share():
                item.start()

    def moments_one(s, low):
        run_moments(s, low, low + 8, decay, enter, signal, smooth, direct, slope, last)

    def carry_one(s):
        if s == 0:
            for item in share():
                item.wait()
        run_entering(True, s, block_decay, ends, me, back_enter)
        run_carried(True, s, decay, weight, back_enter, back, back)

    def norm_one_back():
        for n in range(states):
            total = slope[n]
            for s in range(sequences):
                total = total + decay[n] * back_enter[s, n] * last[s, n]
            small_sum[:, n] = direct[n]
            small_sum[:, states + n] = total
        centre, scale = statistics(masked)
        line = [back[s].reshape(block_len, features) for s in range(sequences)]
        line = jnp.concatenate(line, axis=0)

        def blocks(ref, k):
            span = slice(k * lanes, (k + 1) * lanes)
            return jnp.concatenate([ref[0, :, span], ref[1, :, span]], axis=1)

        plain, crossed = 0.0, 0.0
        for k in range(tiles):
            g_smooth, hat = blocks(g_mixed, k), (masked[k] - centre) * scale
            gain = row_of(3 * states, k)
            grad = blocks(g_normed, k) + g_smooth * row_of(3 * states + 1, k)
            grad = grad + line[:, k * width : (k + 1) * width]
            put_row(2 * states, k, jnp.sum(grad * hat, axis=0, keepdims=True))
            put_row(2 * states + 1, k, jnp.sum(g_smooth * (hat * gain), axis=0, keepdims=True))
            inner = grad * gain
            plain = plain + jnp.sum(inner, axis=1, keepdims=True)
            crossed = crossed + jnp.sum(inner * hat, axis=1, keepdims=True)
            tokens_grad[:, k * width : (k + 1) * width] = inner
        plain, crossed = plain / features, crossed / features
        for k in range(tiles):
            span = slice(k * width, (k + 1) * width)
            hat = (masked[k] - centre) * scale
            g_x = (tokens_grad[:, span] - plain - hat * crossed) * scale
            tokens_grad[:, span] = (middle[k] + g_x) * row_valid[...]

    g_two[...] = jnp.zeros(g_two.shape, jnp.float32)
    g_gated[...] = jnp.zeros(g_gated.shape, jnp.float32)
    g_normed[...] = jnp.zeros(g_normed.shape, jnp.float32)
    g_soft[...] = jnp.zeros(g_soft.shape, jnp.float32)
    small_sum[...] = jnp.zeros(small_sum.shape, jnp.float32)

    def work(at):
        @pl.when((at < 24) | ((at >= 32) & (at < 56)))
        def _():
            step = jnp.where(at < 24, at, at - 8)
            pl.when(step + 2 < steps)(lambda: fetch(step + 2, "start"))
            fetch(step, "wait")

            @pl.when(at < 16)
            def _():
                for parity in range(2):
                    g_two[parity] = g_two[parity] + back_product(g_wide[at], step, parity)

            pl.when(at == 16)(norm_two_back)

            @pl.when((at >= 16) & (at < 24))
            def _():
                j = (at - 16) // 4
                for parity in range(2):
                    more = back_product(projected[12 + at % 4], step, parity)
                    g_gated[j, parity] = g_gated[j, parity] + more

            pl.when(at == 32)(scores_back)

            @pl.when((at >= 32) & (at < 48))
            def _():
                for parity in range(2):
                    more = back_product(projected[at - 32], step, parity)
                    g_mixed[parity] = g_mixed[parity] + more

            @pl.when(at >= 48)
            def _():
                for parity in range(2):
                    more = back_product(value_pre[at - 48], step, parity)
                    g_normed[parity] = g_normed[parity] + more

        pl.when((at >= 24) & (at < 32))(lambda: attention_back(at - 24))
        pl.when(at == 48)(smooth_back)
        for s in range(sequences):
            pl.when(at == 49 + s)(functools.partial(filter_one, s))
            for low in range(0, states, 8):
                number = 51 + s * (states // 8) + low // 8
                pl.when(at == number)(functools.partial(moments_one, s, low))
            pl.when(at == 56 + s)(functools.partial(carry_one, s))
        pl.when(at == 59)(norm_one_back)

    phases = (begin, with_sibling, with_neighbour, with_corner, inner_sum, total_sum, finish)
    fetch(0, "start")
    fetch(1, "start")

    def step(at, carry):
        for number in range(len(phases) - 1, -1, -1):
            chunk = at - number * delay

            @pl.when((chunk >= 0) & (chunk <= chunks))
            def _(number=number, chunk=chunk):
                phases[number](chunk)

        work(at)
        return carry

    lax.fori_loop(0, chunks + 1 + (len(phases) - 1) * delay, step, 0)


def call_backward(operands, grad_shapes):
    g_wide, soft = operands[5], operands[8]
    signal, enter, small = operands[22], operands[23], operands[25]
    _, rows, width = g_wide.shape
    sequences, block_len = soft.shape[:2]
    states = enter.shape[1]
    half, piece, depth = 4 * lanes, lanes // 2, 8
    vmem, anywhere = pl.BlockSpec(memory_space=pltpu.VMEM), pl.BlockSpec(memory_space=pl.ANY)
    shapes = [f32(rows, 8 * lanes)] + [f32(*shape) for shape in grad_shapes] + [f32(lanes, lanes)]
    held = [
        (4, 2, 2, 2, piece, width), (6, 2, 2, 2, piece, width), (4, 2, 2, 2, piece, width),
        (depth, 2, piece, width), (depth, 2, piece, width), (depth, piece, width), (depth, piece, width),
        (depth, 2, piece, width), (depth, 2, piece, width), (depth, 2, piece, width), (depth, lanes, width),
        (8, rows, width), (16, rows, width), (4, rows, width),
    ]
    more = [
        (2, rows, half), (2, 2, rows, half), (2, rows, half), (2, rows, half), soft.shape, (rows, lanes),
        signal.shape, signal.shape, (8, *enter.shape), enter.shape, (3, states, 8, lanes),
        (states, 8, lanes), (states, 8, lanes), enter.shape, (8, lanes, lanes),
    ]
    return pl.pallas_call(
        backward_body,
        out_shape=shapes,
        in_specs=[anywhere] * 5 + [vmem] * (len(operands) - 5),
        out_specs=[vmem] + [anywhere] * (len(shapes) - 1),
        scratch_shapes=[pltpu.VMEM(shape, jnp.float32) for shape in held]
        + [pltpu.VMEM((3, 2, half, width), jnp.bfloat16)] * 2
        + [pltpu.VMEM(shape, jnp.float32) for shape in more]
        + [
            pltpu.SemaphoreType.DMA((2, 3)),
            pltpu.SemaphoreType.DMA((3,)),
            pltpu.SemaphoreType.DMA((9, depth)),
            pltpu.SemaphoreType.DMA((9, depth)),
            pltpu.SemaphoreType.DMA((2, depth)),
            pltpu.SemaphoreType.DMA((7,)),
            pltpu.SemaphoreType.DMA((7,)),
        ],
        compiler_params=pltpu.CompilerParams(
            collective_id=1, has_side_effects=True, vmem_limit_bytes=62 * 1024 * 1024
        ),
    )(*operands)


def call_kernel(body, shapes, *operands):
    return pl.pallas_call(
        body,
        out_shape=[jax.ShapeDtypeStruct(shape, jnp.float32) for shape in shapes],
        in_specs=[pl.BlockSpec(memory_space=pltpu.VMEM)] * len(operands),
        out_specs=[pl.BlockSpec(memory_space=pltpu.VMEM)] * len(shapes),
        compiler_params=pltpu.CompilerParams(vmem_limit_bytes=32 * 1024 * 1024),
    )(*operands)


def entering(ends, block_decay, backward):
    count, mine = lax.axis_size("seq"), lax.axis_index("seq")
    pieces = lax.all_gather(ends, "seq")
    if backward:
        mine = count - 1 - mine
    total = jnp.zeros_like(ends)
    for position in range(count - 1):
        piece = pieces[count - 1 - position if backward else position]
        total = jnp.where(position < mine, block_decay * total + piece, total)
    return total


def silu(value):
    return value * jax.nn.sigmoid(value)


def silu_slope(value):
    gate = jax.nn.sigmoid(value)
    return gate * (1.0 + value * (1.0 - gate))


def normalise(signal):
    centre = jnp.mean(signal, axis=-1, keepdims=True)
    shifted = signal - centre
    spread = jnp.mean(shifted * shifted, axis=-1, keepdims=True)
    scale = lax.rsqrt(spread + norm_eps)
    return shifted * scale, scale


def normalise_back(grad, gain, hat, scale):
    inner = grad * gain
    return (
        inner
        - jnp.mean(inner, axis=-1, keepdims=True)
        - hat * jnp.mean(inner * hat, axis=-1, keepdims=True)
    ) * scale


def times(left, right):
    return jnp.dot(left, right, precision=triple)


def times_back(left, right):
    return lax.dot_general(left, right, (((1,), (1,)), ((), ())), precision=triple)


def plain_layer(masked_in, normed, mix_pre, g_out, row_valid, key_valid, affine, gain_two, weights):
    value_full, mix_full, merge_full, widen_full, narrow_full = (gather_rows(w) for w in weights)
    rows, width = masked_in.shape
    sequences, _, block_len = key_valid.shape
    value_dim, shared_dim = value_full.shape[1], affine.shape[0]
    mixed = silu(mix_pre)
    value_pre = times(normed, value_full)
    values = silu(value_pre)
    projected = times(mixed, mix_full)
    second_cut = width + shared_dim
    third_cut = second_cut + value_dim
    update = jax.nn.sigmoid(projected[:, :width])
    shared_pre = projected[:, width:second_cut]
    reset_pre = projected[:, second_cut:third_cut]
    shared = silu(shared_pre)
    reset_gate = silu(reset_pre)
    queries = (shared * affine[:, 0] + affine[:, 2]).reshape(sequences, block_len, shared_dim)
    key_rows = (shared * affine[:, 1]).reshape(sequences, block_len, shared_dim)
    score_scale = shared_dim ** (-0.5)
    scores = jnp.einsum("cqz,ckz->cqk", queries, key_rows, precision=exact) * score_scale
    scores = jnp.where(key_valid > 0.5, scores, masked_score)
    soft = jax.nn.softmax(scores, axis=-1)
    values_cut = values.reshape(sequences, block_len, value_dim)
    attended = jnp.einsum("cqk,ckv->cqv", soft, values_cut, precision=triple)
    attended = attended.reshape(rows, value_dim)
    gated = attended * reset_gate
    cand_pre = projected[:, third_cut:] + times(gated, merge_full)
    candidate = silu(cand_pre)
    middle = masked_in + update * (candidate - masked_in)
    hat_two, scale_two = normalise(middle)
    normed_two = hat_two * gain_two
    wide_pre = times(normed_two, widen_full)
    hidden = silu(wide_pre)
    block_out = (middle + times(hidden, narrow_full)) * row_valid

    g_wide = times_back(g_out, narrow_full) * silu_slope(wide_pre)
    g_normed_two = times_back(g_wide, widen_full)
    gain_sum = jnp.sum(g_normed_two * hat_two, axis=0)
    g_middle = g_out + normalise_back(g_normed_two, gain_two, hat_two, scale_two)
    g_cand = g_middle * update * silu_slope(cand_pre)
    g_gated = times_back(g_cand, merge_full)
    g_attended = (g_gated * reset_gate).reshape(sequences, block_len, value_dim)
    g_soft = jnp.einsum("cqv,ckv->cqk", g_attended, values_cut, precision=triple)
    g_values = jnp.einsum("cqk,cqv->ckv", soft, g_attended, precision=triple)
    g_scores = soft * (g_soft - jnp.sum(g_soft * soft, axis=-1, keepdims=True))
    g_scores = jnp.where(key_valid > 0.5, g_scores, 0.0) * score_scale
    g_queries = jnp.einsum("cqk,ckz->cqz", g_scores, key_rows, precision=exact)
    g_keys = jnp.einsum("cqk,cqz->ckz", g_scores, queries, precision=exact)
    g_queries = g_queries.reshape(rows, shared_dim)
    g_keys = g_keys.reshape(rows, shared_dim)
    terms = (g_queries * shared, g_keys * shared, g_queries)
    affine_sum = jnp.stack([jnp.sum(term, axis=0) for term in terms])
    g_shared = (g_queries * affine[:, 0] + g_keys * affine[:, 1]) * silu_slope(shared_pre)
    g_update = g_middle * (candidate - masked_in) * update * (1.0 - update)
    g_reset = g_gated * attended * silu_slope(reset_pre)
    g_projected = jnp.concatenate([g_update, g_shared, g_reset, g_cand], axis=1)
    g_mixed = times_back(g_projected, mix_full)
    g_val = g_values.reshape(rows, value_dim) * silu_slope(value_pre)
    g_from_values = times_back(g_val, value_full)

    def total(packed):
        count = lax.axis_size("seq")
        features = packed.shape[1] // count

        def reduced(whole, tiled=True):
            part = lax.psum_scatter(whole, "seq", scatter_dimension=0, tiled=tiled)
            return lax.psum(part, "batch")

        pairs = (
            (normed, g_val),
            (mixed, g_projected),
            (gated, g_cand),
            (normed_two, g_wide),
            (hidden, g_out),
        )
        grads = tuple(reduced(product_grad(*pair)) for pair in pairs)
        blocks = packed.reshape(-1, count, features).transpose(1, 0, 2)
        return grads + (reduced(blocks, False),)

    return block_out, g_mixed, g_from_values, g_middle * (1.0 - update), gain_sum, affine_sum, total


def plane_layer(tokens, out_grad, valid, logits, rows_of, affine, weights):
    sequences, block_len, width = tokens.shape
    rows = sequences * block_len
    states, own = logits[0].shape
    device = lax.axis_index("seq")
    alpha, delta, beta, gamma = logits
    alpha_rate, damp_rate = jax.nn.sigmoid(alpha), jax.nn.sigmoid(delta)
    out_scale = states ** (-0.5)
    weight = alpha_rate * beta * gamma * out_scale
    block_decay = jnp.exp(block_len * jnp.log1p(-alpha_rate * damp_rate))
    spread = lax.dynamic_update_slice(
        jnp.zeros((3, own), jnp.float32), affine.T, (0, device * affine.shape[0])
    )
    packed = jnp.concatenate([1.0 - alpha_rate * damp_rate, weight, block_decay, rows_of, spread])
    packed = jnp.pad(packed, ((0, -packed.shape[0] % 8), (0, 0)))
    row_valid = valid.reshape(rows, 1)
    key_valid = valid.reshape(sequences, 1, block_len)
    (
        w_high, w_low, value_pre, attended, projected, shared_pre, soft, cand_pre, middle, block_out,
        two_h, two_l, gated_h, gated_l, hidden_h, hidden_l, g_wide,
        normed_h, normed_l, mixed_h, mixed_l, masked, g_out, signal, enter, mix_pre, small, shared_w,
    ) = call_forward(
        weights, packed, tokens.reshape(rows, width), out_grad.reshape(rows, width), row_valid, key_valid, states
    )
    value_weight, mix_weight, merge_weight, widen_weight, narrow_weight = weights
    tokens_grad, narrow, widen, merge, mix, value, sums = call_backward(
        (
            w_high, w_low, value_pre, projected, middle, g_wide, attended, shared_pre, soft, cand_pre,
            two_h, two_l, gated_h, gated_l, hidden_h, hidden_l, normed_h, normed_l, mixed_h, mixed_l,
            masked, g_out, signal, enter, mix_pre, small, shared_w, row_valid, key_valid,
        ),
        [w.shape for w in (narrow_weight, widen_weight, merge_weight, mix_weight, value_weight)],
    )
    direct, slope = sums[:states], sums[states : 2 * states]
    decay_grad = weight * slope
    alpha_grad = (beta * gamma * out_scale * direct - damp_rate * decay_grad) * (
        alpha_rate * (1.0 - alpha_rate)
    )
    delta_grad = -alpha_rate * decay_grad * damp_rate * (1.0 - damp_rate)
    beta_grad = alpha_rate * gamma * out_scale * direct
    gamma_grad = alpha_rate * beta * out_scale * direct
    affine_grad = lax.dynamic_slice(
        sums[2 * states + 3 : 2 * states + 6], (0, device * affine.shape[0]), affine.T.shape
    )
    return (
        block_out.reshape(tokens.shape),
        tokens_grad.reshape(tokens.shape),
        sums[2 * states],
        alpha_grad.T,
        delta_grad.T,
        beta_grad.T,
        gamma_grad.T,
        sums[2 * states + 1],
        value,
        mix,
        affine_grad.T,
        merge,
        sums[2 * states + 2],
        widen,
        narrow,
    )


def per_device(
    tokens,
    lengths,
    out_grad,
    first_gain,
    smooth_alpha,
    smooth_delta,
    smooth_beta,
    smooth_gamma,
    smooth_omega,
    value_weight,
    mix_weight,
    query_affine,
    merge_weight,
    second_gain,
    widen_weight,
    narrow_weight,
):
    sequences, block_len, width = tokens.shape
    count = lax.axis_size("seq")
    states = smooth_alpha.shape[1]
    own = first_gain.shape[0]
    own_shared = query_affine.shape[0]
    rows = sequences * block_len
    shared_dim = own_shared * count
    offsets = lax.axis_index("seq") * block_len + lax.iota(jnp.int32, block_len)
    valid = (offsets[None, :] < lengths[:, None]).astype(jnp.float32)
    weights = (value_weight, mix_weight, merge_weight, widen_weight, narrow_weight)
    if count == 8 and lax.axis_size("batch") == 4:
        logits = (smooth_alpha.T, smooth_delta.T, smooth_beta.T, smooth_gamma.T)
        rows_of = jnp.stack([first_gain, smooth_omega, second_gain])
        return plane_layer(tokens, out_grad, valid, logits, rows_of, query_affine, weights)

    affine_row = jnp.pad(query_affine.reshape(-1), (0, own - 3 * own_shared))
    packed = [
        smooth_alpha.T,
        smooth_delta.T,
        smooth_beta.T,
        smooth_gamma.T,
        jnp.stack([first_gain, smooth_omega, second_gain, affine_row]),
    ]
    small = lax.all_gather(jnp.concatenate(packed, axis=0), "seq").transpose(1, 0, 2)

    tiles = (width // lanes, lanes)
    alpha_rate = jax.nn.sigmoid(small[:states].reshape(states, *tiles))
    damp_rate = jax.nn.sigmoid(small[states : 2 * states].reshape(states, *tiles))
    beta = small[2 * states : 3 * states].reshape(states, *tiles)
    gamma = small[3 * states : 4 * states].reshape(states, *tiles)
    gain_one = small[4 * states].reshape(1, width)
    omega = small[4 * states + 1].reshape(1, width)
    gain_two = small[4 * states + 2].reshape(1, width)
    affine = small[4 * states + 3, :, : 3 * own_shared].reshape(shared_dim, 3)
    out_scale = states ** (-0.5)
    decay = 1.0 - alpha_rate * damp_rate
    block_decay = jnp.exp(block_len * jnp.log1p(-alpha_rate * damp_rate))
    weight = alpha_rate * beta * gamma * out_scale

    row_valid = valid.reshape(rows, 1)
    key_valid = valid.reshape(sequences, 1, block_len)

    masked_in = tokens.reshape(rows, width) * row_valid
    g_out = out_grad.reshape(rows, width) * row_valid
    hat_one, scale_one = normalise(masked_in)
    normed = hat_one * gain_one
    tiled = (sequences, block_len) + tiles
    ending = (sequences, states) + tiles
    signal = normed.reshape(tiled)
    local, ends = call_kernel(
        functools.partial(filter_body, False), [tiled, ending], decay, weight, signal
    )
    enter = entering(ends, block_decay, False)
    (smoothed,) = call_kernel(
        functools.partial(carried_body, False), [tiled], decay, weight, enter, local
    )
    mix_pre = smoothed.reshape(rows, width) + omega * normed

    results = plain_layer(
        masked_in, normed, mix_pre, g_out, row_valid, key_valid, affine, gain_two, weights
    )
    block_out, g_mixed, g_from_values, g_rest, second_gain_sum, affine_sum, total = results
    g_smooth = g_mixed * silu_slope(mix_pre)

    smooth_tiled = g_smooth.reshape(tiled)
    back_local, back_ends = call_kernel(
        functools.partial(filter_body, True), [tiled, ending], decay, weight, smooth_tiled
    )
    back_enter = entering(back_ends, block_decay, True)
    direct, slope, last = call_kernel(
        moments_body,
        [(states,) + tiles, (states,) + tiles, ending],
        decay,
        enter,
        signal,
        smooth_tiled,
    )
    (back_full,) = call_kernel(
        functools.partial(carried_body, True), [tiled], decay, weight, back_enter, back_local
    )
    slope = slope + decay * jnp.sum(back_enter * last, axis=0)
    decay_grad = weight * slope
    alpha_grad = (beta * gamma * out_scale * direct - damp_rate * decay_grad) * (
        alpha_rate * (1.0 - alpha_rate)
    )
    delta_grad = -alpha_rate * decay_grad * damp_rate * (1.0 - damp_rate)
    beta_grad = alpha_rate * gamma * out_scale * direct
    gamma_grad = alpha_rate * beta * out_scale * direct

    g_normed = g_from_values + g_smooth * omega + back_full.reshape(rows, width)
    tokens_grad = (g_rest + normalise_back(g_normed, gain_one, hat_one, scale_one)) * row_valid
    first_gain_sum = jnp.sum(g_normed * hat_one, axis=0)
    omega_sum = jnp.sum(g_smooth * normed, axis=0)
    affine_rows = jnp.pad(
        affine_sum.T.reshape(count, 3 * own_shared), ((0, 0), (0, own - 3 * own_shared))
    )
    small_rows = [
        alpha_grad.reshape(states, width),
        delta_grad.reshape(states, width),
        beta_grad.reshape(states, width),
        gamma_grad.reshape(states, width),
        jnp.stack([first_gain_sum, omega_sum, second_gain_sum, affine_rows.reshape(width)]),
    ]
    value_grad, mix_grad, merge_grad, widen_grad, narrow_grad, small_grad = total(
        jnp.concatenate(small_rows, axis=0)
    )

    return (
        block_out.reshape(tokens.shape),
        tokens_grad.reshape(tokens.shape),
        small_grad[4 * states],
        small_grad[:states].T,
        small_grad[states : 2 * states].T,
        small_grad[2 * states : 3 * states].T,
        small_grad[3 * states : 4 * states].T,
        small_grad[4 * states + 1],
        value_grad,
        mix_grad,
        small_grad[4 * states + 3, : 3 * own_shared].reshape(own_shared, 3),
        merge_grad,
        small_grad[4 * states + 2],
        widen_grad,
        narrow_grad,
    )


def solution(mesh):
    rows = P("batch", "seq", None)
    split = P("seq", None)
    in_specs = (
        (rows, P("batch"), rows, P("seq"))
        + (split,) * 4
        + (P("seq"),)
        + (split,) * 4
        + (P("seq"),)
        + (split,) * 2
    )
    out_specs = (
        (rows, rows, P("seq"))
        + (split,) * 4
        + (P("seq"),)
        + (split,) * 4
        + (P("seq"),)
        + (split,) * 2
    )
    return jax.shard_map(
        per_device, mesh=mesh, in_specs=in_specs, out_specs=out_specs, check_vma=False
    )
```

time: 767 us -> 604 us (0.79)
  local copies, waits for them, and re-layouts: 81.4 us -> 16.3 us
  Pallas kernels: 611 us -> 582 us
  other arithmetic: 32.2 us -> 4.14 us
  between operations: 15 us -> 0.76 us
  blocking collectives: 12 us -> 0 us
    pallas_call x7 -> x1, Pallas kernels: 372 us -> 319 us  [call_backward(): pl.pallas_call(backward_body, out_shape=shapes, in_specs=[anywhere] * 5 +...]
    reshape x17 -> x0, local copies, waits for them, and re-layouts: 28.2 us -> none  [the longest x4 10.5 us: from_places(): value.reshape(2, rows, 4, columns // 4).transpose(1, 2, 0, 3)]
    pallas_call x1, Pallas kernels: 240 us -> 263 us  [call_forward(): pl.pallas_call(forward_body, out_shape=shapes, in_specs=[anywhere] * len(...]
    transpose x11 -> x1, local copies, waits for them, and re-layouts: 16 us -> 0.65 us  [plane_layer(): return (block_out.reshape(tokens.shape), tokens_grad.reshape(tokens.shape...]
    slice x10 -> x1, local copies, waits for them, and re-layouts: 14.4 us -> 0.67 us  [plane_layer(): sums[2 * states + 3:2 * states + 6]]
    reduce_sum x5 -> x0, other arithmetic: 12.9 us -> none  [the longest x1 7.44 us: per_device(): first_gain_sum = jnp.sum(g_normed * hat_one, axis=0)]
    all_gather x1 -> x0, blocking collectives: 12 us -> none  [per_device(): lax.all_gather(jnp.concatenate(packed, axis=0), 'seq').transpose(1, 0, 2)]
  transfers between devices with their start and end apart: 2 -> 0, of which waited for: 1 -> 0; matrix products, arithmetic and copies ran while one was open for 7% -> 0% of each run, Pallas kernels for 1% -> 0%
where the time goes in v3:
time: 604 us; the launch traced here: 603 us
  Pallas kernels  582 us (96%)
  local copies, waits for them, and re-layouts  16.3 us (3%)
    pallas_call x1, Pallas kernels, call_backward(): pl.pallas_call(backward_body, out_shape=shapes, in_specs=[anywhere] * 5 +...  319 us
    pallas_call x1, Pallas kernels, call_forward(): pl.pallas_call(forward_body, out_shape=shapes, in_specs=[anywhere] * len(...  263 us

profile of v3, /device:TPU:0, one launch (start us, length us, event | category | flops | bytes accessed | tf_op | source)
XLA Modules:
  0.0 603.2 jit_solution(15893570554212400752)
XLA Ops:
  0.7 1.3 compare_convert_fusion.key_valid
  2.0 0.7 compare_convert_fusion.1
  2.7 0.8 dynamic_update_slice.3
  3.5 0.8 fusion.12
  4.2 0.7 concatenate.3
  4.9 0.6 pad.4.packed
  5.6 0.8 copy.31.row_valid
  6.4 262.7 %shard_map.271 = (bf16[64,2,512,256]{3,2,1,0:T(8,128)(2,1)}, bf16[64,2,512,256]{3,2,1,0:T(8,128)(2,1)}, f32[8,256,256]{2,1,0:T(8,128)}, f32[8,256,256]{2,1,0:T(8...) custom-call(f32[128,2048]{1,0:T(8,128)} %value_ref.1, ...), custom_call_target="tpu_custom_call" | custom-call | tf_op jit(solution)/shard_map/pallas_call | solution.py:543
  269.1 0.0 copy-start.7
  269.1 0.0 copy-start.8
  269.1 0.0 copy-start.9
  269.1 0.0 copy-start.10
  269.2 0.0 copy-start.3
  269.2 319.3 %shard_map.272 = (f32[256,1024]{1,0:T(8,128)}, f32[512,1024]{1,0:T(8,128)}, f32[128,4096]{1,0:T(8,128)}, f32[256,1024]{1,0:T(8,128)}, f32[128,4224]{1,0:T(8,128)...) custom-call(bf16[64,2,512,256]{3,2,1,0:T(8,128)(2,1)} %get-tuple-element.51.w_high, ...), custom_call_target="tpu_custom_call" | custom-call | tf_op jit(solution)/shard_map/pallas_call | solution.py:1046
  588.5 0.0 copy-start.6
  588.5 1.3 slice_bitcast_fusion
  589.8 0.7 slice.22
  590.4 0.0 copy-done.7
  590.4 0.0 copy-done.8
  590.5 0.0 copy-done.9
  590.5 0.0 copy-done.10
  590.5 1.3 fusion.14
  591.8 0.6 dynamic-slice_bitcast_fusion
  592.5 0.0 copy-done.3
  592.5 0.0 copy-start.5
  592.5 1.0 copy.41
  593.4 0.0 copy-done.6
  593.4 0.0 copy-start
  593.4 1.0 copy.42
  594.4 0.0 copy-done.5
  594.4 1.0 copy.43
  595.4 0.2 copy-done
  595.6 0.0 copy-start.4
  595.6 1.3 copy.44
  596.9 0.6 copy-done.4
  597.6 0.0 copy-start.2
  597.6 1.0 copy.45
  598.5 1.0 copy-done.2
  599.5 0.0 copy-start.1
  599.5 1.3 copy.46
  600.9 1.0 copy-done.1
  601.9 1.3 copy.47
  (2 shorter events, 0.0 us)
Async XLA Ops:
  269.1 321.3 %copy-start.7 = (f32[128,16]{0,1:T(8,128)S(1)}, f32[128,16]{0,1:T(8,128)}, u32[]{:S(2)}) copy-start(f32[128,16]{0,1:T(8,128)} %param.21) | copy-start | bytes 24580
  269.1 321.3 %copy-start.8 = (f32[128,16]{0,1:T(8,128)S(1)}, f32[128,16]{0,1:T(8,128)}, u32[]{:S(2)}) copy-start(f32[128,16]{0,1:T(8,128)} %param.20) | copy-start | bytes 24580
  269.1 321.3 %copy-start.9 = (f32[128,16]{0,1:T(8,128)S(1)}, f32[128,16]{0,1:T(8,128)}, u32[]{:S(2)}) copy-start(f32[128,16]{0,1:T(8,128)} %param.23) | copy-start | bytes 24580
  269.1 321.3 %copy-start.10 = (f32[128,16]{0,1:T(8,128)S(1)}, f32[128,16]{0,1:T(8,128)}, u32[]{:S(2)}) copy-start(f32[128,16]{0,1:T(8,128)} %param.22) | copy-start | bytes 24580
  269.2 323.3 %copy-start.3 = (f32[256,1024]{1,0:T(8,128)S(1)}, f32[256,1024]{1,0:T(8,128)}, u32[]{:S(2)}) copy-start(f32[256,1024]{1,0:T(8,128)} %get-tuple-element.50) | copy-start | bytes 3145732
  588.5 5.0 copy-start.6
  592.5 1.9 copy-start.5
  593.4 2.2 copy-start
  595.6 2.0 copy-start.4
  597.6 2.0 copy-start.2
  599.5 2.3 copy-start.1

commit v4 on v3

--- a/solution.py
+++ b/solution.py
@@ -163,20 +163,24 @@
         )
 
 
+kept_count = 25
 gather_shapes = ((1, 8), (1, 16), (2, 4), (1, 16), (4, 4))
 
 
 def forward_body(
     value_ref, mix_ref, merge_ref, widen_ref, narrow_ref, packed, tokens, out_grad, row_valid, key_valid,
-    w_high, w_low, value_pre, attended, projected, shared_pre, soft, cand_pre, middle, block_out,
-    two_h, two_l, gated_h, gated_l, hidden_h, hidden_l, g_wide,
-    normed_h, normed_l, mixed_h, mixed_l, masked, g_out, signal, enter, mix_pre, small, shared_w,
-    buf, stage_h, stage_l, g_hidden, smoothed, ends, tables, loaded, sent, came, stored, near, sent_all, came_all,
+    block_out, w_high, w_low, *refs,
 ):
+    kept, held, refs = refs[:kept_count], refs[kept_count : 2 * kept_count], refs[2 * kept_count :]
+    (
+        hidden_h, hidden_l, g_out, g_wide, two_h, two_l, gated_h, gated_l, mixed_h, mixed_l, normed_h, normed_l,
+        value_pre, projected, middle, attended, shared_pre, soft, cand_pre, masked, signal, enter, mix_pre, small, shared_w,
+    ) = held
+    buf, stage_h, stage_l, g_hidden, smoothed, ends, tables = refs[:7]
+    loaded, sent, came, stored, near, sent_all, came_all, saved = refs[7:]
     weights = (value_ref, mix_ref, merge_ref, widen_ref, narrow_ref)
     firsts, chunks = chunk_table(gather_shapes)
-    depth, delay = buf.shape[0], 2
-    width = buf.shape[-1]
+    depth, width = buf.shape[0], buf.shape[-1]
     half = lanes * 4
     me, level = lax.axis_index("seq"), lax.axis_index("batch")
     core, along_x, along_y = me % 2, (me // 2) % 2, me // 4
@@ -185,7 +189,6 @@
     id_corner = id_x + 4 - 8 * along_y
     mine, at_x, at_y, at_corner = (place_of(device) for device in (me, id_x, id_y, id_corner))
     above, below = (level + 1) % 4, (level + 3) % 4
-    quarter, eighth = lanes // 4, lanes // 8
 
     barrier = pltpu.get_barrier_semaphore()
     for other in range(1, 8):
@@ -194,29 +197,49 @@
         pl.semaphore_signal(barrier, inc=1, **on_other(batch=target))
     pl.semaphore_wait(barrier, 9)
 
-    def link(kind, chunk):
+    names = ["x", "y", "sibling", "corner_x", "corner_y", "x_more", "y_more"]
+    names += ["sibling_x", "sibling_y", "sibling_corner"]
+    names += [f"ring{number}{of}" for of in ("", "_x", "_y") for number in range(3)]
+
+    def link(name, chunk):
         slot = chunk % depth
-
-        def rows(place, start, count):
-            return buf.at[slot, place, pl.ds(pl.multiple_of(start, 8), count)]
-
-        piece, target = (
-            lambda: (buf.at[slot, mine], {"seq": id_x}),
-            lambda: (buf.at[slot, mine], {"seq": id_y}),
-            lambda: (buf.at[slot, mine], {"seq": id_sibling}),
-            lambda: (rows(at_x, level * quarter, eighth), {"seq": id_y}),
-            lambda: (rows(at_y, level * quarter + eighth, eighth), {"seq": id_x}),
-            lambda: (buf.at[slot, at_x], {"seq": id_sibling}),
-            lambda: (buf.at[slot, at_y], {"seq": id_sibling}),
-            lambda: (rows(at_corner, level * quarter, quarter), {"batch": above}),
-            lambda: (rows(at_corner, ((level + 3) % 4) * quarter, quarter), {"batch": above}),
-            lambda: (rows(at_corner, ((level + 2) % 4) * quarter, quarter), {"batch": above}),
-            lambda: (buf.at[slot, at_corner], {"seq": id_sibling}),
-        )[kind]()
+        block = {"x": at_x, "y": at_y, "corner": at_corner}
+        kind, _, of = name.partition("_")
+        by_x, by_y, by_core, by_z = ({"seq": id_x}, {"seq": id_y}, {"seq": id_sibling}, {"batch": above})
+        if kind == "sibling":
+            piece, target = buf.at[slot, block[of] if of else mine], by_core
+        elif kind == "corner":
+            if of == "x":
+                piece, target = buf.at[slot, at_x, level, pl.ds(0, 2)], by_y
+            else:
+                piece, target = buf.at[slot, at_y, level, pl.ds(2, 2)], by_x
+        elif kind[:4] == "ring":
+            quarter = (level + 4 - int(kind[4])) % 4
+            if of:
+                piece = buf.at[slot, block[of], quarter, 3 if of == "x" else 0]
+            else:
+                piece = buf.at[slot, at_corner, quarter]
+            target = by_z
+        else:
+            target = by_x if kind == "x" else by_y
+            if of == "more":
+                piece = buf.at[slot, mine, level, 3 if kind == "x" else 0]
+            elif of == "part":
+                piece = buf.at[slot, mine, :, pl.ds(0 if kind == "x" else 1, 3)]
+            else:
+                piece = buf.at[slot, mine]
+        number = names.index(name.removesuffix("_part"))
         return pltpu.make_async_remote_copy(
-            src_ref=piece, dst_ref=piece, send_sem=sent.at[kind, slot], recv_sem=came.at[kind, slot],
+            src_ref=piece, dst_ref=piece, send_sem=sent.at[number, slot], recv_sem=came.at[number, slot],
             **on_other(**target),
         )
+
+    def shares(chunk):
+        return chunk % 3 != 2
+
+    def own_load(weight, block, column, slot):
+        source = weight.at[pl.ds(block * 4, 4), :, :, pl.ds(pl.multiple_of(column, lanes), width)]
+        return pltpu.make_async_copy(source, buf.at[slot, mine], loaded.at[slot])
 
     def load(chunk):
         slot = chunk % depth
@@ -226,31 +249,69 @@
 
             @pl.when((chunk >= first) & (chunk < first + blocks * wide))
             def _(number=number, first=first, wide=wide, weight=weight):
-                row = ((chunk - first) // wide) * lanes
+                block = (chunk - first) // wide
                 column = ((chunk - first) % wide) * width
                 if number == 1:
-                    column = column + jnp.where(column >= weights[2].shape[1], lanes, 0)
-                source = weight.at[
-                    pl.ds(pl.multiple_of(row, lanes), lanes),
-                    pl.ds(pl.multiple_of(column, lanes), width),
-                ]
-                pltpu.make_async_copy(source, buf.at[slot, mine], loaded.at[slot]).start()
-
-    def exchange(done, begun):
+                    column = column + jnp.where(column >= features, lanes, 0)
+                own_load(weight, block, column, slot).start()
+
+    def send(chunk):
+        own_load(value_ref, 0, 0, chunk % depth).wait()
+        both = shares(chunk)
+        link("sibling", chunk).start()
+
+        @pl.when(both)
+        def _():
+            for name in ("x_part", "y_part", "x_more", "y_more"):
+                link(name, chunk).start()
+
+        @pl.when(jnp.logical_not(both))
+        def _():
+            link("x", chunk).start()
+            link("y", chunk).start()
+
+    def relay(chunk):
+        both = shares(chunk)
+        link("sibling", chunk).wait()
+
+        @pl.when(both)
+        def _():
+            for name in ("x_part", "y_part", "x_more", "y_more"):
+                link(name, chunk).wait()
+            link("ring0_x", chunk).start()
+            link("ring0_y", chunk).start()
+
+        @pl.when(jnp.logical_not(both))
+        def _():
+            link("x", chunk).wait()
+            link("y", chunk).wait()
+
+        link("corner_x", chunk).start()
+        link("corner_y", chunk).start()
+
+    def ring(number):
         def phase(chunk):
-            for kind in done:
-                link(kind, chunk).wait()
-            for kind in begun:
-                link(kind, chunk).start()
+            if number:
+                link(f"ring{number - 1}", chunk).wait()
+            else:
+                link("corner_x", chunk).wait()
+                link("corner_y", chunk).wait()
+
+            @pl.when(shares(chunk))
+            def _():
+                for of in "xy":
+                    link(f"ring{number}_{of}", chunk).wait()
+                    if number < 2:
+                        link(f"ring{number + 1}_{of}", chunk).start()
+
+            link(f"ring{number}", chunk).start()
 
         return phase
 
-    def send(chunk):
-        slot = chunk % depth
-        first = value_ref.at[pl.ds(0, lanes), pl.ds(0, width)]
-        pltpu.make_async_copy(first, buf.at[slot, mine], loaded.at[slot]).wait()
-        for kind in (0, 1, 2):
-            link(kind, chunk).start()
+    def to_sibling(chunk):
+        link("ring2", chunk).wait()
+        for name in ("sibling_x", "sibling_y", "sibling_corner"):
+            link(name, chunk).start()
 
     def store(chunk, kind):
         return pltpu.make_async_copy(
@@ -274,14 +335,16 @@
         if kind == 0:
             source = target = small.at[me]
         elif kind == 1:
-            source = mix_ref.at[:, pl.ds(features, lanes)]
+            source = mix_ref.at[:, :, :, pl.ds(features, lanes)]
             target = shared_w.at[mine]
         else:
             source = target = ends.at[me]
         return list(to_peers(source, target, sent_all.at[kind], came_all.at[kind]))
 
     def own_shared():
-        return pltpu.make_async_copy(mix_ref.at[:, pl.ds(features, lanes)], shared_w.at[mine], near)
+        return pltpu.make_async_copy(
+            mix_ref.at[:, :, :, pl.ds(features, lanes)], shared_w.at[mine], near
+        )
 
     def row_of(number, k):
         return jnp.concatenate(
@@ -369,7 +432,8 @@
 
     def complete(chunk):
         slot = chunk % depth
-        link(10, chunk).wait()
+        for name in ("sibling_x", "sibling_y", "sibling_corner"):
+            link(name, chunk).wait()
 
         @pl.when(chunk >= 2)
         def _():
@@ -466,40 +530,54 @@
                 back = three(grad, (right[0][parity], right[1][parity]), 1, 1)
                 g_hidden[j, parity] = g_hidden[j, parity] + back
 
+    def save(*numbers):
+        return [
+            pltpu.make_async_copy(held[number], kept[number], saved.at[number]) for number in numbers
+        ]
+
+    def begin_save(*numbers):
+        for item in save(*numbers):
+            item.start()
+
     phases = (
-        (0, load),
-        (1, send),
-        (1 + delay, exchange((0, 1, 2), (3, 4, 5, 6))),
-        (1 + 2 * delay, exchange((3, 4, 5, 6), (7,))),
-        (1 + 3 * delay, exchange((7,), (8,))),
-        (1 + 4 * delay, exchange((8,), (9,))),
-        (1 + 5 * delay, exchange((9,), (10,))),
-        (1 + 6 * delay, complete),
-    )
+        (2, relay), (4, ring(0)), (6, ring(1)), (8, ring(2)), (10, to_sibling), (11, complete)
+    )
+    last, ahead = phases[-1][0], 1
 
     def step(at, carry):
-        for after, phase in phases[-2:0:-1]:
+        for after, phase in phases[-2::-1]:
 
             @pl.when((at >= after) & (at < after + chunks))
             def _(after=after, phase=phase):
                 phase(at - after)
 
-        pl.when(at < chunks)(lambda: load(at))
-        pl.when(at == 0)(hand_out)
+        @pl.when(at == 0)
+        def _():
+            for chunk in range(ahead):
+                send(chunk)
+            hand_out()
+
+        pl.when((at >= 1) & (at + ahead - 1 < chunks))(lambda: send(at + ahead - 1))
+        pl.when(at + ahead < chunks)(lambda: load(at + ahead))
         pl.when(at == 1)(norm_one)
         for s in range(sequences):
             pl.when(at == 2 + s)(functools.partial(filter_one, s))
             pl.when(at == 5 + s)(functools.partial(carry_one, s))
-        pl.when(at == 8)(mix_in)
-        pl.when(at == 9)(attention)
-
-        @pl.when(at >= phases[-1][0])
-        def _():
-            complete(at - phases[-1][0])
+        pl.when(at == 7)(mix_in)
+        pl.when(at == 8)(attention)
+        pl.when(at == last)(lambda: begin_save(2, 8, 9, 10, 11, 16, 17, 19, 20, 21, 22, 23, 24))
+        pl.when(at == last + firsts[3])(lambda: begin_save(4, 5, 6, 7, 12, 13, 14, 15, 18))
+        pl.when(at == last + firsts[4])(lambda: begin_save(0, 1))
+
+        @pl.when(at >= last)
+        def _():
+            complete(at - last)
 
         return carry
 
-    lax.fori_loop(0, chunks + phases[-1][0], step, 0)
+    for chunk in range(ahead):
+        load(chunk)
+    lax.fori_loop(0, chunks + last, step, 0)
     for chunk in (chunks - 2, chunks - 1):
         for kind in range(2):
             store(chunk, kind).wait()
@@ -512,6 +590,9 @@
             back = g_hidden[2 * (k % 2) + i, (k // 2) % 2, :, (k // 4) * lanes : (k // 4 + 1) * lanes]
             wide = g_wide[k, :, span]
             g_wide[k, :, span] = back * silu_slope(wide)
+    begin_save(3)
+    for item in save(*range(kept_count)):
+        item.wait()
 
 
 def f32(*shape):
@@ -530,23 +611,24 @@
     _, chunks = chunk_table(gather_shapes)
     vmem, anywhere = pl.BlockSpec(memory_space=pltpu.VMEM), pl.BlockSpec(memory_space=pl.ANY)
     line = (sequences, block_len, 8, lanes)
-    shapes = [b16(chunks, 2, half, width)] * 2 + [
-        f32(8, rows, width), f32(8, rows, width), f32(16, rows, width), f32(rows, lanes),
-        f32(sequences, block_len, block_len), f32(4, rows, width), f32(4, rows, width), f32(rows, features),
+    kept = [
+        b16(4, 2, rows, half), b16(4, 2, rows, half), f32(4, rows, width), f32(16, rows, width),
         b16(2, rows, half), b16(2, rows, half), b16(2, 2, rows, half), b16(2, 2, rows, half),
-        b16(4, 2, rows, half), b16(4, 2, rows, half), f32(16, rows, width),
         b16(2, rows, half), b16(2, rows, half), b16(2, rows, half), b16(2, rows, half),
-        f32(4, rows, width), f32(4, rows, width), f32(*line), f32(sequences, states, 8, lanes),
-        f32(2, rows, half), f32(8, *packed.shape), f32(8, lanes, lanes),
+        f32(8, rows, width), f32(16, rows, width), f32(4, rows, width), f32(8, rows, width), f32(rows, lanes),
+        f32(sequences, block_len, block_len), f32(4, rows, width), f32(4, rows, width), f32(*line),
+        f32(sequences, states, 8, lanes), f32(2, rows, half), f32(8, *packed.shape), f32(8, 4, 4, 8, lanes),
     ]
-    depth = 16
+    shapes = [f32(rows, features)] + [b16(chunks, 2, half, width)] * 2 + kept
+    depth, kinds = 16, 19
     return pl.pallas_call(
         forward_body,
         out_shape=shapes,
         in_specs=[anywhere] * len(weights) + [vmem] * 5,
-        out_specs=[anywhere] * 2 + [vmem] * (len(shapes) - 2),
-        scratch_shapes=[
-            pltpu.VMEM((depth, 8, lanes, width), jnp.float32),
+        out_specs=[vmem] + [anywhere] * (len(shapes) - 1),
+        scratch_shapes=[pltpu.VMEM(item.shape, item.dtype) for item in kept]
+        + [
+            pltpu.VMEM((depth, 8, 4, 4, 8, width), jnp.float32),
             pltpu.VMEM((2, 2, half, width), jnp.bfloat16),
             pltpu.VMEM((2, 2, half, width), jnp.bfloat16),
             pltpu.VMEM((4, 2, rows, half), jnp.float32),
@@ -554,32 +636,37 @@
             pltpu.VMEM((8, sequences, states, 8, lanes), jnp.float32),
             pltpu.VMEM((3, states, 8, lanes), jnp.float32),
             pltpu.SemaphoreType.DMA((depth,)),
-            pltpu.SemaphoreType.DMA((11, depth)),
-            pltpu.SemaphoreType.DMA((11, depth)),
+            pltpu.SemaphoreType.DMA((kinds, depth)),
+            pltpu.SemaphoreType.DMA((kinds, depth)),
             pltpu.SemaphoreType.DMA((2, 2)),
             pltpu.SemaphoreType.DMA,
             pltpu.SemaphoreType.DMA((3, 7)),
             pltpu.SemaphoreType.DMA((3, 7)),
+            pltpu.SemaphoreType.DMA((kept_count,)),
         ],
         compiler_params=pltpu.CompilerParams(
             collective_id=2, has_side_effects=True, vmem_limit_bytes=62 * 1024 * 1024
         ),
-    )(*weights, packed, tokens, out_grad, row_valid, key_valid)
+    )(*[w.reshape(-1, 4, 8, w.shape[1]) for w in weights], packed, tokens, out_grad, row_valid, key_valid)
 
 
 reduce_shapes = ((4, 4), (1, 16), (2, 4), (1, 16), (1, 8))
 
 
 def backward_body(
-    w_high, w_low, value_src, projected_src, middle_src, g_wide, attended, shared_pre, soft, cand_pre,
-    two_h, two_l, gated_h, gated_l, hidden_h, hidden_l, normed_h, normed_l, mixed_h, mixed_l,
-    masked, g_out, signal, enter, mix_pre, small, shared_w, row_valid, key_valid,
-    tokens_grad, narrow_grad, widen_grad, merge_grad, mix_grad, value_grad, small_grad,
-    away, keep, got, got_x, got_y, got_xy, got_yx, part, from_edge, from_inner, done,
-    value_pre, projected, middle, buf_h, buf_l, g_two, g_gated, g_mixed, g_normed, g_soft, g_shared,
-    smooth, back, ends, back_enter, tables, direct, slope, last, small_sum,
-    fetched, read, sent, came, written, sent_all, came_all,
+    row_valid, key_valid, w_high, w_low, *refs,
 ):
+    kept, outs, refs = refs[:kept_count], refs[kept_count : kept_count + 7], refs[kept_count + 7 :]
+    held, refs = refs[:kept_count], refs[kept_count:]
+    (
+        hidden_h, hidden_l, g_out, g_wide, two_h, two_l, gated_h, gated_l, mixed_h, mixed_l, normed_h, normed_l,
+        value_pre, projected, middle, attended, shared_pre, soft, cand_pre, masked, signal, enter, mix_pre, small, shared_w,
+    ) = held
+    tokens_grad, narrow_grad, widen_grad, merge_grad, mix_grad, value_grad, small_grad = outs
+    away, keep, got, got_x, got_y, got_xy, got_yx, part, from_edge, from_inner, done = refs[:11]
+    buf_h, buf_l, g_two, g_gated, g_mixed, g_normed, g_soft, g_shared = refs[11:19]
+    smooth, back, ends, back_enter, tables, direct, slope, last, small_sum = refs[19:28]
+    fetched, read, sent, came, written, sent_all, came_all = refs[28:]
     lefts = (
         (hidden_h, hidden_l), (two_h, two_l), (gated_h, gated_l), (mixed_h, mixed_l), (normed_h, normed_l)
     )
@@ -587,7 +674,6 @@
     grads = (narrow_grad, widen_grad, merge_grad, mix_grad, value_grad)
     firsts, chunks = chunk_table(reduce_shapes)
     gathered, _ = chunk_table(gather_shapes)
-    delay = 2
     tiles, rows, width = masked.shape
     half, features = 4 * lanes, tiles * width
     sequences, block_len = soft.shape[:2]
@@ -603,9 +689,7 @@
 
     copies_in = [
         pltpu.make_async_copy(source, target, read.at[number])
-        for number, (source, target) in enumerate(
-            ((middle_src, middle), (projected_src, projected), (value_src, value_pre))
-        )
+        for number, (source, target) in enumerate(zip(kept, held))
     ]
     for item in copies_in:
         item.start()
@@ -737,8 +821,9 @@
         slot = slot_in(part, chunk)
         link(3, chunk).wait()
         link(4, chunk).wait()
-        part[slot, 0] = got_x[slot, along_y] + got_xy[slot]
-        part[slot, 1] = got_y[slot, along_x] + got_yx[slot]
+        first, second = slot_in(got_x, chunk), slot_in(got_xy, chunk)
+        part[slot, 0] = got_x[first, along_y] + got_xy[second]
+        part[slot, 1] = got_y[first, along_x] + got_yx[second]
         pl.when(is_edge)(lambda: link(5, chunk).start())
 
     def inner_sum(chunk):
@@ -812,8 +897,6 @@
         return centre, lax.rsqrt(total / features + norm_eps)
 
     def norm_two_back():
-        for item in copies_in:
-            item.wait()
         centre, scale = statistics(middle)
 
         def grad_of(k):
@@ -1005,38 +1088,44 @@
             pl.when(at == 56 + s)(functools.partial(carry_one, s))
         pl.when(at == 59)(norm_one_back)
 
-    phases = (begin, with_sibling, with_neighbour, with_corner, inner_sum, total_sum, finish)
+    phases = (
+        (0, begin), (1, with_sibling), (3, with_neighbour), (5, with_corner), (7, inner_sum), (9, total_sum), (11, finish)
+    )
     fetch(0, "start")
     fetch(1, "start")
 
+    def arrive(first, end):
+        for item in copies_in[first:end]:
+            item.wait()
+
+    arrive(0, 3)
+
     def step(at, carry):
-        for number in range(len(phases) - 1, -1, -1):
-            chunk = at - number * delay
-
-            @pl.when((chunk >= 0) & (chunk <= chunks))
-            def _(number=number, chunk=chunk):
-                phases[number](chunk)
-
+        for after, phase in phases[::-1]:
+
+            @pl.when((at >= after) & (at <= after + chunks))
+            def _(after=after, phase=phase):
+                phase(at - after)
+
+        pl.when(at == 0)(lambda: arrive(3, 4))
+        pl.when(at == 8)(lambda: arrive(4, kept_count))
         work(at)
         return carry
 
-    lax.fori_loop(0, chunks + 1 + (len(phases) - 1) * delay, step, 0)
-
-
-def call_backward(operands, grad_shapes):
-    g_wide, soft = operands[5], operands[8]
-    signal, enter, small = operands[22], operands[23], operands[25]
-    _, rows, width = g_wide.shape
-    sequences, block_len = soft.shape[:2]
+    lax.fori_loop(0, chunks + 1 + phases[-1][0], step, 0)
+
+
+def call_backward(row_valid, key_valid, w_high, w_low, kept, grad_shapes):
+    _, rows, width = kept[3].shape
+    soft, signal, enter = kept[17], kept[20], kept[21]
     states = enter.shape[1]
     half, piece, depth = 4 * lanes, lanes // 2, 8
     vmem, anywhere = pl.BlockSpec(memory_space=pltpu.VMEM), pl.BlockSpec(memory_space=pl.ANY)
     shapes = [f32(rows, 8 * lanes)] + [f32(*shape) for shape in grad_shapes] + [f32(lanes, lanes)]
     held = [
         (4, 2, 2, 2, piece, width), (6, 2, 2, 2, piece, width), (4, 2, 2, 2, piece, width),
-        (depth, 2, piece, width), (depth, 2, piece, width), (depth, piece, width), (depth, piece, width),
+        (9, 2, piece, width), (9, 2, piece, width), (depth, piece, width), (depth, piece, width),
         (depth, 2, piece, width), (depth, 2, piece, width), (depth, 2, piece, width), (depth, lanes, width),
-        (8, rows, width), (16, rows, width), (4, rows, width),
     ]
     more = [
         (2, rows, half), (2, 2, rows, half), (2, rows, half), (2, rows, half), soft.shape, (rows, lanes),
@@ -1046,14 +1135,15 @@
     return pl.pallas_call(
         backward_body,
         out_shape=shapes,
-        in_specs=[anywhere] * 5 + [vmem] * (len(operands) - 5),
+        in_specs=[vmem] * 2 + [anywhere] * (2 + kept_count),
         out_specs=[vmem] + [anywhere] * (len(shapes) - 1),
-        scratch_shapes=[pltpu.VMEM(shape, jnp.float32) for shape in held]
+        scratch_shapes=[pltpu.VMEM(item.shape, item.dtype) for item in kept]
+        + [pltpu.VMEM(shape, jnp.float32) for shape in held]
         + [pltpu.VMEM((3, 2, half, width), jnp.bfloat16)] * 2
         + [pltpu.VMEM(shape, jnp.float32) for shape in more]
         + [
             pltpu.SemaphoreType.DMA((2, 3)),
-            pltpu.SemaphoreType.DMA((3,)),
+            pltpu.SemaphoreType.DMA((kept_count,)),
             pltpu.SemaphoreType.DMA((9, depth)),
             pltpu.SemaphoreType.DMA((9, depth)),
             pltpu.SemaphoreType.DMA((2, depth)),
@@ -1063,7 +1153,7 @@
         compiler_params=pltpu.CompilerParams(
             collective_id=1, has_side_effects=True, vmem_limit_bytes=62 * 1024 * 1024
         ),
-    )(*operands)
+    )(row_valid, key_valid, w_high, w_low, *kept)
 
 
 def call_kernel(body, shapes, *operands):
@@ -1221,20 +1311,16 @@
     packed = jnp.pad(packed, ((0, -packed.shape[0] % 8), (0, 0)))
     row_valid = valid.reshape(rows, 1)
     key_valid = valid.reshape(sequences, 1, block_len)
-    (
-        w_high, w_low, value_pre, attended, projected, shared_pre, soft, cand_pre, middle, block_out,
-        two_h, two_l, gated_h, gated_l, hidden_h, hidden_l, g_wide,
-        normed_h, normed_l, mixed_h, mixed_l, masked, g_out, signal, enter, mix_pre, small, shared_w,
-    ) = call_forward(
+    block_out, w_high, w_low, *kept = call_forward(
         weights, packed, tokens.reshape(rows, width), out_grad.reshape(rows, width), row_valid, key_valid, states
     )
     value_weight, mix_weight, merge_weight, widen_weight, narrow_weight = weights
     tokens_grad, narrow, widen, merge, mix, value, sums = call_backward(
-        (
-            w_high, w_low, value_pre, projected, middle, g_wide, attended, shared_pre, soft, cand_pre,
-            two_h, two_l, gated_h, gated_l, hidden_h, hidden_l, normed_h, normed_l, mixed_h, mixed_l,
-            masked, g_out, signal, enter, mix_pre, small, shared_w, row_valid, key_valid,
-        ),
+        row_valid,
+        key_valid,
+        w_high,
+        w_low,
+        kept,
         [w.shape for w in (narrow_weight, widen_weight, merge_weight, mix_weight, value_weight)],
     )
     direct, slope = sums[:states], sums[states : 2 * states]

time: 604 us -> 580 us (0.960)
  Pallas kernels: 582 us -> 558 us
    pallas_call x1, Pallas kernels: 263 us -> 239 us  [call_forward(): pl.pallas_call(forward_body, out_shape=shapes, in_specs=[anywhere] * len(...]
where the time goes in v4:
time: 580 us; the launch traced here: 579 us
  Pallas kernels  558 us (96%)
  local copies, waits for them, and re-layouts  16.3 us (3%)
    pallas_call x1, Pallas kernels, call_backward(): pl.pallas_call(backward_body, out_shape=shapes, in_specs=[vmem] * 2 + [an...  319 us
    pallas_call x1, Pallas kernels, call_forward(): pl.pallas_call(forward_body, out_shape=shapes, in_specs=[anywhere] * len(...  239 us

profile of v4, /device:TPU:0, one launch (start us, length us, event | category | flops | bytes accessed | tf_op | source)
XLA Modules:
  0.0 579.1 jit_solution(18297365468014812567)
XLA Ops:
  0.7 1.3 compare_convert_fusion.key_valid
  2.0 0.7 compare_convert_fusion.1
  2.7 0.8 dynamic_update_slice.3
  3.5 0.8 fusion.12
  4.2 0.7 concatenate.3
  4.9 0.6 pad.4.packed
  5.6 0.8 copy.31.row_valid
  6.4 239.2 %shard_map.271 = (f32[256,1024]{1,0:T(8,128)}, bf16[64,2,512,256]{3,2,1,0:T(8,128)(2,1)}, bf16[64,2,512,256]{3,2,1,0:T(8,128)(2,1)}, bf16[4,2,256,512]{3,2,1,0:T...) custom-call(f32[4,4,8,2048]{3,2,1,0:T(8,128)} %bitcast.108, ...), custom_call_target="tpu_custom_call" | custom-call | tf_op jit(solution)/shard_map/pallas_call | solution.py:624
  245.6 0.0 copy-start.7
  245.6 0.0 copy-start.8
  245.6 0.0 copy-start.9
  245.6 0.0 copy-start.10
  245.6 0.0 copy-start.3
  245.6 318.7 %shard_map.272 = (f32[256,1024]{1,0:T(8,128)}, f32[512,1024]{1,0:T(8,128)}, f32[128,4096]{1,0:T(8,128)}, f32[256,1024]{1,0:T(8,128)}, f32[128,4224]{1,0:T(8,128)...) custom-call(f32[256,1]{1,0:T(8,128)} %copy.31.row_valid, f32[2,1,128]{2,1,0:T(1,128)} %compare_convert_fusion.key_valid, ...), custom_call_target="tpu_custom_call" | custom-call | tf_op jit(solution)/shard_map/pallas_call | solution.py:1135
  564.4 0.0 copy-start.6
  564.4 1.3 slice_bitcast_fusion
  565.7 0.7 slice.22
  566.4 0.0 copy-done.7
  566.4 0.0 copy-done.8
  566.4 0.0 copy-done.9
  566.4 0.0 copy-done.10
  566.4 1.3 fusion.14
  567.8 0.6 dynamic-slice_bitcast_fusion
  568.4 0.0 copy-done.3
  568.4 0.0 copy-start.5
  568.4 1.0 copy.41
  569.4 0.0 copy-done.6
  569.4 0.0 copy-start
  569.4 1.0 copy.42
  570.4 0.0 copy-done.5
  570.4 1.0 copy.43
  571.3 0.2 copy-done
  571.5 0.0 copy-start.4
  571.5 1.3 copy.44
  572.9 0.6 copy-done.4
  573.5 0.0 copy-start.2
  573.5 1.0 copy.45
  574.5 1.0 copy-done.2
  575.5 0.0 copy-start.1
  575.5 1.3 copy.46
  576.8 1.0 copy-done.1
  577.8 1.3 copy.47
  (2 shorter events, 0.0 us)
Async XLA Ops:
  245.6 320.8 %copy-start.7 = (f32[128,16]{0,1:T(8,128)S(1)}, f32[128,16]{0,1:T(8,128)}, u32[]{:S(2)}) copy-start(f32[128,16]{0,1:T(8,128)} %param.21) | copy-start | bytes 24580
  245.6 320.8 %copy-start.8 = (f32[128,16]{0,1:T(8,128)S(1)}, f32[128,16]{0,1:T(8,128)}, u32[]{:S(2)}) copy-start(f32[128,16]{0,1:T(8,128)} %param.20) | copy-start | bytes 24580
  245.6 320.8 %copy-start.9 = (f32[128,16]{0,1:T(8,128)S(1)}, f32[128,16]{0,1:T(8,128)}, u32[]{:S(2)}) copy-start(f32[128,16]{0,1:T(8,128)} %param.23) | copy-start | bytes 24580
  245.6 320.8 %copy-start.10 = (f32[128,16]{0,1:T(8,128)S(1)}, f32[128,16]{0,1:T(8,128)}, u32[]{:S(2)}) copy-start(f32[128,16]{0,1:T(8,128)} %param.22) | copy-start | bytes 24580
  245.6 322.8 %copy-start.3 = (f32[256,1024]{1,0:T(8,128)S(1)}, f32[256,1024]{1,0:T(8,128)}, u32[]{:S(2)}) copy-start(f32[256,1024]{1,0:T(8,128)} %get-tuple-element.50) | copy-start | bytes 3145732
  564.4 5.0 copy-start.6
  568.4 1.9 copy-start.5
  569.4 2.2 copy-start
  571.5 2.0 copy-start.4
  573.5 2.0 copy-start.2
  575.5 2.3 copy-start.1

commit v5 on v4

--- a/solution.py
+++ b/solution.py
@@ -127,21 +127,6 @@
             run_moments(s, low, min(low + 8, states), decay_ref, enter_ref, signal_ref, grad_ref, *outs)
 
 
-def run_entering(reverse, s, block_ref, ends_ref, me, enter_ref):
-    count = ends_ref.shape[0]
-    mine = count - 1 - me if reverse else me
-
-    def one(n, carry):
-        total = jnp.zeros(block_ref.shape[1:], jnp.float32)
-        for position in range(count - 1):
-            piece = ends_ref[count - 1 - position if reverse else position, s, n]
-            total = jnp.where(position < mine, block_ref[n] * total + piece, total)
-        enter_ref[s, n] = total
-        return carry
-
-    lax.fori_loop(0, block_ref.shape[0], one, 0)
-
-
 def on_other(**coordinate):
     return dict(device_id=coordinate, device_id_type=pl.DeviceIdType.MESH)
 
@@ -154,13 +139,87 @@
     return firsts, chunk
 
 
-def to_peers(source, target, sent, came):
+def others_of(me):
+    core, along_x, along_y = me % 2, (me // 2) % 2, me // 4
+    across_x = me + 2 - 4 * along_x
+    return me + 1 - 2 * core, across_x, me + 4 - 8 * along_y, across_x + 4 - 8 * along_y
+
+
+def state_exchange(reverse, block_ref, ends, chip_ends, halves_ref, enter_ref, sent, came):
     me = lax.axis_index("seq")
-    for k in range(1, 8):
-        yield pltpu.make_async_remote_copy(
-            src_ref=source, dst_ref=target, send_sem=sent.at[k - 1], recv_sem=came.at[k - 1],
-            **on_other(seq=(me // 4 + k // 4) % 2 * 4 + (me // 2 + k // 2) % 2 * 2 + (me + k) % 2),
-        )
+    core, chip = me % 2, me // 2
+    sibling, *chips = others_of(me)
+    first = 1 if reverse else 0
+    _, sequences, states = ends.shape[:3]
+    half = states // 2
+
+    def copies(step):
+        if step == 0:
+            pairs = [(ends.at[core], sibling)]
+        elif step == 1:
+            pairs = [(chip_ends.at[chip], other) for other in chips]
+        else:
+            pairs = [(halves_ref.at[core], sibling)]
+        for number, (piece, other) in enumerate(pairs):
+            at = (0, 1, 4)[step] + number
+            yield pltpu.make_async_remote_copy(
+                src_ref=piece, dst_ref=piece, send_sem=sent.at[at], recv_sem=came.at[at], **on_other(seq=other)
+            )
+
+    def start(step):
+        for item in copies(step):
+            item.start()
+
+    def wait(step):
+        for item in copies(step):
+            item.wait()
+
+    def share_ends():
+        start(0)
+
+    def to_chips():
+        wait(0)
+
+        def one(i, carry):
+            n = core * half + i
+            for s in range(sequences):
+                chip_ends[chip, s, i] = block_ref[n] * ends[first, s, n] + ends[1 - first, s, n]
+            return carry
+
+        lax.fori_loop(0, half, one, 0)
+        start(1)
+
+    def share_entering():
+        wait(1)
+        mine = 3 - chip if reverse else chip
+
+        def one(i, carry):
+            decay = block_ref[core * half + i]
+            decay = decay * decay
+            for s in range(sequences):
+                total = jnp.zeros(block_ref.shape[1:], jnp.float32)
+                for position in range(3):
+                    piece = chip_ends[3 - position if reverse else position, s, i]
+                    total = jnp.where(position < mine, decay * total + piece, total)
+                halves_ref[core, s, i] = total
+            return carry
+
+        lax.fori_loop(0, half, one, 0)
+        start(2)
+
+    def enter():
+        wait(2)
+
+        def one(n, carry):
+            for s in range(sequences):
+                total = halves_ref[n // half, s, n % half]
+                later = block_ref[n] * total + ends[first, s, n]
+                enter_ref[s, n] = jnp.where(core == first, total, later)
+            return carry
+
+        lax.fori_loop(0, states, one, 0)
+
+    return share_ends, to_chips, share_entering, enter
 
 
 kept_count = 25
@@ -176,26 +235,23 @@
         hidden_h, hidden_l, g_out, g_wide, two_h, two_l, gated_h, gated_l, mixed_h, mixed_l, normed_h, normed_l,
         value_pre, projected, middle, attended, shared_pre, soft, cand_pre, masked, signal, enter, mix_pre, small, shared_w,
     ) = held
-    buf, stage_h, stage_l, g_hidden, smoothed, ends, tables = refs[:7]
-    loaded, sent, came, stored, near, sent_all, came_all, saved = refs[7:]
+    buf, stage_h, stage_l, g_hidden, smoothed, ends, chip_ends, halves_in, tables = refs[:9]
+    loaded, sent, came, stored, near, sent_all, came_all, sent_state, came_state, saved = refs[9:]
     weights = (value_ref, mix_ref, merge_ref, widen_ref, narrow_ref)
     firsts, chunks = chunk_table(gather_shapes)
     depth, width = buf.shape[0], buf.shape[-1]
     half = lanes * 4
     me, level = lax.axis_index("seq"), lax.axis_index("batch")
-    core, along_x, along_y = me % 2, (me // 2) % 2, me // 4
-    id_sibling = me + 1 - 2 * core
-    id_x, id_y = me + 2 - 4 * along_x, me + 4 - 8 * along_y
-    id_corner = id_x + 4 - 8 * along_y
+    id_sibling, id_x, id_y, id_corner = others_of(me)
     mine, at_x, at_y, at_corner = (place_of(device) for device in (me, id_x, id_y, id_corner))
     above, below = (level + 1) % 4, (level + 3) % 4
 
     barrier = pltpu.get_barrier_semaphore()
-    for other in range(1, 8):
-        pl.semaphore_signal(barrier, inc=1, **on_other(seq=(me + other) % 8))
+    for other in (id_sibling, id_x, id_y, id_corner):
+        pl.semaphore_signal(barrier, inc=1, **on_other(seq=other))
     for target in (above, below):
         pl.semaphore_signal(barrier, inc=1, **on_other(batch=target))
-    pl.semaphore_wait(barrier, 9)
+    pl.semaphore_wait(barrier, 6)
 
     names = ["x", "y", "sibling", "corner_x", "corner_y", "x_more", "y_more"]
     names += ["sibling_x", "sibling_y", "sibling_corner"]
@@ -331,15 +387,22 @@
     features = tokens.shape[1]
     tiles = features // width
 
-    def share(kind):
-        if kind == 0:
-            source = target = small.at[me]
-        elif kind == 1:
-            source = mix_ref.at[:, :, :, pl.ds(features, lanes)]
-            target = shared_w.at[mine]
-        else:
-            source = target = ends.at[me]
-        return list(to_peers(source, target, sent_all.at[kind], came_all.at[kind]))
+    share_ends, to_chips, share_entering, enter_states = state_exchange(
+        False, block_decay, ends, chip_ends, halves_in, enter, sent_state, came_state
+    )
+
+    def share(kind, numbers):
+        sources = (me,) * 4 + (id_x, id_y, id_corner)
+        targets = (id_sibling, id_x, id_y, id_corner) + (id_sibling,) * 3
+        for number in numbers:
+            if kind == 0:
+                piece = small.at[sources[number]]
+            else:
+                piece = shared_w.at[place_of(sources[number])]
+            yield pltpu.make_async_remote_copy(
+                src_ref=piece, dst_ref=piece, send_sem=sent_all.at[kind, number],
+                recv_sem=came_all.at[kind, number], **on_other(seq=targets[number]),
+            )
 
     def own_shared():
         return pltpu.make_async_copy(
@@ -352,17 +415,24 @@
         )
 
     def hand_out():
+        own_shared().start()
         small[me] = packed[...]
+        for item in share(0, range(4)):
+            item.start()
+        own_shared().wait()
+        for item in share(1, range(4)):
+            item.start()
+
+    def pass_on():
         for kind in (0, 1):
-            for item in share(kind):
+            for item in share(kind, range(4)):
+                item.wait()
+            for item in share(kind, range(4, 7)):
                 item.start()
-        own_shared().start()
 
     def norm_one():
-        for kind in (0, 1):
-            for item in share(kind):
-                item.wait()
-        own_shared().wait()
+        for item in share(0, range(4, 7)):
+            item.wait()
         for kind in range(3):
             for n in range(states):
                 tables[kind, n] = small[:, kind * states + n]
@@ -385,16 +455,13 @@
             signal[s] = rows.reshape(signal.shape[1:])
 
     def filter_one(s):
-        run_filter(False, s, decay, weight, signal, smoothed, ends.at[me])
+        run_filter(False, s, decay, weight, signal, smoothed, ends.at[me % 2])
         if s == sequences - 1:
-            for item in share(2):
-                item.start()
+            share_ends()
 
     def carry_one(s):
         if s == 0:
-            for item in share(2):
-                item.wait()
-        run_entering(False, s, block_decay, ends, me, enter)
+            enter_states()
         run_carried(False, s, decay, weight, enter, smoothed, smoothed)
 
     def mix_in():
@@ -411,6 +478,8 @@
                 mixed_h[to], mixed_l[to] = halves(mixed[:, cut])
 
     def attention():
+        for item in share(1, range(4, 7)):
+            item.wait()
         shared_full = halves(shared_w[...].reshape(2, half, lanes))
         total = product(mixed_h, mixed_l, shared_full)
         affine = tree_sum([small[k, 3 * states + 3 : 3 * states + 6] for k in range(8)])
@@ -559,12 +628,19 @@
 
         pl.when((at >= 1) & (at + ahead - 1 < chunks))(lambda: send(at + ahead - 1))
         pl.when(at + ahead < chunks)(lambda: load(at + ahead))
-        pl.when(at == 1)(norm_one)
+        pl.when(at == 1)(pass_on)
+        pl.when(at == 2)(norm_one)
         for s in range(sequences):
-            pl.when(at == 2 + s)(functools.partial(filter_one, s))
-            pl.when(at == 5 + s)(functools.partial(carry_one, s))
-        pl.when(at == 7)(mix_in)
-        pl.when(at == 8)(attention)
+            pl.when(at == 3 + s)(functools.partial(filter_one, s))
+            pl.when(at == 8 + s)(functools.partial(carry_one, s))
+        pl.when(at == 5)(to_chips)
+        pl.when(at == 7)(share_entering)
+
+        @pl.when(at == 10)
+        def _():
+            mix_in()
+            attention()
+
         pl.when(at == last)(lambda: begin_save(2, 8, 9, 10, 11, 16, 17, 19, 20, 21, 22, 23, 24))
         pl.when(at == last + firsts[3])(lambda: begin_save(4, 5, 6, 7, 12, 13, 14, 15, 18))
         pl.when(at == last + firsts[4])(lambda: begin_save(0, 1))
@@ -633,15 +709,19 @@
             pltpu.VMEM((2, 2, half, width), jnp.bfloat16),
             pltpu.VMEM((4, 2, rows, half), jnp.float32),
             pltpu.VMEM(line, jnp.float32),
-            pltpu.VMEM((8, sequences, states, 8, lanes), jnp.float32),
+            pltpu.VMEM((2, sequences, states, 8, lanes), jnp.float32),
+            pltpu.VMEM((4, sequences, states // 2, 8, lanes), jnp.float32),
+            pltpu.VMEM((2, sequences, states // 2, 8, lanes), jnp.float32),
             pltpu.VMEM((3, states, 8, lanes), jnp.float32),
             pltpu.SemaphoreType.DMA((depth,)),
             pltpu.SemaphoreType.DMA((kinds, depth)),
             pltpu.SemaphoreType.DMA((kinds, depth)),
             pltpu.SemaphoreType.DMA((2, 2)),
             pltpu.SemaphoreType.DMA,
-            pltpu.SemaphoreType.DMA((3, 7)),
-            pltpu.SemaphoreType.DMA((3, 7)),
+            pltpu.SemaphoreType.DMA((2, 7)),
+            pltpu.SemaphoreType.DMA((2, 7)),
+            pltpu.SemaphoreType.DMA((5,)),
+            pltpu.SemaphoreType.DMA((5,)),
             pltpu.SemaphoreType.DMA((kept_count,)),
         ],
         compiler_params=pltpu.CompilerParams(
@@ -665,8 +745,8 @@
     tokens_grad, narrow_grad, widen_grad, merge_grad, mix_grad, value_grad, small_grad = outs
     away, keep, got, got_x, got_y, got_xy, got_yx, part, from_edge, from_inner, done = refs[:11]
     buf_h, buf_l, g_two, g_gated, g_mixed, g_normed, g_soft, g_shared = refs[11:19]
-    smooth, back, ends, back_enter, tables, direct, slope, last, small_sum = refs[19:28]
-    fetched, read, sent, came, written, sent_all, came_all = refs[28:]
+    smooth, back, ends, chip_ends, halves_in, back_enter, tables, direct, slope, last, small_sum = refs[19:30]
+    fetched, read, sent, came, written, sent_state, came_state = refs[30:]
     lefts = (
         (hidden_h, hidden_l), (two_h, two_l), (gated_h, gated_l), (mixed_h, mixed_l), (normed_h, normed_l)
     )
@@ -683,9 +763,8 @@
     core, along_x, along_y = me % 2, (me // 2) % 2, me // 4
     is_edge = (level == 0) | (level == 3)
     partner = jnp.where(level < 2, 1 - level, 5 - level)
-    sibling, across_x, across_y = (
-        {"seq": me + bit * (1 - 2 * own)} for bit, own in ((1, core), (2, along_x), (4, along_y))
-    )
+    near = others_of(me)
+    sibling, across_x, across_y = ({"seq": other} for other in near[:3])
 
     copies_in = [
         pltpu.make_async_copy(source, target, read.at[number])
@@ -695,18 +774,18 @@
         item.start()
 
     barrier = pltpu.get_barrier_semaphore()
-    for other in range(1, 8):
-        pl.semaphore_signal(barrier, inc=1, **on_other(seq=(me + other) % 8))
+    for other in near:
+        pl.semaphore_signal(barrier, inc=1, **on_other(seq=other))
     pl.semaphore_signal(barrier, inc=1, **on_other(batch=partner))
 
     @pl.when(jnp.logical_not(is_edge))
     def _():
         pl.semaphore_signal(barrier, inc=1, **on_other(batch=3 - level))
-        pl.semaphore_wait(barrier, 9)
+        pl.semaphore_wait(barrier, 6)
 
     @pl.when(is_edge)
     def _():
-        pl.semaphore_wait(barrier, 8)
+        pl.semaphore_wait(barrier, 5)
 
     def slot_in(ref, chunk):
         return chunk % ref.shape[0]
@@ -984,23 +1063,21 @@
             ]
             smooth[s] = jnp.concatenate(blocks, axis=1).reshape(smooth.shape[1:])
 
-    def share():
-        return list(to_peers(ends.at[me], ends.at[me], sent_all, came_all))
+    share_ends, to_chips, share_entering, enter_states = state_exchange(
+        True, block_decay, ends, chip_ends, halves_in, back_enter, sent_state, came_state
+    )
 
     def filter_one(s):
-        run_filter(True, s, decay, weight, smooth, back, ends.at[me])
+        run_filter(True, s, decay, weight, smooth, back, ends.at[core])
         if s == sequences - 1:
-            for item in share():
-                item.start()
+            share_ends()
 
     def moments_one(s, low):
         run_moments(s, low, low + 8, decay, enter, signal, smooth, direct, slope, last)
 
     def carry_one(s):
         if s == 0:
-            for item in share():
-                item.wait()
-        run_entering(True, s, block_decay, ends, me, back_enter)
+            enter_states()
         run_carried(True, s, decay, weight, back_enter, back, back)
 
     def norm_one_back():
@@ -1086,6 +1163,8 @@
                 number = 51 + s * (states // 8) + low // 8
                 pl.when(at == number)(functools.partial(moments_one, s, low))
             pl.when(at == 56 + s)(functools.partial(carry_one, s))
+        pl.when(at == 52)(to_chips)
+        pl.when(at == 54)(share_entering)
         pl.when(at == 59)(norm_one_back)
 
     phases = (
@@ -1129,7 +1208,8 @@
     ]
     more = [
         (2, rows, half), (2, 2, rows, half), (2, rows, half), (2, rows, half), soft.shape, (rows, lanes),
-        signal.shape, signal.shape, (8, *enter.shape), enter.shape, (3, states, 8, lanes),
+        signal.shape, signal.shape, (2, *enter.shape), (4, enter.shape[0], states // 2, 8, lanes),
+        (2, enter.shape[0], states // 2, 8, lanes), enter.shape, (3, states, 8, lanes),
         (states, 8, lanes), (states, 8, lanes), enter.shape, (8, lanes, lanes),
     ]
     return pl.pallas_call(
@@ -1147,8 +1227,8 @@
             pltpu.SemaphoreType.DMA((9, depth)),
             pltpu.SemaphoreType.DMA((9, depth)),
             pltpu.SemaphoreType.DMA((2, depth)),
-            pltpu.SemaphoreType.DMA((7,)),
-            pltpu.SemaphoreType.DMA((7,)),
+            pltpu.SemaphoreType.DMA((5,)),
+            pltpu.SemaphoreType.DMA((5,)),
         ],
         compiler_params=pltpu.CompilerParams(
             collective_id=1, has_side_effects=True, vmem_limit_bytes=62 * 1024 * 1024

time: 580 us -> 558 us (0.962)
  Pallas kernels: 558 us -> 537 us
    pallas_call x1, Pallas kernels: 239 us -> 227 us  [call_forward(): pl.pallas_call(forward_body, out_shape=shapes, in_specs=[anywhere] * len(...]
    pallas_call x1, Pallas kernels: 319 us -> 309 us  [call_backward(): pl.pallas_call(backward_body, out_shape=shapes, in_specs=[vmem] * 2 + [an...]
where the time goes in v5:
time: 558 us
  Pallas kernels  537 us (96%)
  local copies, waits for them, and re-layouts  16.3 us (3%)
    pallas_call x1, Pallas kernels, call_backward(): pl.pallas_call(backward_body, out_shape=shapes, in_specs=[vmem] * 2 + [an...  309 us
    pallas_call x1, Pallas kernels, call_forward(): pl.pallas_call(forward_body, out_shape=shapes, in_specs=[anywhere] * len(...  227 us

profile of v5, /device:TPU:0, one launch (start us, length us, event | category | flops | bytes accessed | tf_op | source)
XLA Modules:
  0.0 557.7 jit_solution(15350978685359121101)
XLA Ops:
  0.7 1.3 compare_convert_fusion.key_valid
  2.0 0.7 compare_convert_fusion.1
  2.7 0.8 dynamic_update_slice.3
  3.5 0.8 fusion.12
  4.2 0.7 concatenate.3
  4.9 0.6 pad.4.packed
  5.6 0.8 copy.31.row_valid
  6.4 227.4 %shard_map.271 = (f32[256,1024]{1,0:T(8,128)}, bf16[64,2,512,256]{3,2,1,0:T(8,128)(2,1)}, bf16[64,2,512,256]{3,2,1,0:T(8,128)(2,1)}, bf16[4,2,256,512]{3,2,1,0:T...) custom-call(f32[4,4,8,2048]{3,2,1,0:T(8,128)} %bitcast.108, ...), custom_call_target="tpu_custom_call" | custom-call | tf_op jit(solution)/shard_map/pallas_call | solution.py:700
  233.8 0.0 copy-start.7
  233.8 0.0 copy-start.8
  233.8 0.0 copy-start.9
  233.8 0.0 copy-start.10
  233.8 0.0 copy-start.3
  233.9 309.1 %shard_map.272 = (f32[256,1024]{1,0:T(8,128)}, f32[512,1024]{1,0:T(8,128)}, f32[128,4096]{1,0:T(8,128)}, f32[256,1024]{1,0:T(8,128)}, f32[128,4224]{1,0:T(8,128)...) custom-call(f32[256,1]{1,0:T(8,128)} %copy.31.row_valid, f32[2,1,128]{2,1,0:T(1,128)} %compare_convert_fusion.key_valid, ...), custom_call_target="tpu_custom_call" | custom-call | tf_op jit(solution)/shard_map/pallas_call | solution.py:1215
  542.9 0.0 copy-start.6
  543.0 1.3 slice_bitcast_fusion
  544.3 0.7 slice.22
  544.9 0.0 copy-done.7
  544.9 0.0 copy-done.8
  544.9 0.0 copy-done.9
  544.9 0.0 copy-done.10
  545.0 1.3 fusion.14
  546.3 0.6 dynamic-slice_bitcast_fusion
  547.0 0.0 copy-done.3
  547.0 0.0 copy-start.5
  547.0 1.0 copy.41
  547.9 0.0 copy-done.6
  547.9 0.0 copy-start
  547.9 1.0 copy.42
  548.9 0.0 copy-done.5
  548.9 1.0 copy.43
  549.9 0.2 copy-done
  550.1 0.0 copy-start.4
  550.1 1.3 copy.44
  551.4 0.6 copy-done.4
  552.1 0.0 copy-start.2
  552.1 1.0 copy.45
  553.0 1.0 copy-done.2
  554.0 0.0 copy-start.1
  554.0 1.3 copy.46
  555.3 1.0 copy-done.1
  556.4 1.3 copy.47
  (2 shorter events, 0.0 us)
Async XLA Ops:
  233.8 311.1 %copy-start.7 = (f32[128,16]{0,1:T(8,128)S(1)}, f32[128,16]{0,1:T(8,128)}, u32[]{:S(2)}) copy-start(f32[128,16]{0,1:T(8,128)} %param.21) | copy-start | bytes 24580
  233.8 311.1 %copy-start.8 = (f32[128,16]{0,1:T(8,128)S(1)}, f32[128,16]{0,1:T(8,128)}, u32[]{:S(2)}) copy-start(f32[128,16]{0,1:T(8,128)} %param.20) | copy-start | bytes 24580
  233.8 311.1 %copy-start.9 = (f32[128,16]{0,1:T(8,128)S(1)}, f32[128,16]{0,1:T(8,128)}, u32[]{:S(2)}) copy-start(f32[128,16]{0,1:T(8,128)} %param.23) | copy-start | bytes 24580
  233.8 311.1 %copy-start.10 = (f32[128,16]{0,1:T(8,128)S(1)}, f32[128,16]{0,1:T(8,128)}, u32[]{:S(2)}) copy-start(f32[128,16]{0,1:T(8,128)} %param.22) | copy-start | bytes 24580
  233.8 313.1 %copy-start.3 = (f32[256,1024]{1,0:T(8,128)S(1)}, f32[256,1024]{1,0:T(8,128)}, u32[]{:S(2)}) copy-start(f32[256,1024]{1,0:T(8,128)} %get-tuple-element.50) | copy-start | bytes 3145732
  542.9 5.0 copy-start.6
  547.0 1.9 copy-start.5
  547.9 2.2 copy-start
  550.1 2.0 copy-start.4
  552.1 2.0 copy-start.2
  554.0 2.3 copy-start.1

commit v6 on v5

--- a/solution.py
+++ b/solution.py
@@ -744,9 +744,10 @@
     ) = held
     tokens_grad, narrow_grad, widen_grad, merge_grad, mix_grad, value_grad, small_grad = outs
     away, keep, got, got_x, got_y, got_xy, got_yx, part, from_edge, from_inner, done = refs[:11]
-    buf_h, buf_l, g_two, g_gated, g_mixed, g_normed, g_soft, g_shared = refs[11:19]
-    smooth, back, ends, chip_ends, halves_in, back_enter, tables, direct, slope, last, small_sum = refs[19:30]
-    fetched, read, sent, came, written, sent_state, came_state = refs[30:]
+    ring, bend, straight, *refs = refs[11:]
+    buf_h, buf_l, g_two, g_gated, g_mixed, g_normed, g_soft, g_shared = refs[:8]
+    smooth, back, ends, chip_ends, halves_in, back_enter, tables, direct, slope, last, small_sum = refs[8:19]
+    fetched, read, sent, came, written, sent_state, came_state = refs[19:]
     lefts = (
         (hidden_h, hidden_l), (two_h, two_l), (gated_h, gated_l), (mixed_h, mixed_l), (normed_h, normed_l)
     )
@@ -776,41 +777,78 @@
     barrier = pltpu.get_barrier_semaphore()
     for other in near:
         pl.semaphore_signal(barrier, inc=1, **on_other(seq=other))
-    pl.semaphore_signal(barrier, inc=1, **on_other(batch=partner))
-
-    @pl.when(jnp.logical_not(is_edge))
-    def _():
-        pl.semaphore_signal(barrier, inc=1, **on_other(batch=3 - level))
-        pl.semaphore_wait(barrier, 6)
-
-    @pl.when(is_edge)
-    def _():
-        pl.semaphore_wait(barrier, 5)
+    above = (level + 1) % 4
+    for other in (above, (level + 3) % 4):
+        pl.semaphore_signal(barrier, inc=1, **on_other(batch=other))
+    pl.semaphore_wait(barrier, 6)
 
     def slot_in(ref, chunk):
         return chunk % ref.shape[0]
+
+    def turns(chunk):
+        return (chunk % 2 == 1) & (chunk < 45)
+
+    def slot_of(chunk, plain, turning):
+        number = chunk // 2
+        return jnp.where(turns(chunk), plain + number % turning, chunk % plain)
+
+    def turn_slot(chunk):
+        return chunk // 2 % 6
+
+    def keep_slot(chunk):
+        return slot_of(chunk, 4, 6)
+
+    def part_slot(chunk):
+        return slot_of(chunk, 6, 4)
+
+    def done_slot(chunk):
+        return slot_of(chunk, 4, 4)
+
+    def flag_slot(chunk):
+        return slot_of(chunk, 8, 6)
+
+    quarter, eighth = lanes // 4, lanes // 8
+
+    def rows_of(ref, index, first, count):
+        half_rows = ref.shape[-2]
+        start = pl.multiple_of(first % half_rows, 8)
+        return (*index, first // half_rows, pl.ds(start, count))
 
     def link(kind, chunk):
         def at(ref, *index):
             return ref.at[(slot_in(ref, chunk), *index)]
 
+        to, turn = keep_slot(chunk), turn_slot(chunk)
+        for_z, hold = part_slot(chunk), keep.at[to]
         source, target, device = (
             lambda: (at(away), at(got), sibling),
-            lambda: (at(keep, slice(None), 1 - along_x, 0), at(got_x), across_x),
-            lambda: (at(keep, 1 - along_y, slice(None), 1), at(got_y), across_y),
+            lambda: (hold.at[:, 1 - along_x, 0], at(got_x), across_x),
+            lambda: (hold.at[1 - along_y, :, 1], at(got_y), across_y),
             lambda: (at(got_x, 1 - along_y), at(got_xy), across_y),
             lambda: (at(got_y, 1 - along_x), at(got_yx), across_x),
-            lambda: (at(part), at(from_edge), {"batch": partner}),
-            lambda: (at(part), at(from_inner), {"batch": 3 - level}),
+            lambda: (part.at[for_z], from_edge.at[for_z], {"batch": partner}),
+            lambda: (part.at[for_z], from_inner.at[for_z], {"batch": 3 - level}),
+            None,
+            None,
+            lambda: (
+                keep.at[rows_of(keep, (to, 1 - along_y, 1 - along_x), (level + 3) % 4 * quarter, quarter)],
+                ring.at[0, turn], {"batch": above},
+            ),
+            lambda: (ring.at[0, turn], ring.at[1, turn], {"batch": above}),
+            lambda: (ring.at[1, turn], ring.at[2, turn], {"batch": above}),
+            lambda: (ring.at[2, turn, pl.ds(0, eighth)], bend.at[0, turn], across_x),
+            lambda: (ring.at[2, turn, pl.ds(eighth, eighth)], bend.at[1, turn], across_y),
+            lambda: (hold.at[along_y, 1 - along_x], straight.at[0, turn], across_x),
+            lambda: (hold.at[1 - along_y, along_x], straight.at[1, turn], across_y),
         )[kind]()
-        slot = chunk % sent.shape[1]
+        slot = flag_slot(chunk)
         return pltpu.make_async_remote_copy(
             src_ref=source, dst_ref=target, send_sem=sent.at[kind, slot], recv_sem=came.at[kind, slot],
             **on_other(**device),
         )
 
     def results(chunk, call):
-        slot, at = slot_in(done, chunk), chunk % sent.shape[1]
+        slot, at = done_slot(chunk), flag_slot(chunk)
 
         def pieces(number, source, target):
             yield lambda: pltpu.make_async_copy(source, target, written.at[number, at])
@@ -841,7 +879,7 @@
             call(*pieces(1, done.at[slot, :, pl.ds(lanes, lanes)], small_grad))
 
     def begin(chunk):
-        slot, to = slot_in(away, chunk), slot_in(keep, chunk)
+        slot, to = slot_in(away, chunk), keep_slot(chunk)
         for (blocks, wide), first, (high, low), (right, shift) in zip(
             reduce_shapes, firsts, lefts, rights
         ):
@@ -880,33 +918,73 @@
             fill(keep, to, core)
 
     def with_sibling(chunk):
-        slot = slot_in(keep, chunk)
+        slot = keep_slot(chunk)
         link(0, chunk).wait()
         keep[slot] = keep[slot] + got[slot_in(got, chunk)]
-        link(1, chunk).start()
-        link(2, chunk).start()
+        turning = turns(chunk)
+        pl.when(turning)(lambda: link(9, chunk).start())
+
+        @pl.when(jnp.logical_not(turning))
+        def _():
+            link(1, chunk).start()
+            link(2, chunk).start()
 
     def with_neighbour(chunk):
-        slot = slot_in(got_x, chunk)
+        slot, from_slot = slot_in(got_x, chunk), keep_slot(chunk)
         link(1, chunk).wait()
         link(2, chunk).wait()
-        from_slot = slot_in(keep, chunk)
         got_x[slot] = got_x[slot] + keep[from_slot, :, along_x, 0]
         got_y[slot] = got_y[slot] + keep[from_slot, along_y, :, 1]
         link(3, chunk).start()
         link(4, chunk).start()
 
+    def to_edge_or_on(chunk):
+        pl.when(is_edge)(lambda: link(5, chunk).start())
+
     def with_corner(chunk):
-        slot = slot_in(part, chunk)
+        slot = part_slot(chunk)
         link(3, chunk).wait()
         link(4, chunk).wait()
         first, second = slot_in(got_x, chunk), slot_in(got_xy, chunk)
         part[slot, 0] = got_x[first, along_y] + got_xy[second]
         part[slot, 1] = got_y[first, along_x] + got_yx[second]
-        pl.when(is_edge)(lambda: link(5, chunk).start())
+        to_edge_or_on(chunk)
+
+    def along_z(number):
+        def phase(chunk):
+            slot = turn_slot(chunk)
+            link(9 + number, chunk).wait()
+            place = (keep_slot(chunk), 1 - along_y, 1 - along_x)
+            own = keep[rows_of(keep, place, (level + 2 - number) % 4 * quarter, quarter)]
+            ring[number, slot] = ring[number, slot] + own
+            if number < 2:
+                link(10 + number, chunk).start()
+            else:
+                link(12, chunk).start()
+                link(13, chunk).start()
+
+        return phase
+
+    def go_straight(chunk):
+        slot, to = turn_slot(chunk), keep_slot(chunk)
+        link(12, chunk).wait()
+        link(13, chunk).wait()
+        upper = rows_of(keep, (to, 1 - along_y, along_x), level * quarter, eighth)
+        lower = rows_of(keep, (to, along_y, 1 - along_x), level * quarter + eighth, eighth)
+        keep[upper] = keep[upper] + bend[0, slot]
+        keep[lower] = keep[lower] + bend[1, slot]
+        link(14, chunk).start()
+        link(15, chunk).start()
+
+    def with_both(chunk):
+        slot, turn = part_slot(chunk), turn_slot(chunk)
+        link(14, chunk).wait()
+        link(15, chunk).wait()
+        part[slot] = keep[keep_slot(chunk), along_y, along_x] + straight[0, turn] + straight[1, turn]
+        to_edge_or_on(chunk)
 
     def inner_sum(chunk):
-        slot = slot_in(part, chunk)
+        slot = part_slot(chunk)
         pl.when(is_edge)(lambda: link(5, chunk).wait_send())
 
         @pl.when(jnp.logical_not(is_edge))
@@ -916,12 +994,12 @@
             link(6, chunk).start()
 
     def total_sum(chunk):
-        slot = slot_in(part, chunk)
+        slot = part_slot(chunk)
 
         @pl.when(jnp.logical_not(is_edge))
         def _():
             link(6, chunk).wait()
-            done[slot] = (part[slot] + from_inner[slot]).reshape(done.shape[1:])
+            done[done_slot(chunk)] = (part[slot] + from_inner[slot]).reshape(done.shape[1:])
 
             def start(stay, go):
                 stay().start()
@@ -1011,20 +1089,20 @@
         projected[4 + m] = grad * attended[m] * (gate * (1.0 + pre * (1.0 - gate)))
         pre = value_pre[m]
         gate = jax.nn.sigmoid(pre)
-        values, bend = pre * gate, gate * (1.0 + pre * (1.0 - gate))
+        values, curve = pre * gate, gate * (1.0 + pre * (1.0 - gate))
         g_values = []
         for s in range(sequences):
             span = slice(s * block_len, (s + 1) * block_len)
             own = halves(g_attended[span])
             g_soft[s] = g_soft[s] + three(own, halves(values[span]), 1, 1)
-            g_values.append(three(halves(soft[s]), own, 0, 0) * bend[span])
+            g_values.append(three(halves(soft[s]), own, 0, 0) * curve[span])
         value_pre[m] = jnp.concatenate(g_values, axis=0)
 
     def scores_back():
         affine = tree_sum([small[k, 3 * states + 3 : 3 * states + 6] for k in range(8)])
         pre = shared_pre[...]
         gate = jax.nn.sigmoid(pre)
-        shared, bend = pre * gate, gate * (1.0 + pre * (1.0 - gate))
+        shared, curve = pre * gate, gate * (1.0 + pre * (1.0 - gate))
         score_scale = shared.shape[1] ** (-0.5)
         queries = shared * affine[0:1] + affine[2:3]
         keys = shared * affine[1:2]
@@ -1036,7 +1114,7 @@
             g_scores = jnp.where(key_valid[s] > 0.5, g_scores, 0.0) * score_scale
             g_queries = contract(g_scores, keys[span], 1, 0, exact)
             g_keys = contract(g_scores, queries[span], 0, 0, exact)
-            g_shared[span] = (g_queries * affine[0:1] + g_keys * affine[1:2]) * bend[span]
+            g_shared[span] = (g_queries * affine[0:1] + g_keys * affine[1:2]) * curve[span]
             terms = (g_queries * shared[span], g_keys * shared[span], g_queries)
             for number, term in enumerate(terms):
                 sums[number] = sums[number] + jnp.sum(term, axis=0, keepdims=True)
@@ -1167,8 +1245,13 @@
         pl.when(at == 54)(share_entering)
         pl.when(at == 59)(norm_one_back)
 
+    every, straight_on, turning = None, False, True
     phases = (
-        (0, begin), (1, with_sibling), (3, with_neighbour), (5, with_corner), (7, inner_sum), (9, total_sum), (11, finish)
+        (0, begin, every), (1, with_sibling, every),
+        (3, with_neighbour, straight_on), (5, with_corner, straight_on), (7, inner_sum, straight_on),
+        (9, total_sum, straight_on), (11, finish, straight_on),
+        (3, along_z(0), turning), (5, along_z(1), turning), (7, along_z(2), turning), (9, go_straight, turning),
+        (11, with_both, turning), (13, inner_sum, turning), (15, total_sum, turning), (17, finish, turning),
     )
     fetch(0, "start")
     fetch(1, "start")
@@ -1180,31 +1263,36 @@
     arrive(0, 3)
 
     def step(at, carry):
-        for after, phase in phases[::-1]:
-
-            @pl.when((at >= after) & (at <= after + chunks))
-            def _(after=after, phase=phase):
-                phase(at - after)
+        for after, phase, which in sorted(phases, key=lambda item: -item[0]):
+            chunk = at - after
+            wanted = (chunk >= 0) & (chunk <= chunks)
+            if which is not None:
+                wanted = wanted & (turns(chunk) == which)
+
+            @pl.when(wanted)
+            def _(chunk=chunk, phase=phase):
+                phase(chunk)
 
         pl.when(at == 0)(lambda: arrive(3, 4))
         pl.when(at == 8)(lambda: arrive(4, kept_count))
         work(at)
         return carry
 
-    lax.fori_loop(0, chunks + 1 + phases[-1][0], step, 0)
+    lax.fori_loop(0, chunks + 1 + 11, step, 0)
 
 
 def call_backward(row_valid, key_valid, w_high, w_low, kept, grad_shapes):
     _, rows, width = kept[3].shape
     soft, signal, enter = kept[17], kept[20], kept[21]
     states = enter.shape[1]
-    half, piece, depth = 4 * lanes, lanes // 2, 8
+    half, piece = 4 * lanes, lanes // 2
     vmem, anywhere = pl.BlockSpec(memory_space=pltpu.VMEM), pl.BlockSpec(memory_space=pl.ANY)
     shapes = [f32(rows, 8 * lanes)] + [f32(*shape) for shape in grad_shapes] + [f32(lanes, lanes)]
     held = [
-        (4, 2, 2, 2, piece, width), (6, 2, 2, 2, piece, width), (4, 2, 2, 2, piece, width),
-        (9, 2, piece, width), (9, 2, piece, width), (depth, piece, width), (depth, piece, width),
-        (depth, 2, piece, width), (depth, 2, piece, width), (depth, 2, piece, width), (depth, lanes, width),
+        (4, 2, 2, 2, piece, width), (10, 2, 2, 2, piece, width), (4, 2, 2, 2, piece, width),
+        (6, 2, piece, width), (6, 2, piece, width), (6, piece, width), (6, piece, width),
+        (10, 2, piece, width), (10, 2, piece, width), (10, 2, piece, width), (8, lanes, width),
+        (3, 6, lanes // 4, width), (2, 6, lanes // 8, width), (2, 6, 2, piece, width),
     ]
     more = [
         (2, rows, half), (2, 2, rows, half), (2, rows, half), (2, rows, half), soft.shape, (rows, lanes),
@@ -1224,9 +1312,9 @@
         + [
             pltpu.SemaphoreType.DMA((2, 3)),
             pltpu.SemaphoreType.DMA((kept_count,)),
-            pltpu.SemaphoreType.DMA((9, depth)),
-            pltpu.SemaphoreType.DMA((9, depth)),
-            pltpu.SemaphoreType.DMA((2, depth)),
+            pltpu.SemaphoreType.DMA((16, 14)),
+            pltpu.SemaphoreType.DMA((16, 14)),
+            pltpu.SemaphoreType.DMA((2, 14)),
             pltpu.SemaphoreType.DMA((5,)),
             pltpu.SemaphoreType.DMA((5,)),
         ],

time: 558 us -> 546 us (0.978)
  Pallas kernels: 537 us -> 524 us
    pallas_call x1, Pallas kernels: 309 us -> 296 us  [call_backward(): pl.pallas_call(backward_body, out_shape=shapes, in_specs=[vmem] * 2 + [an...]
where the time goes in v6:
time: 546 us; the launch traced here: 545 us
  Pallas kernels  524 us (96%)
  local copies, waits for them, and re-layouts  16.3 us (3%)
    pallas_call x1, Pallas kernels, call_backward(): pl.pallas_call(backward_body, out_shape=shapes, in_specs=[vmem] * 2 + [an...  296 us
    pallas_call x1, Pallas kernels, call_forward(): pl.pallas_call(forward_body, out_shape=shapes, in_specs=[anywhere] * len(...  227 us

profile of v6, /device:TPU:0, one launch (start us, length us, event | category | flops | bytes accessed | tf_op | source)
XLA Modules:
  0.0 545.1 jit_solution(11232742992081478166)
XLA Ops:
  0.7 1.3 compare_convert_fusion.key_valid
  2.0 0.7 compare_convert_fusion.1
  2.7 0.8 dynamic_update_slice.3
  3.5 0.8 fusion.12
  4.2 0.7 concatenate.3
  4.9 0.6 pad.4.packed
  5.6 0.8 copy.31.row_valid
  6.4 227.4 %shard_map.271 = (f32[256,1024]{1,0:T(8,128)}, bf16[64,2,512,256]{3,2,1,0:T(8,128)(2,1)}, bf16[64,2,512,256]{3,2,1,0:T(8,128)(2,1)}, bf16[4,2,256,512]{3,2,1,0:T...) custom-call(f32[4,4,8,2048]{3,2,1,0:T(8,128)} %bitcast.108, ...), custom_call_target="tpu_custom_call" | custom-call | tf_op jit(solution)/shard_map/pallas_call | solution.py:700
  233.8 0.0 copy-start.7
  233.8 0.0 copy-start.8
  233.8 0.0 copy-start.9
  233.8 0.0 copy-start.10
  233.8 0.0 copy-start.3
  233.9 296.5 %shard_map.272 = (f32[256,1024]{1,0:T(8,128)}, f32[512,1024]{1,0:T(8,128)}, f32[128,4096]{1,0:T(8,128)}, f32[256,1024]{1,0:T(8,128)}, f32[128,4224]{1,0:T(8,128)...) custom-call(f32[256,1]{1,0:T(8,128)} %copy.31.row_valid, f32[2,1,128]{2,1,0:T(1,128)} %compare_convert_fusion.key_valid, ...), custom_call_target="tpu_custom_call" | custom-call | tf_op jit(solution)/shard_map/pallas_call | solution.py:1303
  530.4 0.0 copy-start.6
  530.4 1.3 slice_bitcast_fusion
  531.7 0.7 slice.22
  532.4 0.0 copy-done.7
  532.4 0.0 copy-done.8
  532.4 0.0 copy-done.9
  532.4 0.0 copy-done.10
  532.4 1.3 fusion.14
  533.7 0.6 dynamic-slice_bitcast_fusion
  534.4 0.0 copy-done.3
  534.4 0.0 copy-start.5
  534.4 1.0 copy.41
  535.3 0.0 copy-done.6
  535.3 0.0 copy-start
  535.4 1.0 copy.42
  536.3 0.0 copy-done.5
  536.3 1.0 copy.43
  537.3 0.2 copy-done
  537.5 0.0 copy-start.4
  537.5 1.3 copy.44
  538.9 0.6 copy-done.4
  539.5 0.0 copy-start.2
  539.5 1.0 copy.45
  540.4 1.0 copy-done.2
  541.4 0.0 copy-start.1
  541.4 1.3 copy.46
  542.8 1.0 copy-done.1
  543.8 1.3 copy.47
  (2 shorter events, 0.0 us)
Async XLA Ops:
  233.8 298.6 %copy-start.7 = (f32[128,16]{0,1:T(8,128)S(1)}, f32[128,16]{0,1:T(8,128)}, u32[]{:S(2)}) copy-start(f32[128,16]{0,1:T(8,128)} %param.21) | copy-start | bytes 24580
  233.8 298.5 %copy-start.8 = (f32[128,16]{0,1:T(8,128)S(1)}, f32[128,16]{0,1:T(8,128)}, u32[]{:S(2)}) copy-start(f32[128,16]{0,1:T(8,128)} %param.20) | copy-start | bytes 24580
  233.8 298.5 %copy-start.9 = (f32[128,16]{0,1:T(8,128)S(1)}, f32[128,16]{0,1:T(8,128)}, u32[]{:S(2)}) copy-start(f32[128,16]{0,1:T(8,128)} %param.23) | copy-start | bytes 24580
  233.8 298.5 %copy-start.10 = (f32[128,16]{0,1:T(8,128)S(1)}, f32[128,16]{0,1:T(8,128)}, u32[]{:S(2)}) copy-start(f32[128,16]{0,1:T(8,128)} %param.22) | copy-start | bytes 24580
  233.8 300.5 %copy-start.3 = (f32[256,1024]{1,0:T(8,128)S(1)}, f32[256,1024]{1,0:T(8,128)}, u32[]{:S(2)}) copy-start(f32[256,1024]{1,0:T(8,128)} %get-tuple-element.50) | copy-start | bytes 3145732
  530.4 5.0 copy-start.6
  534.4 1.9 copy-start.5
  535.3 2.2 copy-start
  537.5 2.0 copy-start.4
  539.5 2.0 copy-start.2
  541.4 2.3 copy-start.1

commit v7 on v6

--- a/solution.py
+++ b/solution.py
@@ -291,7 +291,7 @@
         )
 
     def shares(chunk):
-        return chunk % 3 != 2
+        return (chunk % 3 != 2) & (chunk < 58)
 
     def own_load(weight, block, column, slot):
         source = weight.at[pl.ds(block * 4, 4), :, :, pl.ds(pl.multiple_of(column, lanes), width)]
@@ -786,7 +786,7 @@
         return chunk % ref.shape[0]
 
     def turns(chunk):
-        return (chunk % 2 == 1) & (chunk < 45)
+        return (chunk % 2 == 1) & (chunk < 49)
 
     def slot_of(chunk, plain, turning):
         number = chunk // 2

time: 546 us -> 542 us (level)
  no operation moved by 1% of the time
where the time goes in v7:
time: 542 us; the launch traced here: 541 us
  Pallas kernels  520 us (96%)
  local copies, waits for them, and re-layouts  16.3 us (3%)
    pallas_call x1, Pallas kernels, call_backward(): pl.pallas_call(backward_body, out_shape=shapes, in_specs=[vmem] * 2 + [an...  294 us
    pallas_call x1, Pallas kernels, call_forward(): pl.pallas_call(forward_body, out_shape=shapes, in_specs=[anywhere] * len(...  226 us

profile of v7, /device:TPU:0, one launch (start us, length us, event | category | flops | bytes accessed | tf_op | source)
XLA Modules:
  0.0 541.3 jit_solution(11215469163680231839)
XLA Ops:
  0.7 1.3 compare_convert_fusion.key_valid
  2.0 0.7 compare_convert_fusion.1
  2.7 0.8 dynamic_update_slice.3
  3.5 0.8 fusion.12
  4.2 0.7 concatenate.3
  4.9 0.6 pad.4.packed
  5.6 0.8 copy.31.row_valid
  6.4 225.7 %shard_map.271 = (f32[256,1024]{1,0:T(8,128)}, bf16[64,2,512,256]{3,2,1,0:T(8,128)(2,1)}, bf16[64,2,512,256]{3,2,1,0:T(8,128)(2,1)}, bf16[4,2,256,512]{3,2,1,0:T...) custom-call(f32[4,4,8,2048]{3,2,1,0:T(8,128)} %bitcast.108, ...), custom_call_target="tpu_custom_call" | custom-call | tf_op jit(solution)/shard_map/pallas_call | solution.py:700
  232.1 0.0 copy-start.7
  232.1 0.0 copy-start.8
  232.1 0.0 copy-start.9
  232.1 0.0 copy-start.10
  232.1 0.0 copy-start.3
  232.1 294.4 %shard_map.272 = (f32[256,1024]{1,0:T(8,128)}, f32[512,1024]{1,0:T(8,128)}, f32[128,4096]{1,0:T(8,128)}, f32[256,1024]{1,0:T(8,128)}, f32[128,4224]{1,0:T(8,128)...) custom-call(f32[256,1]{1,0:T(8,128)} %copy.31.row_valid, f32[2,1,128]{2,1,0:T(1,128)} %compare_convert_fusion.key_valid, ...), custom_call_target="tpu_custom_call" | custom-call | tf_op jit(solution)/shard_map/pallas_call | solution.py:1303
  526.6 0.0 copy-start.6
  526.6 1.3 slice_bitcast_fusion
  527.9 0.7 slice.22
  528.6 0.0 copy-done.7
  528.6 0.0 copy-done.8
  528.6 0.0 copy-done.9
  528.6 0.0 copy-done.10
  528.6 1.3 fusion.14
  529.9 0.6 dynamic-slice_bitcast_fusion
  530.6 0.0 copy-done.3
  530.6 0.0 copy-start.5
  530.6 1.0 copy.41
  531.6 0.0 copy-done.6
  531.6 0.0 copy-start
  531.6 1.0 copy.42
  532.5 0.0 copy-done.5
  532.5 1.0 copy.43
  533.5 0.2 copy-done
  533.7 0.0 copy-start.4
  533.7 1.3 copy.44
  535.1 0.6 copy-done.4
  535.7 0.0 copy-start.2
  535.7 1.0 copy.45
  536.7 1.0 copy-done.2
  537.6 0.0 copy-start.1
  537.7 1.3 copy.46
  539.0 1.0 copy-done.1
  540.0 1.3 copy.47
  (2 shorter events, 0.0 us)
Async XLA Ops:
  232.1 296.5 %copy-start.7 = (f32[128,16]{0,1:T(8,128)S(1)}, f32[128,16]{0,1:T(8,128)}, u32[]{:S(2)}) copy-start(f32[128,16]{0,1:T(8,128)} %param.21) | copy-start | bytes 24580
  232.1 296.5 %copy-start.8 = (f32[128,16]{0,1:T(8,128)S(1)}, f32[128,16]{0,1:T(8,128)}, u32[]{:S(2)}) copy-start(f32[128,16]{0,1:T(8,128)} %param.20) | copy-start | bytes 24580
  232.1 296.5 %copy-start.9 = (f32[128,16]{0,1:T(8,128)S(1)}, f32[128,16]{0,1:T(8,128)}, u32[]{:S(2)}) copy-start(f32[128,16]{0,1:T(8,128)} %param.23) | copy-start | bytes 24580
  232.1 296.5 %copy-start.10 = (f32[128,16]{0,1:T(8,128)S(1)}, f32[128,16]{0,1:T(8,128)}, u32[]{:S(2)}) copy-start(f32[128,16]{0,1:T(8,128)} %param.22) | copy-start | bytes 24580
  232.1 298.5 %copy-start.3 = (f32[256,1024]{1,0:T(8,128)S(1)}, f32[256,1024]{1,0:T(8,128)}, u32[]{:S(2)}) copy-start(f32[256,1024]{1,0:T(8,128)} %get-tuple-element.50) | copy-start | bytes 3145732
  526.6 5.0 copy-start.6
  530.6 1.9 copy-start.5
  531.6 2.2 copy-start
  533.7 2.0 copy-start.4
  535.7 2.0 copy-start.2
  537.6 2.3 copy-start.1

commit v8 on v7

--- a/solution.py
+++ b/solution.py
@@ -611,7 +611,7 @@
     phases = (
         (2, relay), (4, ring(0)), (6, ring(1)), (8, ring(2)), (10, to_sibling), (11, complete)
     )
-    last, ahead = phases[-1][0], 1
+    last, ahead = phases[-1][0], 2
 
     def step(at, carry):
         for after, phase in phases[-2::-1]:
@@ -746,8 +746,8 @@
     away, keep, got, got_x, got_y, got_xy, got_yx, part, from_edge, from_inner, done = refs[:11]
     ring, bend, straight, *refs = refs[11:]
     buf_h, buf_l, g_two, g_gated, g_mixed, g_normed, g_soft, g_shared = refs[:8]
-    smooth, back, ends, chip_ends, halves_in, back_enter, tables, direct, slope, last, small_sum = refs[8:19]
-    fetched, read, sent, came, written, sent_state, came_state = refs[19:]
+    smooth, back, ends, chip_ends, halves_in, back_enter, tables, direct, slope, last, small_sum, stat = refs[8:20]
+    fetched, read, sent, came, written, sent_state, came_state = refs[20:]
     lefts = (
         (hidden_h, hidden_l), (two_h, two_l), (gated_h, gated_l), (mixed_h, mixed_l), (normed_h, normed_l)
     )
@@ -1053,23 +1053,36 @@
             total = total + jnp.sum(shifted * shifted, axis=1, keepdims=True)
         return centre, lax.rsqrt(total / features + norm_eps)
 
-    def norm_two_back():
-        centre, scale = statistics(middle)
-
-        def grad_of(k):
-            span = slice(k * lanes, (k + 1) * lanes)
-            return jnp.concatenate([g_two[0, :, span], g_two[1, :, span]], axis=1)
-
+    def store_statistics(ref):
+        for number, value in enumerate(statistics(ref)):
+            stat[number] = jnp.broadcast_to(value, (rows, lanes))
+
+    def store_means(plain, crossed):
+        for number, value in enumerate((plain, crossed)):
+            stat[2 + number] = jnp.broadcast_to(value / features, (rows, lanes))
+
+    def stored(number):
+        return stat[number, :, 0:1], stat[number + 1, :, 0:1]
+
+    def grad_two(k):
+        span = slice(k * lanes, (k + 1) * lanes)
+        return jnp.concatenate([g_two[0, :, span], g_two[1, :, span]], axis=1)
+
+    def norm_two_sums():
+        centre, scale = stored(0)
         plain, crossed = 0.0, 0.0
         for k in range(tiles):
-            grad, hat = grad_of(k), (middle[k] - centre) * scale
+            grad, hat = grad_two(k), (middle[k] - centre) * scale
             put_row(2 * states + 2, k, jnp.sum(grad * hat, axis=0, keepdims=True))
             inner = grad * row_of(3 * states + 2, k)
             plain = plain + jnp.sum(inner, axis=1, keepdims=True)
             crossed = crossed + jnp.sum(inner * hat, axis=1, keepdims=True)
-        plain, crossed = plain / features, crossed / features
+        store_means(plain, crossed)
+
+    def norm_two_back():
+        (centre, scale), (plain, crossed) = stored(0), stored(2)
         for k in range(tiles):
-            inner, hat = grad_of(k) * row_of(3 * states + 2, k), (middle[k] - centre) * scale
+            inner, hat = grad_two(k) * row_of(3 * states + 2, k), (middle[k] - centre) * scale
             g_middle = g_out[k] + (inner - plain - hat * crossed) * scale
             update = jax.nn.sigmoid(projected[k])
             pre = cand_pre[k]
@@ -1122,14 +1135,18 @@
             for k in range(8):
                 row = 2 * states + 3 + number
                 small_sum[k, row : row + 1] = sums[number]
+
+    def shared_back():
         own, full = halves(g_shared[...]), halves(shared_w[...].reshape(2, half, lanes))
         for parity in range(2):
             g_mixed[parity] = three(own, (full[0][parity], full[1][parity]), 1, 1)
 
-    def smooth_back():
+    def load_tables():
         for kind in range(3):
             for n in range(states):
                 tables[kind, n] = small[:, kind * states + n]
+
+    def smooth_back():
         for parity in range(2):
             pre = mix_pre[parity]
             g_mixed[parity] = g_mixed[parity] * silu_slope(pre)
@@ -1154,30 +1171,29 @@
         run_moments(s, low, low + 8, decay, enter, signal, smooth, direct, slope, last)
 
     def carry_one(s):
-        if s == 0:
-            enter_states()
         run_carried(True, s, decay, weight, back_enter, back, back)
 
-    def norm_one_back():
+    def both_blocks(ref, k):
+        span = slice(k * lanes, (k + 1) * lanes)
+        return jnp.concatenate([ref[0, :, span], ref[1, :, span]], axis=1)
+
+    def state_sums():
         for n in range(states):
             total = slope[n]
             for s in range(sequences):
                 total = total + decay[n] * back_enter[s, n] * last[s, n]
             small_sum[:, n] = direct[n]
             small_sum[:, states + n] = total
-        centre, scale = statistics(masked)
+
+    def norm_one_sums():
+        centre, scale = stored(0)
         line = [back[s].reshape(block_len, features) for s in range(sequences)]
         line = jnp.concatenate(line, axis=0)
-
-        def blocks(ref, k):
-            span = slice(k * lanes, (k + 1) * lanes)
-            return jnp.concatenate([ref[0, :, span], ref[1, :, span]], axis=1)
-
         plain, crossed = 0.0, 0.0
         for k in range(tiles):
-            g_smooth, hat = blocks(g_mixed, k), (masked[k] - centre) * scale
+            g_smooth, hat = both_blocks(g_mixed, k), (masked[k] - centre) * scale
             gain = row_of(3 * states, k)
-            grad = blocks(g_normed, k) + g_smooth * row_of(3 * states + 1, k)
+            grad = both_blocks(g_normed, k) + g_smooth * row_of(3 * states + 1, k)
             grad = grad + line[:, k * width : (k + 1) * width]
             put_row(2 * states, k, jnp.sum(grad * hat, axis=0, keepdims=True))
             put_row(2 * states + 1, k, jnp.sum(g_smooth * (hat * gain), axis=0, keepdims=True))
@@ -1185,7 +1201,10 @@
             plain = plain + jnp.sum(inner, axis=1, keepdims=True)
             crossed = crossed + jnp.sum(inner * hat, axis=1, keepdims=True)
             tokens_grad[:, k * width : (k + 1) * width] = inner
-        plain, crossed = plain / features, crossed / features
+        store_means(plain, crossed)
+
+    def norm_one_back():
+        (centre, scale), (plain, crossed) = stored(0), stored(2)
         for k in range(tiles):
             span = slice(k * width, (k + 1) * width)
             hat = (masked[k] - centre) * scale
@@ -1199,9 +1218,19 @@
     small_sum[...] = jnp.zeros(small_sum.shape, jnp.float32)
 
     def work(at):
-        @pl.when((at < 24) | ((at >= 32) & (at < 56)))
-        def _():
-            step = jnp.where(at < 24, at, at - 8)
+        merging, mixing, valuing = 18, 35, 51
+        in_merge = (at >= merging) & (at < merging + 8)
+        in_mix = (at >= mixing) & (at < mixing + 16)
+        in_value = (at >= valuing) & (at < valuing + 8)
+        pl.when(at == 14)(lambda: store_statistics(middle))
+        pl.when(at == 16)(norm_two_sums)
+        pl.when(at == 17)(norm_two_back)
+        pl.when(at == 34)(scores_back)
+        pl.when(at == 35)(shared_back)
+
+        @pl.when((at < 16) | in_merge | in_mix | in_value)
+        def _():
+            step = jnp.where(at < 16, at, jnp.where(at < merging + 8, at - 2, at - 11))
             pl.when(step + 2 < steps)(lambda: fetch(step + 2, "start"))
             fetch(step, "wait")
 
@@ -1210,40 +1239,41 @@
                 for parity in range(2):
                     g_two[parity] = g_two[parity] + back_product(g_wide[at], step, parity)
 
-            pl.when(at == 16)(norm_two_back)
-
-            @pl.when((at >= 16) & (at < 24))
+            @pl.when(in_merge)
             def _():
-                j = (at - 16) // 4
+                j, tile = (at - merging) // 4, (at - merging) % 4
                 for parity in range(2):
-                    more = back_product(projected[12 + at % 4], step, parity)
+                    more = back_product(projected[12 + tile], step, parity)
                     g_gated[j, parity] = g_gated[j, parity] + more
 
-            pl.when(at == 32)(scores_back)
-
-            @pl.when((at >= 32) & (at < 48))
+            @pl.when(in_mix)
             def _():
                 for parity in range(2):
-                    more = back_product(projected[at - 32], step, parity)
+                    more = back_product(projected[at - mixing], step, parity)
                     g_mixed[parity] = g_mixed[parity] + more
 
-            @pl.when(at >= 48)
+            @pl.when(in_value)
             def _():
                 for parity in range(2):
-                    more = back_product(value_pre[at - 48], step, parity)
+                    more = back_product(value_pre[at - valuing], step, parity)
                     g_normed[parity] = g_normed[parity] + more
 
-        pl.when((at >= 24) & (at < 32))(lambda: attention_back(at - 24))
-        pl.when(at == 48)(smooth_back)
+        pl.when((at >= 26) & (at < 34))(lambda: attention_back(at - 26))
+        pl.when(at == 28)(load_tables)
+        pl.when(at == 30)(lambda: store_statistics(masked))
+        pl.when(at == 51)(smooth_back)
         for s in range(sequences):
-            pl.when(at == 49 + s)(functools.partial(filter_one, s))
+            pl.when(at == 52 + s)(functools.partial(filter_one, s))
             for low in range(0, states, 8):
-                number = 51 + s * (states // 8) + low // 8
+                number = 54 + s * (states // 8) + low // 8
                 pl.when(at == number)(functools.partial(moments_one, s, low))
-            pl.when(at == 56 + s)(functools.partial(carry_one, s))
-        pl.when(at == 52)(to_chips)
-        pl.when(at == 54)(share_entering)
-        pl.when(at == 59)(norm_one_back)
+            pl.when(at == 60 + s)(functools.partial(carry_one, s))
+        pl.when(at == 55)(to_chips)
+        pl.when(at == 57)(share_entering)
+        pl.when(at == 59)(enter_states)
+        pl.when(at == 61)(state_sums)
+        pl.when(at == 62)(norm_one_sums)
+        pl.when(at == 63)(norm_one_back)
 
     every, straight_on, turning = None, False, True
     phases = (
@@ -1298,7 +1328,7 @@
         (2, rows, half), (2, 2, rows, half), (2, rows, half), (2, rows, half), soft.shape, (rows, lanes),
         signal.shape, signal.shape, (2, *enter.shape), (4, enter.shape[0], states // 2, 8, lanes),
         (2, enter.shape[0], states // 2, 8, lanes), enter.shape, (3, states, 8, lanes),
-        (states, 8, lanes), (states, 8, lanes), enter.shape, (8, lanes, lanes),
+        (states, 8, lanes), (states, 8, lanes), enter.shape, (8, lanes, lanes), (4, rows, lanes),
     ]
     return pl.pallas_call(
         backward_body,

time: 542 us -> 543 us (level)
  no operation moved by 1% of the time
where the time goes in v8:
time: 543 us; the launch traced here: 542 us
  Pallas kernels  521 us (96%)
  local copies, waits for them, and re-layouts  16.3 us (3%)
    pallas_call x1, Pallas kernels, call_backward(): pl.pallas_call(backward_body, out_shape=shapes, in_specs=[vmem] * 2 + [an...  295 us
    pallas_call x1, Pallas kernels, call_forward(): pl.pallas_call(forward_body, out_shape=shapes, in_specs=[anywhere] * len(...  226 us

profile of v8, /device:TPU:0, one launch (start us, length us, event | category | flops | bytes accessed | tf_op | source)
XLA Modules:
  0.0 542.1 jit_solution(15424334362578217998)
XLA Ops:
  0.7 1.3 compare_convert_fusion.key_valid
  2.0 0.7 compare_convert_fusion.1
  2.7 0.8 dynamic_update_slice.3
  3.5 0.8 fusion.12
  4.2 0.7 concatenate.3
  4.9 0.6 pad.4.packed
  5.6 0.8 copy.31.row_valid
  6.4 225.8 %shard_map.271 = (f32[256,1024]{1,0:T(8,128)}, bf16[64,2,512,256]{3,2,1,0:T(8,128)(2,1)}, bf16[64,2,512,256]{3,2,1,0:T(8,128)(2,1)}, bf16[4,2,256,512]{3,2,1,0:T...) custom-call(f32[4,4,8,2048]{3,2,1,0:T(8,128)} %bitcast.108, ...), custom_call_target="tpu_custom_call" | custom-call | tf_op jit(solution)/shard_map/pallas_call | solution.py:700
  232.1 0.0 copy-start.7
  232.2 0.0 copy-start.8
  232.2 0.0 copy-start.9
  232.2 0.0 copy-start.10
  232.2 0.0 copy-start.3
  232.2 295.1 %shard_map.272 = (f32[256,1024]{1,0:T(8,128)}, f32[512,1024]{1,0:T(8,128)}, f32[128,4096]{1,0:T(8,128)}, f32[256,1024]{1,0:T(8,128)}, f32[128,4224]{1,0:T(8,128)...) custom-call(f32[256,1]{1,0:T(8,128)} %copy.31.row_valid, f32[2,1,128]{2,1,0:T(1,128)} %compare_convert_fusion.key_valid, ...), custom_call_target="tpu_custom_call" | custom-call | tf_op jit(solution)/shard_map/pallas_call | solution.py:1333
  527.3 0.0 copy-start.6
  527.3 1.3 slice_bitcast_fusion
  528.6 0.7 slice.22
  529.3 0.0 copy-done.7
  529.3 0.0 copy-done.8
  529.3 0.0 copy-done.9
  529.3 0.0 copy-done.10
  529.3 1.3 fusion.14
  530.7 0.6 dynamic-slice_bitcast_fusion
  531.3 0.0 copy-done.3
  531.3 0.0 copy-start.5
  531.3 1.0 copy.41
  532.3 0.0 copy-done.6
  532.3 0.0 copy-start
  532.3 1.0 copy.42
  533.3 0.0 copy-done.5
  533.3 1.0 copy.43
  534.2 0.2 copy-done
  534.5 0.0 copy-start.4
  534.5 1.3 copy.44
  535.8 0.6 copy-done.4
  536.4 0.0 copy-start.2
  536.4 1.0 copy.45
  537.4 1.0 copy-done.2
  538.4 0.0 copy-start.1
  538.4 1.3 copy.46
  539.7 1.0 copy-done.1
  540.7 1.3 copy.47
  (2 shorter events, 0.0 us)
Async XLA Ops:
  232.1 297.2 %copy-start.7 = (f32[128,16]{0,1:T(8,128)S(1)}, f32[128,16]{0,1:T(8,128)}, u32[]{:S(2)}) copy-start(f32[128,16]{0,1:T(8,128)} %param.21) | copy-start | bytes 24580
  232.2 297.1 %copy-start.8 = (f32[128,16]{0,1:T(8,128)S(1)}, f32[128,16]{0,1:T(8,128)}, u32[]{:S(2)}) copy-start(f32[128,16]{0,1:T(8,128)} %param.20) | copy-start | bytes 24580
  232.2 297.1 %copy-start.9 = (f32[128,16]{0,1:T(8,128)S(1)}, f32[128,16]{0,1:T(8,128)}, u32[]{:S(2)}) copy-start(f32[128,16]{0,1:T(8,128)} %param.23) | copy-start | bytes 24580
  232.2 297.1 %copy-start.10 = (f32[128,16]{0,1:T(8,128)S(1)}, f32[128,16]{0,1:T(8,128)}, u32[]{:S(2)}) copy-start(f32[128,16]{0,1:T(8,128)} %param.22) | copy-start | bytes 24580
  232.2 299.1 %copy-start.3 = (f32[256,1024]{1,0:T(8,128)S(1)}, f32[256,1024]{1,0:T(8,128)}, u32[]{:S(2)}) copy-start(f32[256,1024]{1,0:T(8,128)} %get-tuple-element.50) | copy-start | bytes 3145732
  527.3 5.0 copy-start.6
  531.3 1.9 copy-start.5
  532.3 2.2 copy-start
  534.5 2.0 copy-start.4
  536.4 2.0 copy-start.2
  538.4 2.3 copy-start.1
